TPU v7x, 32 devices: a whole 2x2x4 slice. The times are simulated.
32 devices in a mesh: section: 2 (over core), row: 8 (over z, y), col: 2 (over x).
Axes of the slice: x: 2, y: 2, z: 4, core: 2. Of those that a mesh axis runs over, the one named last changes fastest.
Arguments:
- hidden_in: bfloat16 [8, 256, 3072], P('row', None, 'col')
- patch_ends: int32 [8, 4], P('row'), may hold values from 1 to 256, as said below
- timestep: int32 [8], P('row'), may hold values from 0 to 999
- mod_weight: bfloat16 [2, 256, 3, 3072], P('section'), may hold values from -0.75 to 0.75
- qkv_weight: bfloat16 [2, 3072, 3, 3072], P('section', 'row', None, 'col'), may hold values from -0.109375 to 0.109375
- out_weight: bfloat16 [2, 3072, 3072], P('section', 'col', 'row'), may hold values from -0.109375 to 0.109375
- stale_keys: bfloat16 [2, 8, 256, 3072], P('section', 'row', None, 'col'), may hold values from -1.5 to 1.5
- stale_values: bfloat16 [2, 8, 256, 3072], P('section', 'row', None, 'col'), may hold values from -6 to 6
Outputs:
- layer_out: bfloat16 [2, 8, 256, 3072], P('section', 'row', None, 'col')
Inputs may be any that keep to these rules, and one draw needn't show every extreme that they name: patch_ends rises along each request's 4 patches; each patch holds at least one and at most 64 positions, and in every draw some request has all 4 patches of exactly 64 positions.
All inputs are finite; a program needn't handle non-finite values.
Results may differ from a plain program's by a relative error of at most 0.018.
Values may be sent and summed in bfloat16 or wider, within the bound.
No kernel may reach another device: no remote copies, remote signals or barrier semaphores. Data moves between devices by JAX's collectives and lax.ppermute only.
A program may use at most 128 MiB of HBM per device.

v0:
```python
import functools
import math

import jax
import jax.numpy as jnp
from jax import lax
from jax.experimental import pallas as pl
from jax.experimental.pallas import tpu as pltpu
from jax.sharding import PartitionSpec as P

HD = 128
FREQ = 256
NP = 4
AXES = ("section", "row", "col")
VMEM_LIMIT = 56 * 1024 * 1024


def send_to(array, where):
    ns, nr, nc = (lax.axis_size(axis) for axis in AXES)
    pairs = []
    for s in range(ns):
        for i in range(nr):
            for c in range(nc):
                ts, ti, tc = where(s, i, c)
                pairs.append(((s * nr + i) * nc + c, (ts * nr + ti) * nc + tc))
    return lax.ppermute(array, AXES, pairs)


def to_core(array):
    return send_to(array, lambda s, i, c: (1 - s, i, c))


def after(array, *others):
    return lax.optimization_barrier((array,) + others)[0]


def pick(array, index):
    return lax.dynamic_index_in_dim(array, index, 0, keepdims=False)


def embed_time(timestep):
    half_width = FREQ // 2
    frequency = jnp.exp(
        jnp.arange(half_width, dtype=jnp.float32) * (-math.log(10000.0) / half_width)
    )
    angles = timestep.astype(jnp.float32)[:, None] * frequency[None, :]
    return jnp.concatenate([jnp.cos(angles), jnp.sin(angles)], axis=1).astype(jnp.bfloat16)


def any_spec():
    return pl.BlockSpec(memory_space=pl.ANY)


def vmem_spec():
    return pl.BlockSpec(memory_space=pltpu.VMEM)


def load_rows(pieces, target, sem, first, rows_each):
    i = lax.axis_index("row")
    copies = []
    for d, piece in enumerate(pieces):
        if rows_each is None:
            place = target.at[i ^ d]
        else:
            place = target.at[pl.ds(pl.multiple_of((i ^ d) * rows_each, 32), rows_each), :]
        copies.append(pltpu.make_async_copy(piece, place, sem.at[first + d]))
        copies[-1].start()
    return copies


def fresh_and_valid(ends_ref, slot, slot_len):
    key_at = lax.broadcasted_iota(jnp.int32, (slot_len, slot_len), 1)
    query_at = lax.broadcasted_iota(jnp.int32, (slot_len, slot_len), 0)
    limit = jnp.full((slot_len, slot_len), ends_ref[slot, NP - 1], jnp.int32)
    for m in range(NP - 2, -1, -1):
        limit = jnp.where(query_at < ends_ref[slot, m], ends_ref[slot, m], limit)
    return key_at < limit, key_at < ends_ref[slot, NP - 1]


def scores_kernel(plan, ends_ref, mod_ref, *refs):
    slots, slot_len, cols, n_x, n_w, kr, bw, wc = plan
    x_refs, refs = refs[:n_x], refs[n_x:]
    w_refs, refs = (refs[:n_w], refs[n_w : 2 * n_w]), refs[2 * n_w :]
    kv_refs, refs = refs[:slots], refs[slots:]
    xm, weights_ref, xv, wv, kvv, x_sem, w_sem, kv_sem = refs
    s, c = lax.axis_index("section"), lax.axis_index("col")
    half = slot_len // 2
    x_copies, w_copies, kv_copies = [], [], []
    for slot in range(slots):
        for dc in range(cols):
            for h in range(2):
                place = len(x_copies)
                col = lax.rem(c + cols - dc, cols)
                row = slot * slot_len + jnp.where(s == h, 0, half)
                row = pl.multiple_of(row, half)
                x_copies.append(
                    pltpu.make_async_copy(
                        x_refs[place], xv.at[col, pl.ds(row, half), :], x_sem.at[place]
                    )
                )
                x_copies[-1].start()
    for t in range(2):
        w_copies.append(load_rows(w_refs[t], wv.at[t], w_sem, t * n_w, kr))
    for slot in range(slots):
        kv_copies.append(
            pltpu.make_async_copy(kv_refs[slot].at[0], kvv.at[slot], kv_sem.at[slot])
        )
        kv_copies[-1].start()
    for copy in x_copies:
        copy.wait()
    feat = cols * wc
    for slot in range(slots):
        rows = pl.ds(slot * slot_len, slot_len)
        total = jnp.zeros((slot_len, 1), jnp.float32)
        squares = jnp.zeros((slot_len, 1), jnp.float32)
        for col in range(cols):
            part = xv[col, rows, :].astype(jnp.float32)
            total += jnp.sum(part, axis=-1, keepdims=True)
            squares += jnp.sum(part * part, axis=-1, keepdims=True)
        mean = total / feat
        var = squares / feat - mean * mean
        inverse = 1.0 / jnp.sqrt(var + 1e-06)
        for col in range(cols):
            span = pl.ds(col * wc, wc)
            part = xv[col, rows, :].astype(jnp.float32)
            shift = mod_ref[slot, 0:1, span]
            scale = mod_ref[slot, 1:2, span]
            xm[rows, span] = ((part - mean) * inverse * (1.0 + scale) + shift).astype(jnp.bfloat16)
    for copy in w_copies[0] + w_copies[1] + kv_copies:
        copy.wait()
    contract = (((1,), (1,)), ((), ()))

    def normed(block):
        return (
            block / jnp.sqrt(jnp.mean(block * block, axis=-1, keepdims=True) + 1e-06)
        ).astype(jnp.bfloat16)

    for slot in range(slots):
        rows = pl.ds(slot * slot_len, slot_len)
        raw = [jnp.dot(xm[rows, :], wv[t], preferred_element_type=jnp.float32) for t in range(2)]
        fresh, valid = fresh_and_valid(ends_ref, slot, slot_len)
        for head in range(bw // HD):
            lanes = slice(head * HD, (head + 1) * HD)
            query, key = normed(raw[0][:, lanes]), normed(raw[1][:, lanes])
            new_scores = lax.dot_general(query, key, contract, preferred_element_type=jnp.float32)
            old_scores = lax.dot_general(
                query, kvv[slot, :, lanes], contract, preferred_element_type=jnp.float32
            )
            scores = jnp.where(fresh, new_scores, old_scores) * (1.0 / math.sqrt(HD))
            weights = jnp.where(valid, jnp.exp(scores), 0.0)
            weights = weights / jnp.sum(weights, axis=-1, keepdims=True)
            weights_ref[slot, head] = weights.astype(jnp.bfloat16)


def mix_kernel(plan, ends_ref, xm_ref, weights_ref, *refs):
    slots, slot_len, cols, n_w, kr, nr, bw, wc = plan
    v_refs, o_refs, refs = refs[:n_w], refs[n_w : 2 * n_w], refs[2 * n_w :]
    kv_refs, refs = refs[:slots], refs[slots:]
    keep_ref, pass_ref, wv, ov, kvv, att, w_sem, kv_sem = refs
    s, i, c = (lax.axis_index(axis) for axis in AXES)
    half = slot_len // 2
    copies = load_rows(v_refs, wv, w_sem, 0, kr)
    for slot in range(slots):
        copies.append(
            pltpu.make_async_copy(kv_refs[slot].at[1], kvv.at[slot], kv_sem.at[slot])
        )
        copies[-1].start()
    o_copies = load_rows(o_refs, ov, w_sem, n_w, None)
    for copy in copies:
        copy.wait()
    for slot in range(slots):
        rows = pl.ds(slot * slot_len, slot_len)
        raw = jnp.dot(xm_ref[rows, :], wv[...], preferred_element_type=jnp.float32)
        value = raw.astype(jnp.bfloat16)
        fresh, _ = fresh_and_valid(ends_ref, slot, slot_len)
        for head in range(bw // HD):
            lanes = slice(head * HD, (head + 1) * HD)
            weights = weights_ref[slot, head]
            none = jnp.zeros_like(weights)
            mixed = jnp.dot(
                jnp.where(fresh, weights, none),
                value[:, lanes],
                preferred_element_type=jnp.float32,
            ) + jnp.dot(
                jnp.where(fresh, none, weights),
                kvv[slot, :, lanes],
                preferred_element_type=jnp.float32,
            )
            att[rows, lanes] = mixed.astype(jnp.bfloat16)
    for copy in o_copies:
        copy.wait()
    blocks = []
    for side in (s, 1 - s):
        for slot in range(slots):
            row = pl.multiple_of(slot * slot_len + side * half, half)
            blocks.append(att[pl.ds(row, half), :])
    lhs = jnp.concatenate(blocks, axis=0)
    for place in range(n_w):
        row = lax.rem(c * (n_w // cols) + place, n_w)
        part = jnp.dot(lhs, ov[row], preferred_element_type=jnp.float32).astype(jnp.bfloat16)
        part = part.reshape(2, slots, half, nr)
        lanes = slice(place * nr, (place + 1) * nr)
        keep_ref[:, :, lanes] = part[0]
        pass_ref[:, :, lanes] = part[1]


def mod_kernel(slots, feats_ref, weight_ref, out_ref):
    for k in range(3):
        part = jnp.dot(feats_ref[...], weight_ref[k], preferred_element_type=jnp.float32)
        for slot in range(slots):
            out_ref[slot, k : k + 1, :] = part[slot : slot + 1, :]


GATES = {
    "V0.4": ("Q0.4",),
    "V0.6": ("Q0.6",),
    "O0.4": ("K0.4",),
    "O0.6": ("K0.6",),
    "Q1.4": ("V0.4",),
    "Q1.6": ("V0.6",),
    "K1.4": ("O0.4",),
    "K1.6": ("O0.6",),
    "V1.4": ("Q1.4",),
    "V1.6": ("Q1.6",),
    "O1.4": ("K1.4",),
    "O1.6": ("K1.6",),
    "O0.2": ("Q0.2",),
    "Q1.2": ("K0.2",),
    "K1.2": ("S0.2",),
    "V1.2": ("V0.2",),
    "O1.2": ("O0.2",),
    "S1.2": ("Q1.2",),
    "K0.1": ("Q0.1",),
    "K0.3": ("Q0.3",),
    "Q0.5": ("K0.1",),
    "Q0.7": ("K0.3",),
    "V0.1": ("Q0.5",),
    "V0.3": ("Q0.7",),
    "K0.5": ("V0.1",),
    "K0.7": ("V0.3",),
    "O0.1": ("K0.5",),
    "O0.3": ("K0.7",),
    "V0.5": ("O0.1",),
    "V0.7": ("O0.3",),
    "Q1.1": ("V0.5",),
    "Q1.3": ("V0.7",),
    "O0.5": ("Q1.1",),
    "O0.7": ("Q1.3",),
    "K1.1": ("O0.5",),
    "K1.3": ("O0.7",),
    "Q1.5": ("K1.1",),
    "Q1.7": ("K1.3",),
    "V1.1": ("Q1.5",),
    "V1.3": ("Q1.7",),
    "K1.5": ("V1.1",),
    "K1.7": ("V1.3",),
    "O1.1": ("K1.5",),
    "O1.3": ("K1.7",),
    "V1.5": ("O1.1",),
    "V1.7": ("O1.3",),
    "O1.5": ("V1.5",),
    "O1.7": ("V1.7",),
    "n": ("aQ",),
    "x.0.0": ("Q0.4",),
    "m": ("Q0.6",),
    "p0": ("Q1.4", "Q1.6",),
    "r0.0.1": ("K1.4",),
    "g.2.0": ("K1.6",),
    "k0": ("Q1.2",),
}
TREE = ("x", "r0", "g", )


def shards(
    hidden_in, patch_ends, timestep, mod_weight, qkv_weight, out_weight, stale_keys, stale_values
):
    s, i, c = (lax.axis_index(axis) for axis in AXES)
    sections, rows, cols = (lax.axis_size(axis) for axis in AXES)
    _, slot_len, wc = hidden_in.shape
    feat = mod_weight.shape[-1]
    kr, nr = qkv_weight.shape[1], out_weight.shape[2]
    half = slot_len // 2
    slots = 2 if (wc // HD) % (2 * sections) == 0 else 1
    bw = wc // (sections * slots)
    pair_bit = 2 if slots == 2 else 0
    group_bits = [1 << b for b in reversed(range(rows.bit_length() - 1)) if 1 << b != pair_bit]
    first_bit, last_bits = group_bits[0], group_bits[1:]
    offsets = [0, pair_bit] if slots == 2 else [0]
    places = [(di, dc) for di in offsets for dc in range(cols)]
    mine_at = (i // 2) % 2 if slots == 2 else 0
    gates = GATES if rows == 8 and slots == 2 else {}
    made, steps = {}, {}

    def get(name):
        if name not in made:
            made[name] = None
            made[name] = steps[name]()
        return made[name]

    def gated(array, name):
        waits = [get(other) for other in gates.get(name, ())]
        return after(array, *waits) if waits else array

    def send(name, array, di=0, dc=0):
        def where(si, ii, ci):
            return si, ii ^ di, (ci + dc) % cols

        return send_to(gated(array, name), where)

    def swap(name, array):
        return send_to(gated(array, name), lambda si, ii, ci: (1 - si, ii, ci))

    def step(name):
        def note(make):
            steps[name] = make
            return make

        return note

    wide = slots * bw
    qkv = qkv_weight[0].transpose(1, 0, 2)
    stale = (stale_keys[0, 0], stale_values[0, 0])

    def columns(array, start, width):
        return lax.dynamic_slice_in_dim(array, start, width, array.ndim - 1)

    def cut(kind, start, width):
        if kind == "O":
            return lax.dynamic_slice_in_dim(out_weight[0], start, width, 0)
        if kind == "S":
            return jnp.concatenate([columns(one, start, width) for one in stale])
        return columns(qkv["QKV".index(kind)], start, width)

    def block_of(kind, layer, slot):
        at = (mine_at if slot == 0 else 1 - mine_at) * bw
        got = get("a" + kind)
        other = lax.dynamic_slice_in_dim(got, at, bw, 0) if kind == "O" else columns(got, at, bw)
        block = jnp.where(s == layer, cut(kind, s * wide + at, bw), other)
        return block.reshape(2, slot_len, bw) if kind == "S" else block

    for kind in "QKVOS":
        step("a" + kind)(
            lambda kind=kind: swap("a" + kind, cut(kind, (1 - s) * wide, wide))
        )

    def move(kind, layer, d):
        name = f"{kind}{layer}.{d}"
        for bit in reversed(last_bits):
            if d & bit:
                return send(name, get(f"{kind}{layer}.{d ^ bit}"), bit)
        block = block_of(kind, layer, 1 if d & pair_bit else 0)
        return send(name, block, d) if d else gated(block, name)

    for layer in range(2):
        for kind in "QKVO":
            for d in range(rows):
                step(f"{kind}{layer}.{d}")(functools.partial(move, kind, layer, d))
        for d in offsets:
            step(f"S{layer}.{d}")(functools.partial(move, "S", layer, d))

    def of_rows(kind, layer):
        return [get(f"{kind}{layer}.{d}") for d in range(rows)]

    def stale_of(layer):
        return [get(f"S{layer}.{d}") for d in offsets]

    @step("n")
    def _():
        numbers = jnp.concatenate([patch_ends[0], timestep])
        return jnp.stack([numbers] + [send("n", numbers, di) for di in offsets[1:]])

    @step("m")
    def _():
        feats = jnp.pad(embed_time(get("n")[:, NP]), ((0, 8 - slots), (0, 0)))
        own = pl.pallas_call(
            functools.partial(mod_kernel, slots),
            out_shape=jax.ShapeDtypeStruct((slots, 3, feat), jnp.float32),
            in_specs=[vmem_spec(), vmem_spec()],
            out_specs=vmem_spec(),
            compiler_params=pltpu.CompilerParams(vmem_limit_bytes=VMEM_LIMIT),
            name="modulation",
        )(gated(feats, "m"), mod_weight[0].transpose(1, 0, 2))
        other = swap("mc", own)
        return [jnp.where(s == layer, own, other) for layer in range(2)]

    x_half = lax.dynamic_slice_in_dim(hidden_in[0], s * half, half, 0)
    step("x.0.0")(lambda: gated(x_half, "x.0.0"))
    step("g.0.0")(lambda: finish(0, x_half))
    for kind in "xg":
        for di, dc in places:
            name = f"{kind}.{di}.{dc}"

            def bring(kind=kind, name=name, di=di, dc=dc):
                if dc and kind in TREE:
                    return send(name, get(f"{kind}.{di}.0"), 0, dc)
                return send(name, get(f"{kind}.0.0"), di, dc)

            if (di, dc) != (0, 0):
                step(name)(bring)
            step(name + "c")(lambda name=name: swap(name + "c", get(name)))

    def x_pieces(kind):
        return [get(f"{kind}.{di}.{dc}" + end) for di, dc in places for end in ("", "c")]

    def scores(layer):
        pieces = x_pieces("xg"[layer])
        plan = (slots, slot_len, cols, len(pieces), rows, kr, bw, wc)
        return pl.pallas_call(
            functools.partial(scores_kernel, plan),
            out_shape=(
                jax.ShapeDtypeStruct((slots * slot_len, feat), jnp.bfloat16),
                jax.ShapeDtypeStruct((slots, bw // HD, slot_len, slot_len), jnp.bfloat16),
            ),
            in_specs=[pl.BlockSpec(memory_space=pltpu.SMEM), vmem_spec()]
            + [any_spec()] * (len(pieces) + 2 * rows + slots),
            out_specs=(vmem_spec(), vmem_spec()),
            scratch_shapes=[
                pltpu.VMEM((cols, slots * slot_len, wc), jnp.bfloat16),
                pltpu.VMEM((2, feat, bw), jnp.bfloat16),
                pltpu.VMEM((slots, slot_len, bw), jnp.bfloat16),
                pltpu.SemaphoreType.DMA((len(pieces),)),
                pltpu.SemaphoreType.DMA((2 * rows,)),
                pltpu.SemaphoreType.DMA((slots,)),
            ],
            compiler_params=pltpu.CompilerParams(vmem_limit_bytes=VMEM_LIMIT),
            name="scores",
        )(
            gated(get("n")[:, :NP], f"k{layer}"),
            get("m")[layer],
            *pieces,
            *of_rows("Q", layer),
            *of_rows("K", layer),
            *stale_of(layer),
        )

    def mix(layer):
        plan = (slots, slot_len, cols, rows, kr, nr, bw, wc)
        shape = jax.ShapeDtypeStruct((slots, half, feat), jnp.bfloat16)
        return pl.pallas_call(
            functools.partial(mix_kernel, plan),
            out_shape=(shape, shape),
            in_specs=[pl.BlockSpec(memory_space=pltpu.SMEM), vmem_spec(), vmem_spec()]
            + [any_spec()] * (2 * rows + slots),
            out_specs=(vmem_spec(), vmem_spec()),
            scratch_shapes=[
                pltpu.VMEM((feat, bw), jnp.bfloat16),
                pltpu.VMEM((rows, bw, nr), jnp.bfloat16),
                pltpu.VMEM((slots, slot_len, bw), jnp.bfloat16),
                pltpu.VMEM((slots * slot_len, bw), jnp.bfloat16),
                pltpu.SemaphoreType.DMA((2 * rows,)),
                pltpu.SemaphoreType.DMA((slots,)),
            ],
            compiler_params=pltpu.CompilerParams(vmem_limit_bytes=VMEM_LIMIT),
            name="mix",
        )(
            gated(get("n")[:, :NP], f"v{layer}"),
            *get(f"k{layer}"),
            *of_rows("V", layer),
            *of_rows("O", layer),
            *stale_of(layer),
        )

    def parts(layer):
        keep, passed = get(f"v{layer}")
        total = keep.astype(jnp.float32) + get(f"p{layer}").astype(jnp.float32)
        return {
            (di, dc): total[offsets.index(di), :, dc * wc : (dc + 1) * wc] for di, dc in places
        }

    def summed(layer, di):
        part = get(f"t{layer}")[di, 0]
        for dc in range(1, cols):
            part = part + get(f"r{layer}.{di}.{dc}").astype(jnp.float32)
        return part

    def give(layer, di, dc):
        name = f"r{layer}.{di}.{dc}"
        if f"r{layer}" not in TREE:
            return send(name, get(f"t{layer}")[di, dc].astype(jnp.bfloat16), di, dc)
        if dc:
            return send(name, get(f"t{layer}")[di, dc].astype(jnp.bfloat16), 0, dc)
        return send(name, get(f"u{layer}.{di}").astype(jnp.bfloat16), di, 0)

    for layer in range(2):
        step(f"k{layer}")(functools.partial(scores, layer))
        step(f"v{layer}")(functools.partial(mix, layer))
        step(f"p{layer}")(lambda layer=layer: swap(f"p{layer}", get(f"v{layer}")[1]))
        step(f"t{layer}")(functools.partial(parts, layer))
        for di, dc in places:
            if (di, dc) != (0, 0):
                step(f"r{layer}.{di}.{dc}")(functools.partial(give, layer, di, dc))
        for di in offsets:
            step(f"u{layer}.{di}")(functools.partial(summed, layer, di))

    def finish(layer, x_own):
        if f"r{layer}" in TREE:
            branch = get(f"u{layer}.0")
            for di in offsets[1:]:
                branch = branch + get(f"r{layer}.{di}.0").astype(jnp.float32)
        else:
            branch = get(f"t{layer}")[0, 0]
            for di, dc in places[1:]:
                branch = branch + get(f"r{layer}.{di}.{dc}").astype(jnp.float32)
        gate_own = columns(get("m")[layer][0, 2], c * wc, wc)
        updated = x_own.astype(jnp.float32) + gate_own[None, :] * branch
        positions = jnp.arange(half)[:, None] + s * half
        return jnp.where(positions < patch_ends[0, NP - 1], updated, 0.0).astype(jnp.bfloat16)

    first = get("g.0.0")
    second = finish(1, first)
    low = jnp.where(s == 0, first, swap("e", second))
    high = jnp.where(s == 0, get("g.0.0c"), second)
    return jnp.concatenate([low, high], axis=0)[None, None]


def solution(mesh):
    return jax.shard_map(
        shards,
        mesh=mesh,
        in_specs=(
            P("row", None, "col"),
            P("row", None),
            P("row"),
            P("section", None, None, None),
            P("section", "row", None, "col"),
            P("section", "col", "row"),
            P("section", "row", None, "col"),
            P("section", "row", None, "col"),
        ),
        out_specs=P("section", "row", None, "col"),
        check_vma=False,
    )
```

profile of v0, /device:TPU:0, one launch (start us, length us, event | category | flops | bytes accessed | tf_op | source)
XLA Modules:
  0.0 346.2 jit_solution(13592766056953274059)
XLA Ops:
  15.0 3.3 collective-permute-done.16.refs_10_
  23.9 4.6 %collective-permute-done.5.refs_18_ = bf16[384,384]{1,0:T(8,128)(2,1)S(1)} collective-permute-done((bf16[384,384]{1,0:T(8,128)(2,1)}, bf16[384,384]{1,0:T(8,128)(2,1)S(1)}, u32[]{:S(2)}, u32[]{:S(2)}) %collective-permute-start.5) | collective-permute-done | bytes 294944 | tf_op jit(solution)/shard_map/ppermute | solution.py:26
  34.5 8.5 %collective-permute-done.7.refs_12_ = bf16[384,384]{1,0:T(8,128)(2,1)S(1)} collective-permute-done((bf16[384,384]{1,0:T(8,128)(2,1)S(1)}, bf16[384,384]{1,0:T(8,128)(2,1)S(1)}, u32[]{:S(2)}, u32[]{:S(2)}) %collective-permute-start.7) | collective-permute-done | bytes 294944 | tf_op jit(solution)/shard_map/ppermute | solution.py:26
  46.0 4.9 %collective-permute-start.22 = (bf16[384,384]{1,0:T(8,128)(2,1)S(1)}, bf16[384,384]{1,0:T(8,128)(2,1)}, u32[]{:S(2)}, u32[]{:S(2)}) collective-permute-start(bf16[384,384]{1,0:T(8,128)(2,1)S(1)} %get-tuple-element.73.refs_16_), channel_id=1, source_target_pairs={{0,8},{1,9},{2,10},{3,11},{4,12},{5,13},{6,14},{7,15},{8,0},{9,1},... | collective-permute-start | bytes 884744 | tf_op jit(solution)/shard_map/ppermute | solution.py:26
  50.9 4.7 %collective-permute-start.26 = (bf16[384,384]{1,0:T(8,128)(2,1)}, bf16[384,384]{1,0:T(8,128)(2,1)}, u32[]{:S(2)}, u32[]{:S(2)}) collective-permute-start(bf16[384,384]{1,0:T(8,128)(2,1)} %get-tuple-element.150), channel_id=1, source_target_pairs={{0,12},{1,13},{2,14},{3,15},{4,8},{5,9},{6,10},{7,11},{8,4},{9,5},... | collective-permute-start | bytes 884744 | tf_op jit(solution)/shard_map/ppermute | solution.py:26
  60.9 9.7 %collective-permute-done.22.refs_20_ = bf16[384,384]{1,0:T(8,128)(2,1)} collective-permute-done((bf16[384,384]{1,0:T(8,128)(2,1)S(1)}, bf16[384,384]{1,0:T(8,128)(2,1)}, u32[]{:S(2)}, u32[]{:S(2)}) %collective-permute-start.22) | collective-permute-done | bytes 294944 | tf_op jit(solution)/shard_map/ppermute | solution.py:26
  73.4 3.5 %collective-permute-start.32 = (bf16[384,384]{1,0:T(8,128)(2,1)S(1)}, bf16[384,384]{1,0:T(8,128)(2,1)S(1)}, u32[]{:S(2)}, u32[]{:S(2)}) collective-permute-start(bf16[384,384]{1,0:T(8,128)(2,1)S(1)} %get-tuple-element.83.refs_0_), channel_id=1, source_target_pairs={{0,8},{1,9},{2,10},{3,11},{4,12},{5,13},{6,14},{7,15},{8,0},{9,1},... | collective-permute-start | bytes 884744 | tf_op jit(solution)/shard_map/ppermute | solution.py:26
  79.0 3.6 %collective-permute-start.1 = (s32[5]{0:T(128)S(1)}, s32[5]{0:T(128)S(1)}, u32[]{:S(2)}, u32[]{:S(2)}) collective-permute-start(s32[5]{0:T(128)S(1)} %pad_add_fusion.1), channel_id=1, source_target_pairs={{0,4},{1,5},{2,6},{3,7},{4,0},{5,1},{6,2},{7,3},{8,12},{9,13},{10,... | collective-permute-start | bytes 68 | tf_op jit(solution)/shard_map/ppermute | solution.py:26
  86.2 11.2 %collective-permute-done.32.refs_4_ = bf16[384,384]{1,0:T(8,128)(2,1)S(1)} collective-permute-done((bf16[384,384]{1,0:T(8,128)(2,1)S(1)}, bf16[384,384]{1,0:T(8,128)(2,1)S(1)}, u32[]{:S(2)}, u32[]{:S(2)}) %collective-permute-start.32) | collective-permute-done | bytes 294944 | tf_op jit(solution)/shard_map/ppermute | solution.py:26
  102.9 5.8 %collective-permute-done.6.refs_10_ = bf16[384,384]{1,0:T(8,128)(2,1)S(1)} collective-permute-done((bf16[384,384]{1,0:T(8,128)(2,1)S(1)}, bf16[384,384]{1,0:T(8,128)(2,1)S(1)}, u32[]{:S(2)}, u32[]{:S(2)}) %collective-permute-start.6) | collective-permute-done | bytes 294944 | tf_op jit(solution)/shard_map/ppermute | solution.py:26
  110.5 3.8 %modulation.1 = f32[2,3,3072]{2,1,0:T(4,128)} custom-call(bf16[8,256]{1,0:T(8,128)(2,1)} %fusion.19.feats_ref, bf16[3,256,3072]{2,1,0:T(8,128)(2,1)} %bitcast.113), custom_call_target="tpu_custom_call" | custom-call | tf_op jit(solution)/shard_map/modulation/pallas_call | solution.py:375
  120.6 5.7 %collective-permute-done.43.refs_14_ = bf16[384,384]{1,0:T(8,128)(2,1)S(1)} collective-permute-done((bf16[384,384]{1,0:T(8,128)(2,1)}, bf16[384,384]{1,0:T(8,128)(2,1)S(1)}, u32[]{:S(2)}, u32[]{:S(2)}) %collective-permute-start.43) | collective-permute-done | bytes 294944 | tf_op jit(solution)/shard_map/ppermute | solution.py:26
  126.3 5.1 %collective-permute-start.31 = (bf16[2,256,384]{2,1,0:T(8,128)(2,1)S(1)}, bf16[2,256,384]{2,1,0:T(8,128)(2,1)S(1)}, u32[]{:S(2)}, u32[]{:S(2)}) collective-permute-start(bf16[2,256,384]{2,1,0:T(8,128)(2,1)S(1)} %bitcast.120), channel_id=1, source_target_pairs={{0,4},{1,5},{2,6},{3,7},{4,0},{5,1},{6,2},{7,3},{8,12},{9,13},{10,... | collective-permute-start | bytes 1179656 | tf_op jit(solution)/shard_map/ppermute | solution.py:26
  133.8 5.2 %collective-permute-done.31.refs_25_.refs_17_ = bf16[2,256,384]{2,1,0:T(8,128)(2,1)S(1)} collective-permute-done((bf16[2,256,384]{2,1,0:T(8,128)(2,1)S(1)}, bf16[2,256,384]{2,1,0:T(8,128)(2,1)S(1)}, u32[]{:S(2)}, u32[]{:S(2)}) %collective-permute-start.31) | collective-permute-done | bytes 393248 | tf_op jit(solution)/shard_map/ppermute | solution.py:26
  139.0 4.0 %collective-permute-start.46 = (bf16[384,384]{1,0:T(8,128)(2,1)S(1)}, bf16[384,384]{1,0:T(8,128)(2,1)S(1)}, u32[]{:S(2)}, u32[]{:S(2)}) collective-permute-start(bf16[384,384]{1,0:T(8,128)(2,1)S(1)} %copy-done.7), channel_id=1, source_target_pairs={{0,8},{1,9},{2,10},{3,11},{4,12},{5,13},{6,14},{7,15},{8,0},{9,1},... | collective-permute-start | bytes 884744 | tf_op jit(solution)/shard_map/ppermute | solution.py:26
  146.8 12.8 %scores.2 = (bf16[512,3072]{1,0:T(8,128)(2,1)}, bf16[2,3,256,256]{3,2,1,0:T(8,128)(2,1)}) custom-call(s32[2,4]{1,0:T(2,128)} %bitcast.121, f32[2,3,3072]{2,1,0:T(4,128)} %get-tuple-element.172.mod_ref, bf16[128,1536]{1,0:T(8,128)(2,1)} %copy-done.4, bf16[128,1536]{1,0:T(8,128)(2,1)} %copy-done.25, bf16[128,1536]{1,0:T(8,128)(2,1)} %copy-done.20, ...), custom_call_target="tpu_custom_call" | custom-call | tf_op jit(solution)/shard_map/scores/pallas_call | solution.py:408
  160.4 10.1 %mix.2 = (bf16[2,128,3072]{2,1,0:T(8,128)(2,1)}, bf16[2,128,3072]{2,1,0:T(8,128)(2,1)}) custom-call(s32[2,4]{1,0:T(2,128)} %bitcast.122, bf16[512,3072]{1,0:T(8,128)(2,1)} %get-tuple-element.81.xm_ref, bf16[2,3,256,256]{3,2,1,0:T(8,128)(2,1)} %get-tuple-element.82.weights_ref, bf16[384,384]{1,0:T(8,128)(2,1)} %copy-done.12, ...), custom_call_target="tpu_custom_call" | custom-call | tf_op jit(solution)/shard_map/mix/pallas_call | solution.py:439
  186.7 3.5 %collective-permute-done.64.refs_19_ = bf16[384,384]{1,0:T(8,128)(2,1)S(1)} collective-permute-done((bf16[384,384]{1,0:T(8,128)(2,1)S(1)}, bf16[384,384]{1,0:T(8,128)(2,1)S(1)}, u32[]{:S(2)}, u32[]{:S(2)}) %collective-permute-start.64) | collective-permute-done | bytes 294944 | tf_op jit(solution)/shard_map/ppermute | solution.py:26
  191.1 5.5 %collective-permute-done.62.refs_13_ = bf16[384,384]{1,0:T(8,128)(2,1)S(1)} collective-permute-done((bf16[384,384]{1,0:T(8,128)(2,1)S(1)}, bf16[384,384]{1,0:T(8,128)(2,1)S(1)}, u32[]{:S(2)}, u32[]{:S(2)}) %collective-permute-start.62) | collective-permute-done | bytes 294944 | tf_op jit(solution)/shard_map/ppermute | solution.py:26
  204.5 4.7 %collective-permute-done.66.refs_1_ = bf16[384,384]{1,0:T(8,128)(2,1)S(1)} collective-permute-done((bf16[384,384]{1,0:T(8,128)(2,1)S(1)}, bf16[384,384]{1,0:T(8,128)(2,1)S(1)}, u32[]{:S(2)}, u32[]{:S(2)}) %collective-permute-start.66) | collective-permute-done | bytes 294944 | tf_op jit(solution)/shard_map/ppermute | solution.py:26
  212.8 6.3 %collective-permute-done.56.refs_22_ = bf16[384,384]{1,0:T(8,128)(2,1)} collective-permute-done((bf16[384,384]{1,0:T(8,128)(2,1)}, bf16[384,384]{1,0:T(8,128)(2,1)}, u32[]{:S(2)}, u32[]{:S(2)}) %collective-permute-start.56) | collective-permute-done | bytes 294944 | tf_op jit(solution)/shard_map/ppermute | solution.py:26
  220.6 3.7 %collective-permute-start.75 = (bf16[384,384]{1,0:T(8,128)(2,1)}, bf16[384,384]{1,0:T(8,128)(2,1)S(1)}, u32[]{:S(2)}, u32[]{:S(2)}) collective-permute-start(bf16[384,384]{1,0:T(8,128)(2,1)} %get-tuple-element.121), channel_id=1, source_target_pairs={{0,12},{1,13},{2,14},{3,15},{4,8},{5,9},{6,10},{7,11},{8,4},{9,5},... | collective-permute-start | bytes 884744 | tf_op jit(solution)/shard_map/ppermute | solution.py:26
  227.8 5.3 %collective-permute-done.76.refs_10_ = bf16[384,384]{1,0:T(8,128)(2,1)S(1)} collective-permute-done((bf16[384,384]{1,0:T(8,128)(2,1)}, bf16[384,384]{1,0:T(8,128)(2,1)S(1)}, u32[]{:S(2)}, u32[]{:S(2)}) %collective-permute-start.76) | collective-permute-done | bytes 294944 | tf_op jit(solution)/shard_map/ppermute | solution.py:26
  234.8 7.9 %collective-permute-done.72.refs_4_ = bf16[384,384]{1,0:T(8,128)(2,1)S(1)} collective-permute-done((bf16[384,384]{1,0:T(8,128)(2,1)S(1)}, bf16[384,384]{1,0:T(8,128)(2,1)S(1)}, u32[]{:S(2)}, u32[]{:S(2)}) %collective-permute-start.72) | collective-permute-done | bytes 294944 | tf_op jit(solution)/shard_map/ppermute | solution.py:26
  251.0 17.0 %collective-permute-done.79.refs_12_ = bf16[384,384]{1,0:T(8,128)(2,1)S(1)} collective-permute-done((bf16[384,384]{1,0:T(8,128)(2,1)S(1)}, bf16[384,384]{1,0:T(8,128)(2,1)S(1)}, u32[]{:S(2)}, u32[]{:S(2)}) %collective-permute-start.79) | collective-permute-done | bytes 294944 | tf_op jit(solution)/shard_map/ppermute | solution.py:26
  268.0 5.0 %collective-permute-start.71 = (bf16[2,256,384]{2,1,0:T(8,128)(2,1)S(1)}, bf16[2,256,384]{2,1,0:T(8,128)(2,1)S(1)}, u32[]{:S(2)}, u32[]{:S(2)}) collective-permute-start(bf16[2,256,384]{2,1,0:T(8,128)(2,1)S(1)} %bitcast.119), channel_id=1, source_target_pairs={{0,4},{1,5},{2,6},{3,7},{4,0},{5,1},{6,2},{7,3},{8,12},{9,13},{10,... | collective-permute-start | bytes 1179656 | tf_op jit(solution)/shard_map/ppermute | solution.py:26
  275.3 5.3 %collective-permute-done.71.refs_25_.refs_17_ = bf16[2,256,384]{2,1,0:T(8,128)(2,1)S(1)} collective-permute-done((bf16[2,256,384]{2,1,0:T(8,128)(2,1)S(1)}, bf16[2,256,384]{2,1,0:T(8,128)(2,1)S(1)}, u32[]{:S(2)}, u32[]{:S(2)}) %collective-permute-start.71) | collective-permute-done | bytes 393248 | tf_op jit(solution)/shard_map/ppermute | solution.py:26
  283.7 21.8 %scores.3 = (bf16[512,3072]{1,0:T(8,128)(2,1)}, bf16[2,3,256,256]{3,2,1,0:T(8,128)(2,1)}) custom-call(s32[2,4]{1,0:T(2,128)} %bitcast.123, f32[2,3,3072]{2,1,0:T(4,128)} %get-tuple-element.171.mod_ref, bf16[128,1536]{1,0:T(8,128)(2,1)} %copy-done, bf16[128,1536]{1,0:T(8,128)(2,1)} %copy-done.5, bf16[128,1536]{1,0:T(8,128)(2,1)} %copy-done.23, ...), custom_call_target="tpu_custom_call" | custom-call | tf_op jit(solution)/shard_map/scores/pallas_call | solution.py:408
  306.3 10.1 %mix.3 = (bf16[2,128,3072]{2,1,0:T(8,128)(2,1)}, bf16[2,128,3072]{2,1,0:T(8,128)(2,1)}) custom-call(s32[2,4]{1,0:T(2,128)} %bitcast.124, bf16[512,3072]{1,0:T(8,128)(2,1)} %get-tuple-element.116.xm_ref, bf16[2,3,256,256]{3,2,1,0:T(8,128)(2,1)} %get-tuple-element.117.weights_ref, bf16[384,384]{1,0:T(8,128)(2,1)} %get-tuple-element.118.refs_0_, ...), custom_call_target="tpu_custom_call" | custom-call | tf_op jit(solution)/shard_map/mix/pallas_call | solution.py:439
  316.5 3.6 %collective-permute-done.83 = bf16[2,128,3072]{2,1,0:T(8,128)(2,1)S(1)} collective-permute-done((bf16[2,128,3072]{2,1,0:T(8,128)(2,1)}, bf16[2,128,3072]{2,1,0:T(8,128)(2,1)S(1)}, u32[]{:S(2)}, u32[]{:S(2)}) %collective-permute-start.83) | collective-permute-done | bytes 1572896 | tf_op jit(solution)/shard_map/ppermute | solution.py:26
  326.7 8.6 %collective-permute-done.86 = bf16[128,1536]{1,0:T(8,128)(2,1)S(1)} collective-permute-done((bf16[128,1536]{1,0:T(8,128)(2,1)S(1)}, bf16[128,1536]{1,0:T(8,128)(2,1)S(1)}, u32[]{:S(2)}, u32[]{:S(2)}) %collective-permute-start.86) | collective-permute-done | bytes 393248 | tf_op jit(solution)/shard_map/ppermute | solution.py:26
  335.3 7.1 %collective-permute-done.85 = bf16[128,1536]{1,0:T(8,128)(2,1)S(1)} collective-permute-done((bf16[128,1536]{1,0:T(8,128)(2,1)S(1)}, bf16[128,1536]{1,0:T(8,128)(2,1)S(1)}, u32[]{:S(2)}, u32[]{:S(2)}) %collective-permute-start.85) | collective-permute-done | bytes 393248 | tf_op jit(solution)/shard_map/ppermute | solution.py:26
  (364 shorter events, 122.3 us)
Async XLA Ops:
  10.6 22.9 %collective-permute-start.23 = (bf16[384,768]{1,0:T(8,128)(2,1)S(1)}, bf16[384,768]{1,0:T(8,128)(2,1)S(1)}, u32[]{:S(2)}, u32[]{:S(2)}) collective-permute-start(bf16[384,768]{1,0:T(8,128)(2,1)S(1)} %dynamic-slice_bitcast_fusion.1), channel_id=1, source_target_pairs={{0,16},{1,17},{2,18},{3,19},{4,20},{5,21},{6,22},{7,23},{8,24},{9,... | collective-permute-start | bytes 1769480 | tf_op jit(solution)/shard_map/ppermute | solution.py:26
  20.4 22.7 %collective-permute-start.7 = (bf16[384,384]{1,0:T(8,128)(2,1)S(1)}, bf16[384,384]{1,0:T(8,128)(2,1)S(1)}, u32[]{:S(2)}, u32[]{:S(2)}) collective-permute-start(bf16[384,384]{1,0:T(8,128)(2,1)S(1)} %get-tuple-element.153.refs_8_), channel_id=1, source_target_pairs={{0,8},{1,9},{2,10},{3,11},{4,12},{5,13},{6,14},{7,15},{8,0},{9,1},... | collective-permute-start | bytes 884744 | tf_op jit(solution)/shard_map/ppermute | solution.py:26
  23.7 19.4 %collective-permute-start.18 = (bf16[384,384]{1,0:T(8,128)(2,1)S(1)}, bf16[384,384]{1,0:T(8,128)(2,1)S(1)}, u32[]{:S(2)}, u32[]{:S(2)}) collective-permute-start(bf16[384,384]{1,0:T(8,128)(2,1)S(1)} %get-tuple-element.73.refs_16_), channel_id=1, source_target_pairs={{0,2},{1,3},{2,0},{3,1},{4,6},{5,7},{6,4},{7,5},{8,10},{9,11},{10,... | collective-permute-start | bytes 884744 | tf_op jit(solution)/shard_map/ppermute | solution.py:26
  28.6 16.4 %collective-permute-start.2 = (bf16[384,384]{1,0:T(8,128)(2,1)S(1)}, bf16[384,384]{1,0:T(8,128)(2,1)S(1)}, u32[]{:S(2)}, u32[]{:S(2)}) collective-permute-start(bf16[384,384]{1,0:T(8,128)(2,1)S(1)} %get-tuple-element.154), channel_id=1, source_target_pairs={{0,12},{1,13},{2,14},{3,15},{4,8},{5,9},{6,10},{7,11},{8,4},{9,5},... | collective-permute-start | bytes 884744 | tf_op jit(solution)/shard_map/ppermute | solution.py:26
  33.5 25.1 %collective-permute-start.33 = (bf16[768,384]{1,0:T(8,128)(2,1)}, bf16[768,384]{1,0:T(8,128)(2,1)}, u32[]{:S(2)}, u32[]{:S(2)}) collective-permute-start(bf16[768,384]{1,0:T(8,128)(2,1)} %dynamic-slice_bitcast_fusion), channel_id=1, source_target_pairs={{0,16},{1,17},{2,18},{3,19},{4,20},{5,21},{6,22},{7,23},{8,24},{9,... | collective-permute-start | bytes 1769480 | tf_op jit(solution)/shard_map/ppermute | solution.py:26
  46.0 24.5 %collective-permute-start.22 = (bf16[384,384]{1,0:T(8,128)(2,1)S(1)}, bf16[384,384]{1,0:T(8,128)(2,1)}, u32[]{:S(2)}, u32[]{:S(2)}) collective-permute-start(bf16[384,384]{1,0:T(8,128)(2,1)S(1)} %get-tuple-element.73.refs_16_), channel_id=1, source_target_pairs={{0,8},{1,9},{2,10},{3,11},{4,12},{5,13},{6,14},{7,15},{8,0},{9,1},... | collective-permute-start | bytes 884744 | tf_op jit(solution)/shard_map/ppermute | solution.py:26
  50.9 20.8 %collective-permute-start.26 = (bf16[384,384]{1,0:T(8,128)(2,1)}, bf16[384,384]{1,0:T(8,128)(2,1)}, u32[]{:S(2)}, u32[]{:S(2)}) collective-permute-start(bf16[384,384]{1,0:T(8,128)(2,1)} %get-tuple-element.150), channel_id=1, source_target_pairs={{0,12},{1,13},{2,14},{3,15},{4,8},{5,9},{6,10},{7,11},{8,4},{9,5},... | collective-permute-start | bytes 884744 | tf_op jit(solution)/shard_map/ppermute | solution.py:26
  58.6 42.7 %collective-permute-start.30 = (bf16[512,768]{1,0:T(8,128)(2,1)S(1)}, bf16[512,768]{1,0:T(8,128)(2,1)S(1)}, u32[]{:S(2)}, u32[]{:S(2)}) collective-permute-start(bf16[512,768]{1,0:T(8,128)(2,1)S(1)} %pad_maximum_fusion), channel_id=1, source_target_pairs={{0,16},{1,17},{2,18},{3,19},{4,20},{5,21},{6,22},{7,23},{8,24},{9,... | collective-permute-start | bytes 2359304 | tf_op jit(solution)/shard_map/ppermute | solution.py:26
  73.4 24.1 %collective-permute-start.32 = (bf16[384,384]{1,0:T(8,128)(2,1)S(1)}, bf16[384,384]{1,0:T(8,128)(2,1)S(1)}, u32[]{:S(2)}, u32[]{:S(2)}) collective-permute-start(bf16[384,384]{1,0:T(8,128)(2,1)S(1)} %get-tuple-element.83.refs_0_), channel_id=1, source_target_pairs={{0,8},{1,9},{2,10},{3,11},{4,12},{5,13},{6,14},{7,15},{8,0},{9,1},... | collective-permute-start | bytes 884744 | tf_op jit(solution)/shard_map/ppermute | solution.py:26
  82.7 16.5 %collective-permute-start.36 = (bf16[384,384]{1,0:T(8,128)(2,1)S(1)}, bf16[384,384]{1,0:T(8,128)(2,1)S(1)}, u32[]{:S(2)}, u32[]{:S(2)}) collective-permute-start(bf16[384,384]{1,0:T(8,128)(2,1)S(1)} %copy-done.75), channel_id=1, source_target_pairs={{0,12},{1,13},{2,14},{3,15},{4,8},{5,9},{6,10},{7,11},{8,4},{9,5},... | collective-permute-start | bytes 884744 | tf_op jit(solution)/shard_map/ppermute | solution.py:26
  97.7 21.3 %collective-permute-start.40 = (bf16[384,384]{1,0:T(8,128)(2,1)S(1)}, bf16[384,384]{1,0:T(8,128)(2,1)S(1)}, u32[]{:S(2)}, u32[]{:S(2)}) collective-permute-start(bf16[384,384]{1,0:T(8,128)(2,1)S(1)} %get-tuple-element.90.refs_8_), channel_id=1, source_target_pairs={{0,8},{1,9},{2,10},{3,11},{4,12},{5,13},{6,14},{7,15},{8,0},{9,1},... | collective-permute-start | bytes 884744 | tf_op jit(solution)/shard_map/ppermute | solution.py:26
  101.3 30.1 %collective-permute-start.9 = (bf16[128,1536]{1,0:T(8,128)(2,1)S(1)}, bf16[128,1536]{1,0:T(8,128)(2,1)S(1)}, u32[]{:S(2)}, u32[]{:S(2)}) collective-permute-start(bf16[128,1536]{1,0:T(8,128)(2,1)S(1)} %dynamic-slice_bitcast_fusion.6.refs_0_), channel_id=1, source_target_pairs={{0,1},{1,0},{2,3},{3,2},{4,5},{5,4},{6,7},{7,6},{8,9},{9,8},{10,11... | collective-permute-start | bytes 1179656 | tf_op jit(solution)/shard_map/ppermute | solution.py:26
  108.6 22.9 %collective-permute-start.11 = (bf16[128,1536]{1,0:T(8,128)(2,1)S(1)}, bf16[128,1536]{1,0:T(8,128)(2,1)S(1)}, u32[]{:S(2)}, u32[]{:S(2)}) collective-permute-start(bf16[128,1536]{1,0:T(8,128)(2,1)S(1)} %dynamic-slice_bitcast_fusion.6.refs_0_), channel_id=1, source_target_pairs={{0,4},{1,5},{2,6},{3,7},{4,0},{5,1},{6,2},{7,3},{8,12},{9,13},{10,... | collective-permute-start | bytes 1179656 | tf_op jit(solution)/shard_map/ppermute | solution.py:26
  139.0 31.5 %collective-permute-start.46 = (bf16[384,384]{1,0:T(8,128)(2,1)S(1)}, bf16[384,384]{1,0:T(8,128)(2,1)S(1)}, u32[]{:S(2)}, u32[]{:S(2)}) collective-permute-start(bf16[384,384]{1,0:T(8,128)(2,1)S(1)} %copy-done.7), channel_id=1, source_target_pairs={{0,8},{1,9},{2,10},{3,11},{4,12},{5,13},{6,14},{7,15},{8,0},{9,1},... | collective-permute-start | bytes 884744 | tf_op jit(solution)/shard_map/ppermute | solution.py:26
  143.1 27.5 %collective-permute-start.47 = (bf16[384,384]{1,0:T(8,128)(2,1)S(1)}, bf16[384,384]{1,0:T(8,128)(2,1)S(1)}, u32[]{:S(2)}, u32[]{:S(2)}) collective-permute-start(bf16[384,384]{1,0:T(8,128)(2,1)S(1)} %copy-done.38), channel_id=1, source_target_pairs={{0,12},{1,13},{2,14},{3,15},{4,8},{5,9},{6,10},{7,11},{8,4},{9,5},... | collective-permute-start | bytes 884744 | tf_op jit(solution)/shard_map/ppermute | solution.py:26
  177.2 22.8 %collective-permute-start.51 = (bf16[128,1536]{1,0:T(8,128)(2,1)S(1)}, bf16[128,1536]{1,0:T(8,128)(2,1)S(1)}, u32[]{:S(2)}, u32[]{:S(2)}) collective-permute-start(bf16[128,1536]{1,0:T(8,128)(2,1)S(1)} %get-tuple-element.160), channel_id=1, source_target_pairs={{0,1},{1,0},{2,3},{3,2},{4,5},{5,4},{6,7},{7,6},{8,9},{9,8},{10,11... | collective-permute-start | bytes 1179656 | tf_op jit(solution)/shard_map/ppermute | solution.py:26
  198.1 26.2 %collective-permute-start.50 = (bf16[128,1536]{1,0:T(8,128)(2,1)}, bf16[128,1536]{1,0:T(8,128)(2,1)}, u32[]{:S(2)}, u32[]{:S(2)}) collective-permute-start(bf16[128,1536]{1,0:T(8,128)(2,1)} %get-tuple-element.102), channel_id=1, source_target_pairs={{0,1},{1,0},{2,3},{3,2},{4,5},{5,4},{6,7},{7,6},{8,9},{9,8},{10,11... | collective-permute-start | bytes 1179656 | tf_op jit(solution)/shard_map/ppermute | solution.py:26
  200.8 23.8 %collective-permute-start.52 = (bf16[128,1536]{1,0:T(8,128)(2,1)}, bf16[128,1536]{1,0:T(8,128)(2,1)}, u32[]{:S(2)}, u32[]{:S(2)}) collective-permute-start(bf16[128,1536]{1,0:T(8,128)(2,1)} %fusion.8), channel_id=1, source_target_pairs={{0,4},{1,5},{2,6},{3,7},{4,0},{5,1},{6,2},{7,3},{8,12},{9,13},{10,... | collective-permute-start | bytes 1179656 | tf_op jit(solution)/shard_map/ppermute | solution.py:26
  200.8 18.4 %collective-permute-start.56 = (bf16[384,384]{1,0:T(8,128)(2,1)}, bf16[384,384]{1,0:T(8,128)(2,1)}, u32[]{:S(2)}, u32[]{:S(2)}) collective-permute-start(bf16[384,384]{1,0:T(8,128)(2,1)} %get-tuple-element.107), channel_id=1, source_target_pairs={{0,12},{1,13},{2,14},{3,15},{4,8},{5,9},{6,10},{7,11},{8,4},{9,5},... | collective-permute-start | bytes 884744 | tf_op jit(solution)/shard_map/ppermute | solution.py:26
  219.1 23.5 %collective-permute-start.72 = (bf16[384,384]{1,0:T(8,128)(2,1)S(1)}, bf16[384,384]{1,0:T(8,128)(2,1)S(1)}, u32[]{:S(2)}, u32[]{:S(2)}) collective-permute-start(bf16[384,384]{1,0:T(8,128)(2,1)S(1)} %copy-done.8), channel_id=1, source_target_pairs={{0,8},{1,9},{2,10},{3,11},{4,12},{5,13},{6,14},{7,15},{8,0},{9,1},... | collective-permute-start | bytes 884744 | tf_op jit(solution)/shard_map/ppermute | solution.py:26
  220.6 23.7 %collective-permute-start.75 = (bf16[384,384]{1,0:T(8,128)(2,1)}, bf16[384,384]{1,0:T(8,128)(2,1)S(1)}, u32[]{:S(2)}, u32[]{:S(2)}) collective-permute-start(bf16[384,384]{1,0:T(8,128)(2,1)} %get-tuple-element.121), channel_id=1, source_target_pairs={{0,12},{1,13},{2,14},{3,15},{4,8},{5,9},{6,10},{7,11},{8,4},{9,5},... | collective-permute-start | bytes 884744 | tf_op jit(solution)/shard_map/ppermute | solution.py:26
  224.6 18.1 %collective-permute-start.73 = (bf16[384,384]{1,0:T(8,128)(2,1)}, bf16[384,384]{1,0:T(8,128)(2,1)S(1)}, u32[]{:S(2)}, u32[]{:S(2)}) collective-permute-start(bf16[384,384]{1,0:T(8,128)(2,1)} %get-tuple-element.125.refs_8_), channel_id=1, source_target_pairs={{0,2},{1,3},{2,0},{3,1},{4,6},{5,7},{6,4},{7,5},{8,10},{9,11},{10,... | collective-permute-start | bytes 884744 | tf_op jit(solution)/shard_map/ppermute | solution.py:26
  233.1 16.9 %collective-permute-start.57 = (bf16[128,1536]{1,0:T(8,128)(2,1)S(1)}, bf16[128,1536]{1,0:T(8,128)(2,1)S(1)}, u32[]{:S(2)}, u32[]{:S(2)}) collective-permute-start(bf16[128,1536]{1,0:T(8,128)(2,1)S(1)} %fusion.14.refs_0_), channel_id=1, source_target_pairs={{0,4},{1,5},{2,6},{3,7},{4,0},{5,1},{6,2},{7,3},{8,12},{9,13},{10,... | collective-permute-start | bytes 1179656 | tf_op jit(solution)/shard_map/ppermute | solution.py:26
  242.7 25.3 %collective-permute-start.79 = (bf16[384,384]{1,0:T(8,128)(2,1)S(1)}, bf16[384,384]{1,0:T(8,128)(2,1)S(1)}, u32[]{:S(2)}, u32[]{:S(2)}) collective-permute-start(bf16[384,384]{1,0:T(8,128)(2,1)S(1)} %copy-done.9), channel_id=1, source_target_pairs={{0,8},{1,9},{2,10},{3,11},{4,12},{5,13},{6,14},{7,15},{8,0},{9,1},... | collective-permute-start | bytes 884744 | tf_op jit(solution)/shard_map/ppermute | solution.py:26
  242.7 25.2 %collective-permute-start.81 = (bf16[384,384]{1,0:T(8,128)(2,1)S(1)}, bf16[384,384]{1,0:T(8,128)(2,1)S(1)}, u32[]{:S(2)}, u32[]{:S(2)}) collective-permute-start(bf16[384,384]{1,0:T(8,128)(2,1)S(1)} %copy-done.36), channel_id=1, source_target_pairs={{0,12},{1,13},{2,14},{3,15},{4,8},{5,9},{6,10},{7,11},{8,4},{9,5},... | collective-permute-start | bytes 884744 | tf_op jit(solution)/shard_map/ppermute | solution.py:26
  244.3 28.8 %collective-permute-start.74 = (bf16[384,384]{1,0:T(8,128)(2,1)S(1)}, bf16[384,384]{1,0:T(8,128)(2,1)S(1)}, u32[]{:S(2)}, u32[]{:S(2)}) collective-permute-start(bf16[384,384]{1,0:T(8,128)(2,1)S(1)} %collective-permute-done.72.refs_4_), channel_id=1, source_target_pairs={{0,2},{1,3},{2,0},{3,1},{4,6},{5,7},{6,4},{7,5},{8,10},{9,11},{10,... | collective-permute-start | bytes 884744 | tf_op jit(solution)/shard_map/ppermute | solution.py:26
  247.1 27.6 %collective-permute-start.54 = (bf16[128,1536]{1,0:T(8,128)(2,1)S(1)}, bf16[128,1536]{1,0:T(8,128)(2,1)S(1)}, u32[]{:S(2)}, u32[]{:S(2)}) collective-permute-start(bf16[128,1536]{1,0:T(8,128)(2,1)S(1)} %fusion.14.refs_0_), channel_id=1, source_target_pairs={{0,1},{1,0},{2,3},{3,2},{4,5},{5,4},{6,7},{7,6},{8,9},{9,8},{10,11... | collective-permute-start | bytes 1179656 | tf_op jit(solution)/shard_map/ppermute | solution.py:26
  250.0 25.2 %collective-permute-start.59 = (bf16[128,1536]{1,0:T(8,128)(2,1)S(1)}, bf16[128,1536]{1,0:T(8,128)(2,1)S(1)}, u32[]{:S(2)}, u32[]{:S(2)}) collective-permute-start(bf16[128,1536]{1,0:T(8,128)(2,1)S(1)} %collective-permute-done.57.refs_4_), channel_id=1, source_target_pairs={{0,1},{1,0},{2,3},{3,2},{4,5},{5,4},{6,7},{7,6},{8,9},{9,8},{10,11... | collective-permute-start | bytes 1179656 | tf_op jit(solution)/shard_map/ppermute | solution.py:26
  280.6 24.9 %collective-permute-start.80 = (bf16[384,384]{1,0:T(8,128)(2,1)S(1)}, bf16[384,384]{1,0:T(8,128)(2,1)S(1)}, u32[]{:S(2)}, u32[]{:S(2)}) collective-permute-start(bf16[384,384]{1,0:T(8,128)(2,1)S(1)} %collective-permute-done.79.refs_12_), channel_id=1, source_target_pairs={{0,2},{1,3},{2,0},{3,1},{4,6},{5,7},{6,4},{7,5},{8,10},{9,11},{10,... | collective-permute-start | bytes 884744 | tf_op jit(solution)/shard_map/ppermute | solution.py:26
  280.6 24.9 %collective-permute-start.82 = (bf16[384,384]{1,0:T(8,128)(2,1)S(1)}, bf16[384,384]{1,0:T(8,128)(2,1)S(1)}, u32[]{:S(2)}, u32[]{:S(2)}) collective-permute-start(bf16[384,384]{1,0:T(8,128)(2,1)S(1)} %collective-permute-done.81.refs_14_), channel_id=1, source_target_pairs={{0,2},{1,3},{2,0},{3,1},{4,6},{5,7},{6,4},{7,5},{8,10},{9,11},{10,... | collective-permute-start | bytes 884744 | tf_op jit(solution)/shard_map/ppermute | solution.py:26
  324.5 17.9 %collective-permute-start.85 = (bf16[128,1536]{1,0:T(8,128)(2,1)S(1)}, bf16[128,1536]{1,0:T(8,128)(2,1)S(1)}, u32[]{:S(2)}, u32[]{:S(2)}) collective-permute-start(bf16[128,1536]{1,0:T(8,128)(2,1)S(1)} %get-tuple-element.158), channel_id=1, source_target_pairs={{0,4},{1,5},{2,6},{3,7},{4,0},{5,1},{6,2},{7,3},{8,12},{9,13},{10,... | collective-permute-start | bytes 1179656 | tf_op jit(solution)/shard_map/ppermute | solution.py:26
  324.8 18.1 %collective-permute-start.84 = (bf16[128,1536]{1,0:T(8,128)(2,1)S(1)}, bf16[128,1536]{1,0:T(8,128)(2,1)S(1)}, u32[]{:S(2)}, u32[]{:S(2)}) collective-permute-start(bf16[128,1536]{1,0:T(8,128)(2,1)S(1)} %get-tuple-element.156), channel_id=1, source_target_pairs={{0,1},{1,0},{2,3},{3,2},{4,5},{5,4},{6,7},{7,6},{8,9},{9,8},{10,11... | collective-permute-start | bytes 1179656 | tf_op jit(solution)/shard_map/ppermute | solution.py:26
  (145 other events, 2326.1 us)
where the time goes:
time: 351 us; the launch traced here: 346 us
  waiting for transfers between devices  146 us (42%)
  starting transfers between devices  106 us (30%)
  Pallas kernels  58.6 us (17%)
  other arithmetic  19.1 us (5%)
  local copies, waits for them, and re-layouts  13.8 us (4%)
    ppermute x88, waiting for transfers between devices, send_to(): return lax.ppermute(array, AXES, pairs)  146 us
    ppermute x88, starting transfers between devices, send_to(): return lax.ppermute(array, AXES, pairs)  106 us
    pallas_call x2, Pallas kernels, scores(): pl.pallas_call(functools.partial(scores_kernel, plan), out_shape=(jax.Sha...  34.5 us
    pallas_call x2, Pallas kernels, mix(): pl.pallas_call(functools.partial(mix_kernel, plan), out_shape=(shape, sha...  20.3 us
    select_n x5, other arithmetic, block_of(): block = jnp.where(s == layer, cut(kind, s * wide + at, bw), other)  8.92 us
  transfers between devices with their start and end apart: 88, of which 30 were waited for; matrix products, arithmetic and copies ran while one was open for 6% of the time, Pallas kernels for 14%

commit v1 on v0

--- a/solution.py
+++ b/solution.py
@@ -77,37 +77,28 @@
     return key_at < limit, key_at < ends_ref[slot, NP - 1]
 
 
-def scores_kernel(plan, ends_ref, mod_ref, *refs):
-    slots, slot_len, cols, n_x, n_w, kr, bw, wc = plan
-    x_refs, refs = refs[:n_x], refs[n_x:]
-    w_refs, refs = (refs[:n_w], refs[n_w : 2 * n_w]), refs[2 * n_w :]
-    kv_refs, refs = refs[:slots], refs[slots:]
-    xm, weights_ref, xv, wv, kvv, x_sem, w_sem, kv_sem = refs
+def load_x(plan, x_refs, xv, sem):
+    slots, slot_len, cols = plan
     s, c = lax.axis_index("section"), lax.axis_index("col")
     half = slot_len // 2
-    x_copies, w_copies, kv_copies = [], [], []
+    copies = []
     for slot in range(slots):
         for dc in range(cols):
             for h in range(2):
-                place = len(x_copies)
+                place = len(copies)
                 col = lax.rem(c + cols - dc, cols)
-                row = slot * slot_len + jnp.where(s == h, 0, half)
-                row = pl.multiple_of(row, half)
-                x_copies.append(
+                row = pl.multiple_of(slot * slot_len + jnp.where(s == h, 0, half), half)
+                copies.append(
                     pltpu.make_async_copy(
-                        x_refs[place], xv.at[col, pl.ds(row, half), :], x_sem.at[place]
+                        x_refs[place], xv.at[col, pl.ds(row, half), :], sem.at[place]
                     )
                 )
-                x_copies[-1].start()
-    for t in range(2):
-        w_copies.append(load_rows(w_refs[t], wv.at[t], w_sem, t * n_w, kr))
-    for slot in range(slots):
-        kv_copies.append(
-            pltpu.make_async_copy(kv_refs[slot].at[0], kvv.at[slot], kv_sem.at[slot])
-        )
-        kv_copies[-1].start()
-    for copy in x_copies:
-        copy.wait()
+                copies[-1].start()
+    return copies
+
+
+def modulate(plan, wc, mod_ref, xv, xm):
+    slots, slot_len, cols = plan
     feat = cols * wc
     for slot in range(slots):
         rows = pl.ds(slot * slot_len, slot_len)
@@ -119,21 +110,45 @@
             squares += jnp.sum(part * part, axis=-1, keepdims=True)
         mean = total / feat
         var = squares / feat - mean * mean
-        inverse = 1.0 / jnp.sqrt(var + 1e-06)
+        inverse = lax.rsqrt(var + 1e-06)
         for col in range(cols):
             span = pl.ds(col * wc, wc)
             part = xv[col, rows, :].astype(jnp.float32)
             shift = mod_ref[slot, 0:1, span]
             scale = mod_ref[slot, 1:2, span]
             xm[rows, span] = ((part - mean) * inverse * (1.0 + scale) + shift).astype(jnp.bfloat16)
-    for copy in w_copies[0] + w_copies[1] + kv_copies:
+
+
+def modulate_kernel(plan, wc, mod_ref, *refs):
+    n_x = len(refs) - 3
+    x_refs, (xm, xv, sem) = refs[:n_x], refs[n_x:]
+    for copy in load_x(plan, x_refs, xv, sem):
+        copy.wait()
+    modulate(plan, wc, mod_ref, xv, xm)
+
+
+def scores_kernel(plan, ends_ref, *refs):
+    slots, slot_len, n_w, kr, bw = plan
+    x_ref, refs = refs[0], refs[1:]
+    w_refs, refs = (refs[:n_w], refs[n_w : 2 * n_w]), refs[2 * n_w :]
+    kv_refs, refs = refs[:slots], refs[slots:]
+    weights_ref, xm, wv, kvv, x_sem, w_sem, kv_sem = refs
+    x_copies = [pltpu.make_async_copy(x_ref, xm, x_sem.at[0])]
+    x_copies[0].start()
+    copies = load_rows(w_refs[0], wv.at[0], w_sem, 0, kr)
+    copies += load_rows(w_refs[1], wv.at[1], w_sem, n_w, kr)
+    for slot in range(slots):
+        one = kv_refs[slot].at[0]
+        target = kvv.at[slot, pl.ds(slot_len, slot_len), :]
+        copies.append(pltpu.make_async_copy(one, target, kv_sem.at[slot]))
+        copies[-1].start()
+    for copy in x_copies + copies:
         copy.wait()
     contract = (((1,), (1,)), ((), ()))
 
     def normed(block):
-        return (
-            block / jnp.sqrt(jnp.mean(block * block, axis=-1, keepdims=True) + 1e-06)
-        ).astype(jnp.bfloat16)
+        mean = jnp.mean(block * block, axis=-1, keepdims=True)
+        return (block * lax.rsqrt(mean + 1e-06)).astype(jnp.bfloat16)
 
     for slot in range(slots):
         rows = pl.ds(slot * slot_len, slot_len)
@@ -141,67 +156,70 @@
         fresh, valid = fresh_and_valid(ends_ref, slot, slot_len)
         for head in range(bw // HD):
             lanes = slice(head * HD, (head + 1) * HD)
-            query, key = normed(raw[0][:, lanes]), normed(raw[1][:, lanes])
-            new_scores = lax.dot_general(query, key, contract, preferred_element_type=jnp.float32)
-            old_scores = lax.dot_general(
+            query = normed(raw[0][:, lanes])
+            kvv[slot, 0:slot_len, lanes] = normed(raw[1][:, lanes])
+            both = lax.dot_general(
                 query, kvv[slot, :, lanes], contract, preferred_element_type=jnp.float32
             )
-            scores = jnp.where(fresh, new_scores, old_scores) * (1.0 / math.sqrt(HD))
-            weights = jnp.where(valid, jnp.exp(scores), 0.0)
-            weights = weights / jnp.sum(weights, axis=-1, keepdims=True)
-            weights_ref[slot, head] = weights.astype(jnp.bfloat16)
-
-
-def mix_kernel(plan, ends_ref, xm_ref, weights_ref, *refs):
+            scores = jnp.where(fresh, both[:, :slot_len], both[:, slot_len:])
+            weights = jnp.where(valid, jnp.exp(scores * (1.0 / math.sqrt(HD))), 0.0)
+            weights = weights * (1.0 / jnp.sum(weights, axis=-1, keepdims=True))
+            weights_ref[slot, head, :, 0:slot_len] = jnp.where(fresh, weights, 0.0).astype(
+                jnp.bfloat16
+            )
+            weights_ref[slot, head, :, slot_len:] = jnp.where(fresh, 0.0, weights).astype(
+                jnp.bfloat16
+            )
+
+
+def mix_kernel(plan, x_ref, weights_ref, *refs):
     slots, slot_len, cols, n_w, kr, nr, bw, wc = plan
     v_refs, o_refs, refs = refs[:n_w], refs[n_w : 2 * n_w], refs[2 * n_w :]
     kv_refs, refs = refs[:slots], refs[slots:]
-    keep_ref, pass_ref, wv, ov, kvv, att, w_sem, kv_sem = refs
-    s, i, c = (lax.axis_index(axis) for axis in AXES)
+    keep_ref, pass_ref, xm, pv, wv, ov, kvv, att, x_sem, w_sem, kv_sem = refs
+    s, c = lax.axis_index("section"), lax.axis_index("col")
     half = slot_len // 2
+    x_copy = pltpu.make_async_copy(x_ref, xm, x_sem.at[0])
+    x_copy.start()
     copies = load_rows(v_refs, wv, w_sem, 0, kr)
-    for slot in range(slots):
-        copies.append(
-            pltpu.make_async_copy(kv_refs[slot].at[1], kvv.at[slot], kv_sem.at[slot])
-        )
-        copies[-1].start()
+    p_copy = pltpu.make_async_copy(weights_ref, pv, x_sem.at[1])
+    p_copy.start()
+    late = [p_copy]
+    for slot in range(slots):
+        one = kv_refs[slot].at[1]
+        target = kvv.at[slot, pl.ds(slot_len, slot_len), :]
+        late.append(pltpu.make_async_copy(one, target, kv_sem.at[slot]))
+        late[-1].start()
     o_copies = load_rows(o_refs, ov, w_sem, n_w, None)
-    for copy in copies:
+    for copy in [x_copy] + copies:
         copy.wait()
     for slot in range(slots):
         rows = pl.ds(slot * slot_len, slot_len)
-        raw = jnp.dot(xm_ref[rows, :], wv[...], preferred_element_type=jnp.float32)
-        value = raw.astype(jnp.bfloat16)
-        fresh, _ = fresh_and_valid(ends_ref, slot, slot_len)
+        raw = jnp.dot(xm[rows, :], wv[...], preferred_element_type=jnp.float32)
+        kvv[slot, 0:slot_len, :] = raw.astype(jnp.bfloat16)
+    for copy in late:
+        copy.wait()
+    for slot in range(slots):
+        rows = pl.ds(slot * slot_len, slot_len)
         for head in range(bw // HD):
             lanes = slice(head * HD, (head + 1) * HD)
-            weights = weights_ref[slot, head]
-            none = jnp.zeros_like(weights)
-            mixed = jnp.dot(
-                jnp.where(fresh, weights, none),
-                value[:, lanes],
-                preferred_element_type=jnp.float32,
-            ) + jnp.dot(
-                jnp.where(fresh, none, weights),
-                kvv[slot, :, lanes],
-                preferred_element_type=jnp.float32,
-            )
+            mixed = jnp.dot(pv[slot, head], kvv[slot, :, lanes], preferred_element_type=jnp.float32)
             att[rows, lanes] = mixed.astype(jnp.bfloat16)
     for copy in o_copies:
         copy.wait()
-    blocks = []
-    for side in (s, 1 - s):
+    for side, out_ref in ((1 - s, pass_ref), (s, keep_ref)):
+        blocks = []
         for slot in range(slots):
             row = pl.multiple_of(slot * slot_len + side * half, half)
             blocks.append(att[pl.ds(row, half), :])
-    lhs = jnp.concatenate(blocks, axis=0)
-    for place in range(n_w):
-        row = lax.rem(c * (n_w // cols) + place, n_w)
-        part = jnp.dot(lhs, ov[row], preferred_element_type=jnp.float32).astype(jnp.bfloat16)
-        part = part.reshape(2, slots, half, nr)
-        lanes = slice(place * nr, (place + 1) * nr)
-        keep_ref[:, :, lanes] = part[0]
-        pass_ref[:, :, lanes] = part[1]
+        lhs = jnp.concatenate(blocks, axis=0)
+        for place in range(n_w):
+            row = lax.rem(c * (n_w // cols) + place, n_w)
+            part = jnp.dot(lhs, ov[row], preferred_element_type=jnp.float32).astype(jnp.bfloat16)
+            for slot in range(slots):
+                out_ref[slot, :, place * nr : (place + 1) * nr] = part[
+                    slot * half : (slot + 1) * half
+                ]
 
 
 def mod_kernel(slots, feats_ref, weight_ref, out_ref):
@@ -398,27 +416,42 @@
             if (di, dc) != (0, 0):
                 step(name)(bring)
             step(name + "c")(lambda name=name: swap(name + "c", get(name)))
+    x_rest = lax.dynamic_slice_in_dim(hidden_in[0], (1 - s) * half, half, 0)
+    step("x.0.0c")(lambda: x_rest)
 
     def x_pieces(kind):
         return [get(f"{kind}.{di}.{dc}" + end) for di, dc in places for end in ("", "c")]
 
-    def scores(layer):
+    def modulated(layer):
         pieces = x_pieces("xg"[layer])
-        plan = (slots, slot_len, cols, len(pieces), rows, kr, bw, wc)
+        shape = (slots * slot_len, feat)
         return pl.pallas_call(
-            functools.partial(scores_kernel, plan),
-            out_shape=(
-                jax.ShapeDtypeStruct((slots * slot_len, feat), jnp.bfloat16),
-                jax.ShapeDtypeStruct((slots, bw // HD, slot_len, slot_len), jnp.bfloat16),
-            ),
-            in_specs=[pl.BlockSpec(memory_space=pltpu.SMEM), vmem_spec()]
-            + [any_spec()] * (len(pieces) + 2 * rows + slots),
-            out_specs=(vmem_spec(), vmem_spec()),
+            functools.partial(modulate_kernel, (slots, slot_len, cols), wc),
+            out_shape=jax.ShapeDtypeStruct(shape, jnp.bfloat16),
+            in_specs=[vmem_spec()] + [any_spec()] * len(pieces),
+            out_specs=vmem_spec(),
             scratch_shapes=[
                 pltpu.VMEM((cols, slots * slot_len, wc), jnp.bfloat16),
+                pltpu.SemaphoreType.DMA((len(pieces),)),
+            ],
+            compiler_params=pltpu.CompilerParams(vmem_limit_bytes=VMEM_LIMIT),
+            name="modulate",
+        )(gated(get("m")[layer], f"l{layer}"), *pieces)
+
+    def scores(layer):
+        return pl.pallas_call(
+            functools.partial(scores_kernel, (slots, slot_len, rows, kr, bw)),
+            out_shape=jax.ShapeDtypeStruct(
+                (slots, bw // HD, slot_len, 2 * slot_len), jnp.bfloat16
+            ),
+            in_specs=[pl.BlockSpec(memory_space=pltpu.SMEM)]
+            + [any_spec()] * (1 + 2 * rows + slots),
+            out_specs=vmem_spec(),
+            scratch_shapes=[
+                pltpu.VMEM((slots * slot_len, feat), jnp.bfloat16),
                 pltpu.VMEM((2, feat, bw), jnp.bfloat16),
-                pltpu.VMEM((slots, slot_len, bw), jnp.bfloat16),
-                pltpu.SemaphoreType.DMA((len(pieces),)),
+                pltpu.VMEM((slots, 2 * slot_len, bw), jnp.bfloat16),
+                pltpu.SemaphoreType.DMA((1,)),
                 pltpu.SemaphoreType.DMA((2 * rows,)),
                 pltpu.SemaphoreType.DMA((slots,)),
             ],
@@ -426,8 +459,7 @@
             name="scores",
         )(
             gated(get("n")[:, :NP], f"k{layer}"),
-            get("m")[layer],
-            *pieces,
+            get(f"l{layer}"),
             *of_rows("Q", layer),
             *of_rows("K", layer),
             *stale_of(layer),
@@ -439,33 +471,36 @@
         return pl.pallas_call(
             functools.partial(mix_kernel, plan),
             out_shape=(shape, shape),
-            in_specs=[pl.BlockSpec(memory_space=pltpu.SMEM), vmem_spec(), vmem_spec()]
-            + [any_spec()] * (2 * rows + slots),
+            in_specs=[any_spec()] * (2 + 2 * rows + slots),
             out_specs=(vmem_spec(), vmem_spec()),
             scratch_shapes=[
+                pltpu.VMEM((slots * slot_len, feat), jnp.bfloat16),
+                pltpu.VMEM((slots, bw // HD, slot_len, 2 * slot_len), jnp.bfloat16),
                 pltpu.VMEM((feat, bw), jnp.bfloat16),
                 pltpu.VMEM((rows, bw, nr), jnp.bfloat16),
-                pltpu.VMEM((slots, slot_len, bw), jnp.bfloat16),
+                pltpu.VMEM((slots, 2 * slot_len, bw), jnp.bfloat16),
                 pltpu.VMEM((slots * slot_len, bw), jnp.bfloat16),
+                pltpu.SemaphoreType.DMA((2,)),
                 pltpu.SemaphoreType.DMA((2 * rows,)),
                 pltpu.SemaphoreType.DMA((slots,)),
             ],
             compiler_params=pltpu.CompilerParams(vmem_limit_bytes=VMEM_LIMIT),
             name="mix",
         )(
-            gated(get("n")[:, :NP], f"v{layer}"),
-            *get(f"k{layer}"),
+            get(f"l{layer}"),
+            gated(get(f"k{layer}"), f"v{layer}"),
             *of_rows("V", layer),
             *of_rows("O", layer),
             *stale_of(layer),
         )
 
     def parts(layer):
-        keep, passed = get(f"v{layer}")
-        total = keep.astype(jnp.float32) + get(f"p{layer}").astype(jnp.float32)
-        return {
-            (di, dc): total[offsets.index(di), :, dc * wc : (dc + 1) * wc] for di, dc in places
-        }
+        keep, other = get(f"v{layer}")[0], get(f"p{layer}")
+
+        def part(array, di, dc):
+            return array[offsets.index(di), :, dc * wc : (dc + 1) * wc].astype(jnp.float32)
+
+        return {place: part(keep, *place) + part(other, *place) for place in places}
 
     def summed(layer, di):
         part = get(f"t{layer}")[di, 0]
@@ -482,6 +517,7 @@
         return send(name, get(f"u{layer}.{di}").astype(jnp.bfloat16), di, 0)
 
     for layer in range(2):
+        step(f"l{layer}")(functools.partial(modulated, layer))
         step(f"k{layer}")(functools.partial(scores, layer))
         step(f"v{layer}")(functools.partial(mix, layer))
         step(f"p{layer}")(lambda layer=layer: swap(f"p{layer}", get(f"v{layer}")[1]))

time: 351 us -> 366 us (1.043)
  waiting for transfers between devices: 146 us -> 165 us
  starting transfers between devices: 106 us -> 95.9 us
  Pallas kernels: 58.6 us -> 64.2 us
    ppermute x88 -> x87, waiting for transfers between devices: 146 us -> 165 us  [send_to(): return lax.ppermute(array, AXES, pairs)]
    ppermute x88 -> x87, starting transfers between devices: 106 us -> 95.9 us  [send_to(): return lax.ppermute(array, AXES, pairs)]
    pallas_call x2 -> x4, Pallas kernels: 34.5 us -> 42.7 us  [the longest x2 29.1 us: scores(): pl.pallas_call(functools.partial(scores_kernel, (slots, slot_len, rows, k...]
    convert_element_type x0 -> x2, other arithmetic: none -> 3.74 us  [the longest x1 2.12 us: give(): return send(name, get(f't{layer}')[di, dc].astype(jnp.bfloat16), 0, dc)]
    unnamed x178 -> x170, local copies, waits for them, and re-layouts: 5.65 us -> 8.29 us
  transfers between devices with their start and end apart: 88 -> 87, of which waited for: 30 -> 37; matrix products, arithmetic and copies ran while one was open for 6% -> 5% of each run, Pallas kernels for 14% -> 15%
where the time goes in v1:
time: 366 us; the launch traced here: 362 us
  waiting for transfers between devices  165 us (45%)
  starting transfers between devices  95.9 us (26%)
  Pallas kernels  64.2 us (18%)
  other arithmetic  18.8 us (5%)
  local copies, waits for them, and re-layouts  15.5 us (4%)
    ppermute x87, waiting for transfers between devices, send_to(): return lax.ppermute(array, AXES, pairs)  165 us
    ppermute x87, starting transfers between devices, send_to(): return lax.ppermute(array, AXES, pairs)  95.9 us
    pallas_call x2, Pallas kernels, scores(): pl.pallas_call(functools.partial(scores_kernel, (slots, slot_len, rows, k...  29.1 us
    pallas_call x2, Pallas kernels, mix(): pl.pallas_call(functools.partial(mix_kernel, plan), out_shape=(shape, sha...  17.8 us
    pallas_call x2, Pallas kernels, modulated(): pl.pallas_call(functools.partial(modulate_kernel, (slots, slot_len, cols)...  13.6 us
    unnamed x170, local copies, waits for them, and re-layouts  8.29 us
    select_n x5, other arithmetic, block_of(): block = jnp.where(s == layer, cut(kind, s * wide + at, bw), other)  7.81 us
  transfers between devices with their start and end apart: 87, of which 37 were waited for; matrix products, arithmetic and copies ran while one was open for 5% of the time, Pallas kernels for 15%

profile of v1, /device:TPU:0, one launch (start us, length us, event | category | flops | bytes accessed | tf_op | source)
XLA Modules:
  0.0 361.6 jit_solution(12057578265053158530)
XLA Ops:
  23.2 5.3 %collective-permute-done.12.refs_11_ = bf16[384,384]{1,0:T(8,128)(2,1)S(1)} collective-permute-done((bf16[384,384]{1,0:T(8,128)(2,1)S(1)}, bf16[384,384]{1,0:T(8,128)(2,1)S(1)}, u32[]{:S(2)}, u32[]{:S(2)}) %collective-permute-start.12) | collective-permute-done | bytes 294944 | tf_op jit(solution)/shard_map/ppermute | solution.py:26
  32.7 10.3 %collective-permute-done.4.refs_5_ = bf16[384,384]{1,0:T(8,128)(2,1)S(1)} collective-permute-done((bf16[384,384]{1,0:T(8,128)(2,1)S(1)}, bf16[384,384]{1,0:T(8,128)(2,1)S(1)}, u32[]{:S(2)}, u32[]{:S(2)}) %collective-permute-start.4) | collective-permute-done | bytes 294944 | tf_op jit(solution)/shard_map/ppermute | solution.py:26
  47.2 3.5 collective-permute-start.21
  53.1 6.5 %collective-permute-done.26.refs_2_ = bf16[384,384]{1,0:T(8,128)(2,1)S(1)} collective-permute-done((bf16[384,384]{1,0:T(8,128)(2,1)S(1)}, bf16[384,384]{1,0:T(8,128)(2,1)S(1)}, u32[]{:S(2)}, u32[]{:S(2)}) %collective-permute-start.26) | collective-permute-done | bytes 294944 | tf_op jit(solution)/shard_map/ppermute | solution.py:26
  63.8 7.3 %collective-permute-done.21.refs_13_ = bf16[384,384]{1,0:T(8,128)(2,1)} collective-permute-done((bf16[384,384]{1,0:T(8,128)(2,1)S(1)}, bf16[384,384]{1,0:T(8,128)(2,1)}, u32[]{:S(2)}, u32[]{:S(2)}) %collective-permute-start.21) | collective-permute-done | bytes 294944 | tf_op jit(solution)/shard_map/ppermute | solution.py:26
  74.0 5.8 %collective-permute-start.31 = (bf16[384,384]{1,0:T(8,128)(2,1)S(1)}, bf16[384,384]{1,0:T(8,128)(2,1)S(1)}, u32[]{:S(2)}, u32[]{:S(2)}) collective-permute-start(bf16[384,384]{1,0:T(8,128)(2,1)S(1)} %get-tuple-element.77.refs_0_), channel_id=1, source_target_pairs={{0,8},{1,9},{2,10},{3,11},{4,12},{5,13},{6,14},{7,15},{8,0},{9,1},... | collective-permute-start | bytes 884744 | tf_op jit(solution)/shard_map/ppermute | solution.py:26
  85.6 3.6 collective-permute-start.7
  89.3 10.5 %collective-permute-done.31.refs_4_ = bf16[384,384]{1,0:T(8,128)(2,1)S(1)} collective-permute-done((bf16[384,384]{1,0:T(8,128)(2,1)S(1)}, bf16[384,384]{1,0:T(8,128)(2,1)S(1)}, u32[]{:S(2)}, u32[]{:S(2)}) %collective-permute-start.31) | collective-permute-done | bytes 294944 | tf_op jit(solution)/shard_map/ppermute | solution.py:26
  100.6 4.7 %collective-permute-start.1 = (s32[5]{0:T(128)S(1)}, s32[5]{0:T(128)S(1)}, u32[]{:S(2)}, u32[]{:S(2)}) collective-permute-start(s32[5]{0:T(128)S(1)} %pad_add_fusion.1), channel_id=1, source_target_pairs={{0,4},{1,5},{2,6},{3,7},{4,0},{5,1},{6,2},{7,3},{8,12},{9,13},{10,... | collective-permute-start | bytes 68 | tf_op jit(solution)/shard_map/ppermute | solution.py:26
  106.3 5.4 %collective-permute-done.1 = s32[5]{0:T(128)S(1)} collective-permute-done((s32[5]{0:T(128)S(1)}, s32[5]{0:T(128)S(1)}, u32[]{:S(2)}, u32[]{:S(2)}) %collective-permute-start.1) | collective-permute-done | bytes 52 | tf_op jit(solution)/shard_map/ppermute | solution.py:26
  115.1 4.1 %collective-permute-done.38.refs_7_ = bf16[384,384]{1,0:T(8,128)(2,1)S(1)} collective-permute-done((bf16[384,384]{1,0:T(8,128)(2,1)S(1)}, bf16[384,384]{1,0:T(8,128)(2,1)S(1)}, u32[]{:S(2)}, u32[]{:S(2)}) %collective-permute-start.38) | collective-permute-done | bytes 294944 | tf_op jit(solution)/shard_map/ppermute | solution.py:26
  124.9 5.7 %collective-permute-done.9.refs_6_ = bf16[128,1536]{1,0:T(8,128)(2,1)S(1)} collective-permute-done((bf16[128,1536]{1,0:T(8,128)(2,1)S(1)}, bf16[128,1536]{1,0:T(8,128)(2,1)S(1)}, u32[]{:S(2)}, u32[]{:S(2)}) %collective-permute-start.9) | collective-permute-done | bytes 393248 | tf_op jit(solution)/shard_map/ppermute | solution.py:26
  130.6 4.2 %collective-permute-done.39.refs_12_ = bf16[384,384]{1,0:T(8,128)(2,1)S(1)} collective-permute-done((bf16[384,384]{1,0:T(8,128)(2,1)S(1)}, bf16[384,384]{1,0:T(8,128)(2,1)S(1)}, u32[]{:S(2)}, u32[]{:S(2)}) %collective-permute-start.39) | collective-permute-done | bytes 294944 | tf_op jit(solution)/shard_map/ppermute | solution.py:26
  137.6 3.7 %modulation.1 = f32[2,3,3072]{2,1,0:T(4,128)} custom-call(bf16[8,256]{1,0:T(8,128)(2,1)} %fusion.21.feats_ref, bf16[3,256,3072]{2,1,0:T(8,128)(2,1)} %bitcast.107), custom_call_target="tpu_custom_call" | custom-call | tf_op jit(solution)/shard_map/modulation/pallas_call | solution.py:393
  157.3 6.7 %modulate.2.refs_0_.x_ref = bf16[512,3072]{1,0:T(8,128)(2,1)} custom-call(f32[2,3,3072]{2,1,0:T(4,128)} %get-tuple-element.162.mod_ref, bf16[128,1536]{1,0:T(8,128)(2,1)} %copy-done.2, bf16[128,1536]{1,0:T(8,128)(2,1)} %get-tuple-element.159.refs_1_, bf16[128,1536]{1,0:T(8,128)(2,1)} %copy-done.21, bf16[128,1536]{1,0:T(8,128)(2,1)} %copy-done.26, ...), custom_call_target="tpu_custom_call" | custom-call | tf_op jit(solution)/shard_map/modulate/pallas_call | solution.py:428
  167.4 18.9 %scores.2.weights_ref = bf16[2,3,256,512]{3,2,1,0:T(8,128)(2,1)} custom-call(s32[2,4]{1,0:T(2,128)} %bitcast.115, bf16[512,3072]{1,0:T(8,128)(2,1)} %modulate.2.refs_0_.x_ref, bf16[384,384]{1,0:T(8,128)(2,1)} %copy-done.15, bf16[384,384]{1,0:T(8,128)(2,1)} %copy-done.67, bf16[384,384]{1,0:T(8,128)(2,1)} %copy-done.66, bf16[384,384]{1,0:T(8,128)(2,1)} %copy-done.70, ...), custom_call_target="tpu_custom_call" | custom-call | tf_op jit(solution)/shard_map/scores/pallas_call | solution.py:442
  187.8 8.9 %mix.2 = (bf16[2,128,3072]{2,1,0:T(8,128)(2,1)}, bf16[2,128,3072]{2,1,0:T(8,128)(2,1)}) custom-call(bf16[512,3072]{1,0:T(8,128)(2,1)} %modulate.2.refs_0_.x_ref, bf16[2,3,256,512]{3,2,1,0:T(8,128)(2,1)} %scores.2.weights_ref, bf16[384,384]{1,0:T(8,128)(2,1)} %copy-done.11, bf16[384,384]{1,0:T(8,128)(2,1)} %copy-done.38, bf16[384,384]{1,0:T(8,128)(2,1)} %copy-done.37, ...), custom_call_target="tpu_custom_call" | custom-call | tf_op jit(solution)/shard_map/mix/pallas_call | solution.py:471
  211.1 5.3 %collective-permute-done.63.refs_12_ = bf16[384,384]{1,0:T(8,128)(2,1)S(1)} collective-permute-done((bf16[384,384]{1,0:T(8,128)(2,1)S(1)}, bf16[384,384]{1,0:T(8,128)(2,1)S(1)}, u32[]{:S(2)}, u32[]{:S(2)}) %collective-permute-start.63) | collective-permute-done | bytes 294944 | tf_op jit(solution)/shard_map/ppermute | solution.py:26
  217.4 5.4 %collective-permute-done.61.refs_6_ = bf16[384,384]{1,0:T(8,128)(2,1)S(1)} collective-permute-done((bf16[384,384]{1,0:T(8,128)(2,1)S(1)}, bf16[384,384]{1,0:T(8,128)(2,1)S(1)}, u32[]{:S(2)}, u32[]{:S(2)}) %collective-permute-start.61) | collective-permute-done | bytes 294944 | tf_op jit(solution)/shard_map/ppermute | solution.py:26
  230.0 5.4 %collective-permute-done.65.refs_1_ = bf16[384,384]{1,0:T(8,128)(2,1)S(1)} collective-permute-done((bf16[384,384]{1,0:T(8,128)(2,1)S(1)}, bf16[384,384]{1,0:T(8,128)(2,1)S(1)}, u32[]{:S(2)}, u32[]{:S(2)}) %collective-permute-start.65) | collective-permute-done | bytes 294944 | tf_op jit(solution)/shard_map/ppermute | solution.py:26
  239.2 4.9 %collective-permute-done.55.refs_15_ = bf16[384,384]{1,0:T(8,128)(2,1)} collective-permute-done((bf16[384,384]{1,0:T(8,128)(2,1)}, bf16[384,384]{1,0:T(8,128)(2,1)}, u32[]{:S(2)}, u32[]{:S(2)}) %collective-permute-start.55) | collective-permute-done | bytes 294944 | tf_op jit(solution)/shard_map/ppermute | solution.py:26
  252.3 5.1 %collective-permute-done.75.refs_10_ = bf16[384,384]{1,0:T(8,128)(2,1)S(1)} collective-permute-done((bf16[384,384]{1,0:T(8,128)(2,1)}, bf16[384,384]{1,0:T(8,128)(2,1)S(1)}, u32[]{:S(2)}, u32[]{:S(2)}) %collective-permute-start.75) | collective-permute-done | bytes 294944 | tf_op jit(solution)/shard_map/ppermute | solution.py:26
  260.6 7.3 %collective-permute-done.71.refs_4_ = bf16[384,384]{1,0:T(8,128)(2,1)S(1)} collective-permute-done((bf16[384,384]{1,0:T(8,128)(2,1)}, bf16[384,384]{1,0:T(8,128)(2,1)S(1)}, u32[]{:S(2)}, u32[]{:S(2)}) %collective-permute-start.71) | collective-permute-done | bytes 294944 | tf_op jit(solution)/shard_map/ppermute | solution.py:26
  268.7 4.4 %collective-permute-start.78 = (bf16[384,384]{1,0:T(8,128)(2,1)S(1)}, bf16[384,384]{1,0:T(8,128)(2,1)S(1)}, u32[]{:S(2)}, u32[]{:S(2)}) collective-permute-start(bf16[384,384]{1,0:T(8,128)(2,1)S(1)} %copy-done.10), channel_id=1, source_target_pairs={{0,8},{1,9},{2,10},{3,11},{4,12},{5,13},{6,14},{7,15},{8,0},{9,1},... | collective-permute-start | bytes 884744 | tf_op jit(solution)/shard_map/ppermute | solution.py:26
  277.1 16.0 %collective-permute-done.78.refs_12_ = bf16[384,384]{1,0:T(8,128)(2,1)S(1)} collective-permute-done((bf16[384,384]{1,0:T(8,128)(2,1)S(1)}, bf16[384,384]{1,0:T(8,128)(2,1)S(1)}, u32[]{:S(2)}, u32[]{:S(2)}) %collective-permute-start.78) | collective-permute-done | bytes 294944 | tf_op jit(solution)/shard_map/ppermute | solution.py:26
  294.7 5.1 %collective-permute-done.77.refs_7_ = bf16[384,384]{1,0:T(8,128)(2,1)S(1)} collective-permute-done((bf16[384,384]{1,0:T(8,128)(2,1)S(1)}, bf16[384,384]{1,0:T(8,128)(2,1)S(1)}, u32[]{:S(2)}, u32[]{:S(2)}) %collective-permute-start.77) | collective-permute-done | bytes 294944 | tf_op jit(solution)/shard_map/ppermute | solution.py:26
  302.9 6.9 %modulate.3.refs_0_.x_ref = bf16[512,3072]{1,0:T(8,128)(2,1)} custom-call(f32[2,3,3072]{2,1,0:T(4,128)} %get-tuple-element.161.mod_ref, bf16[128,1536]{1,0:T(8,128)(2,1)} %copy-done, bf16[128,1536]{1,0:T(8,128)(2,1)} %copy-done.6, bf16[128,1536]{1,0:T(8,128)(2,1)} %copy-done.25, bf16[128,1536]{1,0:T(8,128)(2,1)} %copy-done.29, bf16[128,1536]{1,0:T(8,128)(2,1)} %copy-done.23, ...), custom_call_target="tpu_custom_call" | custom-call | tf_op jit(solution)/shard_map/modulate/pallas_call | solution.py:428
  310.5 10.2 %scores.3.weights_ref = bf16[2,3,256,512]{3,2,1,0:T(8,128)(2,1)} custom-call(s32[2,4]{1,0:T(2,128)} %bitcast.116, bf16[512,3072]{1,0:T(8,128)(2,1)} %modulate.3.refs_0_.x_ref, bf16[384,384]{1,0:T(8,128)(2,1)} %get-tuple-element.92.refs_1_, bf16[384,384]{1,0:T(8,128)(2,1)} %copy-done.64, bf16[384,384]{1,0:T(8,128)(2,1)} %collective-permute-done.13.refs_3_, ...), custom_call_target="tpu_custom_call" | custom-call | tf_op jit(solution)/shard_map/scores/pallas_call | solution.py:442
  322.2 8.9 %mix.3 = (bf16[2,128,3072]{2,1,0:T(8,128)(2,1)}, bf16[2,128,3072]{2,1,0:T(8,128)(2,1)}) custom-call(bf16[512,3072]{1,0:T(8,128)(2,1)} %modulate.3.refs_0_.x_ref, bf16[2,3,256,512]{3,2,1,0:T(8,128)(2,1)} %scores.3.weights_ref, bf16[384,384]{1,0:T(8,128)(2,1)} %get-tuple-element.110.refs_0_, bf16[384,384]{1,0:T(8,128)(2,1)} %copy-done.42, ...), custom_call_target="tpu_custom_call" | custom-call | tf_op jit(solution)/shard_map/mix/pallas_call | solution.py:471
  331.2 3.6 collective-permute-done.82
  340.8 8.6 %collective-permute-done.85 = bf16[128,1536]{1,0:T(8,128)(2,1)S(1)} collective-permute-done((bf16[128,1536]{1,0:T(8,128)(2,1)S(1)}, bf16[128,1536]{1,0:T(8,128)(2,1)S(1)}, u32[]{:S(2)}, u32[]{:S(2)}) %collective-permute-start.85) | collective-permute-done | bytes 393248 | tf_op jit(solution)/shard_map/ppermute | solution.py:26
  349.4 6.9 %collective-permute-done.84 = bf16[128,1536]{1,0:T(8,128)(2,1)S(1)} collective-permute-done((bf16[128,1536]{1,0:T(8,128)(2,1)S(1)}, bf16[128,1536]{1,0:T(8,128)(2,1)S(1)}, u32[]{:S(2)}, u32[]{:S(2)}) %collective-permute-start.84) | collective-permute-done | bytes 393248 | tf_op jit(solution)/shard_map/ppermute | solution.py:26
  (354 shorter events, 140.7 us)
Async XLA Ops:
  12.1 31.7 %collective-permute-start.22 = (bf16[384,768]{1,0:T(8,128)(2,1)S(1)}, bf16[384,768]{1,0:T(8,128)(2,1)S(1)}, u32[]{:S(2)}, u32[]{:S(2)}) collective-permute-start(bf16[384,768]{1,0:T(8,128)(2,1)S(1)} %dynamic-slice_bitcast_fusion.1), channel_id=1, source_target_pairs={{0,16},{1,17},{2,18},{3,19},{4,20},{5,21},{6,22},{7,23},{8,24},{9,... | collective-permute-start | bytes 1769480 | tf_op jit(solution)/shard_map/ppermute | solution.py:26
  20.3 22.7 %collective-permute-start.4 = (bf16[384,384]{1,0:T(8,128)(2,1)S(1)}, bf16[384,384]{1,0:T(8,128)(2,1)S(1)}, u32[]{:S(2)}, u32[]{:S(2)}) collective-permute-start(bf16[384,384]{1,0:T(8,128)(2,1)S(1)} %get-tuple-element.146.refs_1_), channel_id=1, source_target_pairs={{0,8},{1,9},{2,10},{3,11},{4,12},{5,13},{6,14},{7,15},{8,0},{9,1},... | collective-permute-start | bytes 884744 | tf_op jit(solution)/shard_map/ppermute | solution.py:26
  22.9 20.1 %collective-permute-start.17 = (bf16[384,384]{1,0:T(8,128)(2,1)S(1)}, bf16[384,384]{1,0:T(8,128)(2,1)S(1)}, u32[]{:S(2)}, u32[]{:S(2)}) collective-permute-start(bf16[384,384]{1,0:T(8,128)(2,1)S(1)} %get-tuple-element.69.refs_9_), channel_id=1, source_target_pairs={{0,2},{1,3},{2,0},{3,1},{4,6},{5,7},{6,4},{7,5},{8,10},{9,11},{10,... | collective-permute-start | bytes 884744 | tf_op jit(solution)/shard_map/ppermute | solution.py:26
  43.0 19.7 %collective-permute-start.32 = (bf16[768,384]{1,0:T(8,128)(2,1)S(1)}, bf16[768,384]{1,0:T(8,128)(2,1)S(1)}, u32[]{:S(2)}, u32[]{:S(2)}) collective-permute-start(bf16[768,384]{1,0:T(8,128)(2,1)S(1)} %dynamic-slice_bitcast_fusion), channel_id=1, source_target_pairs={{0,16},{1,17},{2,18},{3,19},{4,20},{5,21},{6,22},{7,23},{8,24},{9,... | collective-permute-start | bytes 1769480 | tf_op jit(solution)/shard_map/ppermute | solution.py:26
  47.2 24.0 %collective-permute-start.21 = (bf16[384,384]{1,0:T(8,128)(2,1)S(1)}, bf16[384,384]{1,0:T(8,128)(2,1)}, u32[]{:S(2)}, u32[]{:S(2)}) collective-permute-start(bf16[384,384]{1,0:T(8,128)(2,1)S(1)} %get-tuple-element.69.refs_9_), channel_id=1, source_target_pairs={{0,8},{1,9},{2,10},{3,11},{4,12},{5,13},{6,14},{7,15},{8,0},{9,1},... | collective-permute-start | bytes 884744 | tf_op jit(solution)/shard_map/ppermute | solution.py:26
  74.0 25.8 %collective-permute-start.31 = (bf16[384,384]{1,0:T(8,128)(2,1)S(1)}, bf16[384,384]{1,0:T(8,128)(2,1)S(1)}, u32[]{:S(2)}, u32[]{:S(2)}) collective-permute-start(bf16[384,384]{1,0:T(8,128)(2,1)S(1)} %get-tuple-element.77.refs_0_), channel_id=1, source_target_pairs={{0,8},{1,9},{2,10},{3,11},{4,12},{5,13},{6,14},{7,15},{8,0},{9,1},... | collective-permute-start | bytes 884744 | tf_op jit(solution)/shard_map/ppermute | solution.py:26
  80.6 20.1 %collective-permute-start.35 = (bf16[384,384]{1,0:T(8,128)(2,1)S(1)}, bf16[384,384]{1,0:T(8,128)(2,1)S(1)}, u32[]{:S(2)}, u32[]{:S(2)}) collective-permute-start(bf16[384,384]{1,0:T(8,128)(2,1)S(1)} %copy-done.54), channel_id=1, source_target_pairs={{0,12},{1,13},{2,14},{3,15},{4,8},{5,9},{6,10},{7,11},{8,4},{9,5},... | collective-permute-start | bytes 884744 | tf_op jit(solution)/shard_map/ppermute | solution.py:26
  85.5 19.8 %collective-permute-start.37 = (bf16[384,384]{1,0:T(8,128)(2,1)}, bf16[384,384]{1,0:T(8,128)(2,1)S(1)}, u32[]{:S(2)}, u32[]{:S(2)}) collective-permute-start(bf16[384,384]{1,0:T(8,128)(2,1)} %collective-permute-done.36.refs_10_), channel_id=1, source_target_pairs={{0,2},{1,3},{2,0},{3,1},{4,6},{5,7},{6,4},{7,5},{8,10},{9,11},{10,... | collective-permute-start | bytes 884744 | tf_op jit(solution)/shard_map/ppermute | solution.py:26
  85.6 28.8 %collective-permute-start.7 = (bf16[128,1536]{1,0:T(8,128)(2,1)S(1)}, bf16[128,1536]{1,0:T(8,128)(2,1)S(1)}, u32[]{:S(2)}, u32[]{:S(2)}) collective-permute-start(bf16[128,1536]{1,0:T(8,128)(2,1)S(1)} %get-tuple-element.66.refs_0_), channel_id=1, source_target_pairs={{0,4},{1,5},{2,6},{3,7},{4,0},{5,1},{6,2},{7,3},{8,12},{9,13},{10,... | collective-permute-start | bytes 1179656 | tf_op jit(solution)/shard_map/ppermute | solution.py:26
  99.8 21.6 %collective-permute-start.29 = (bf16[512,768]{1,0:T(8,128)(2,1)S(1)}, bf16[512,768]{1,0:T(8,128)(2,1)S(1)}, u32[]{:S(2)}, u32[]{:S(2)}) collective-permute-start(bf16[512,768]{1,0:T(8,128)(2,1)S(1)} %pad_maximum_fusion), channel_id=1, source_target_pairs={{0,16},{1,17},{2,18},{3,19},{4,20},{5,21},{6,22},{7,23},{8,24},{9,... | collective-permute-start | bytes 2359304 | tf_op jit(solution)/shard_map/ppermute | solution.py:26
  115.0 19.8 %collective-permute-start.39 = (bf16[384,384]{1,0:T(8,128)(2,1)S(1)}, bf16[384,384]{1,0:T(8,128)(2,1)S(1)}, u32[]{:S(2)}, u32[]{:S(2)}) collective-permute-start(bf16[384,384]{1,0:T(8,128)(2,1)S(1)} %get-tuple-element.84.refs_8_), channel_id=1, source_target_pairs={{0,8},{1,9},{2,10},{3,11},{4,12},{5,13},{6,14},{7,15},{8,0},{9,1},... | collective-permute-start | bytes 884744 | tf_op jit(solution)/shard_map/ppermute | solution.py:26
  121.4 33.0 %collective-permute-start.8 = (bf16[128,1536]{1,0:T(8,128)(2,1)S(1)}, bf16[128,1536]{1,0:T(8,128)(2,1)S(1)}, u32[]{:S(2)}, u32[]{:S(2)}) collective-permute-start(bf16[128,1536]{1,0:T(8,128)(2,1)S(1)} %collective-permute-done.7.refs_4_), channel_id=1, source_target_pairs={{0,16},{1,17},{2,18},{3,19},{4,20},{5,21},{6,22},{7,23},{8,24},{9,... | collective-permute-start | bytes 1179656 | tf_op jit(solution)/shard_map/ppermute | solution.py:26
  124.9 27.7 %collective-permute-start.6 = (bf16[128,1536]{1,0:T(8,128)(2,1)S(1)}, bf16[128,1536]{1,0:T(8,128)(2,1)S(1)}, u32[]{:S(2)}, u32[]{:S(2)}) collective-permute-start(bf16[128,1536]{1,0:T(8,128)(2,1)S(1)} %collective-permute-done.5.refs_2_), channel_id=1, source_target_pairs={{0,16},{1,17},{2,18},{3,19},{4,20},{5,21},{6,22},{7,23},{8,24},{9,... | collective-permute-start | bytes 1179656 | tf_op jit(solution)/shard_map/ppermute | solution.py:26
  130.6 24.8 %collective-permute-start.10 = (bf16[128,1536]{1,0:T(8,128)(2,1)S(1)}, bf16[128,1536]{1,0:T(8,128)(2,1)S(1)}, u32[]{:S(2)}, u32[]{:S(2)}) collective-permute-start(bf16[128,1536]{1,0:T(8,128)(2,1)S(1)} %collective-permute-done.9.refs_6_), channel_id=1, source_target_pairs={{0,16},{1,17},{2,18},{3,19},{4,20},{5,21},{6,22},{7,23},{8,24},{9,... | collective-permute-start | bytes 1179656 | tf_op jit(solution)/shard_map/ppermute | solution.py:26
  150.8 46.0 %collective-permute-start.45 = (bf16[384,384]{1,0:T(8,128)(2,1)S(1)}, bf16[384,384]{1,0:T(8,128)(2,1)S(1)}, u32[]{:S(2)}, u32[]{:S(2)}) collective-permute-start(bf16[384,384]{1,0:T(8,128)(2,1)S(1)} %copy-done.14), channel_id=1, source_target_pairs={{0,8},{1,9},{2,10},{3,11},{4,12},{5,13},{6,14},{7,15},{8,0},{9,1},... | collective-permute-start | bytes 884744 | tf_op jit(solution)/shard_map/ppermute | solution.py:26
  152.6 44.2 %collective-permute-start.46 = (bf16[384,384]{1,0:T(8,128)(2,1)S(1)}, bf16[384,384]{1,0:T(8,128)(2,1)S(1)}, u32[]{:S(2)}, u32[]{:S(2)}) collective-permute-start(bf16[384,384]{1,0:T(8,128)(2,1)S(1)} %copy-done.36), channel_id=1, source_target_pairs={{0,12},{1,13},{2,14},{3,15},{4,8},{5,9},{6,10},{7,11},{8,4},{9,5},... | collective-permute-start | bytes 884744 | tf_op jit(solution)/shard_map/ppermute | solution.py:26
  154.4 32.0 %collective-permute-start.41 = (bf16[384,384]{1,0:T(8,128)(2,1)S(1)}, bf16[384,384]{1,0:T(8,128)(2,1)S(1)}, u32[]{:S(2)}, u32[]{:S(2)}) collective-permute-start(bf16[384,384]{1,0:T(8,128)(2,1)S(1)} %collective-permute-done.39.refs_12_), channel_id=1, source_target_pairs={{0,2},{1,3},{2,0},{3,1},{4,6},{5,7},{6,4},{7,5},{8,10},{9,11},{10,... | collective-permute-start | bytes 884744 | tf_op jit(solution)/shard_map/ppermute | solution.py:26
  155.4 30.9 %collective-permute-start.44 = (bf16[384,384]{1,0:T(8,128)(2,1)S(1)}, bf16[384,384]{1,0:T(8,128)(2,1)S(1)}, u32[]{:S(2)}, u32[]{:S(2)}) collective-permute-start(bf16[384,384]{1,0:T(8,128)(2,1)S(1)} %collective-permute-done.42.refs_14_), channel_id=1, source_target_pairs={{0,2},{1,3},{2,0},{3,1},{4,6},{5,7},{6,4},{7,5},{8,10},{9,11},{10,... | collective-permute-start | bytes 884744 | tf_op jit(solution)/shard_map/ppermute | solution.py:26
  202.6 23.0 %collective-permute-start.50 = (bf16[128,1536]{1,0:T(8,128)(2,1)S(1)}, bf16[128,1536]{1,0:T(8,128)(2,1)S(1)}, u32[]{:S(2)}, u32[]{:S(2)}) collective-permute-start(bf16[128,1536]{1,0:T(8,128)(2,1)S(1)} %get-tuple-element.132), channel_id=1, source_target_pairs={{0,1},{1,0},{2,3},{3,2},{4,5},{5,4},{6,7},{7,6},{8,9},{9,8},{10,11... | collective-permute-start | bytes 1179656 | tf_op jit(solution)/shard_map/ppermute | solution.py:26
  224.1 24.7 %collective-permute-start.49 = (bf16[128,1536]{1,0:T(8,128)(2,1)}, bf16[128,1536]{1,0:T(8,128)(2,1)}, u32[]{:S(2)}, u32[]{:S(2)}) collective-permute-start(bf16[128,1536]{1,0:T(8,128)(2,1)} %get-tuple-element.96), channel_id=1, source_target_pairs={{0,1},{1,0},{2,3},{3,2},{4,5},{5,4},{6,7},{7,6},{8,9},{9,8},{10,11... | collective-permute-start | bytes 1179656 | tf_op jit(solution)/shard_map/ppermute | solution.py:26
  226.5 23.3 %collective-permute-start.51 = (bf16[128,1536]{1,0:T(8,128)(2,1)}, bf16[128,1536]{1,0:T(8,128)(2,1)}, u32[]{:S(2)}, u32[]{:S(2)}) collective-permute-start(bf16[128,1536]{1,0:T(8,128)(2,1)} %fusion.6), channel_id=1, source_target_pairs={{0,4},{1,5},{2,6},{3,7},{4,0},{5,1},{6,2},{7,3},{8,12},{9,13},{10,... | collective-permute-start | bytes 1179656 | tf_op jit(solution)/shard_map/ppermute | solution.py:26
  244.1 23.7 %collective-permute-start.71 = (bf16[384,384]{1,0:T(8,128)(2,1)}, bf16[384,384]{1,0:T(8,128)(2,1)S(1)}, u32[]{:S(2)}, u32[]{:S(2)}) collective-permute-start(bf16[384,384]{1,0:T(8,128)(2,1)} %get-tuple-element.110.refs_0_), channel_id=1, source_target_pairs={{0,8},{1,9},{2,10},{3,11},{4,12},{5,13},{6,14},{7,15},{8,0},{9,1},... | collective-permute-start | bytes 884744 | tf_op jit(solution)/shard_map/ppermute | solution.py:26
  246.8 21.9 %collective-permute-start.74 = (bf16[384,384]{1,0:T(8,128)(2,1)}, bf16[384,384]{1,0:T(8,128)(2,1)S(1)}, u32[]{:S(2)}, u32[]{:S(2)}) collective-permute-start(bf16[384,384]{1,0:T(8,128)(2,1)} %get-tuple-element.113), channel_id=1, source_target_pairs={{0,12},{1,13},{2,14},{3,15},{4,8},{5,9},{6,10},{7,11},{8,4},{9,5},... | collective-permute-start | bytes 884744 | tf_op jit(solution)/shard_map/ppermute | solution.py:26
  249.8 23.4 %collective-permute-start.72 = (bf16[384,384]{1,0:T(8,128)(2,1)}, bf16[384,384]{1,0:T(8,128)(2,1)S(1)}, u32[]{:S(2)}, u32[]{:S(2)}) collective-permute-start(bf16[384,384]{1,0:T(8,128)(2,1)} %get-tuple-element.117.refs_8_), channel_id=1, source_target_pairs={{0,2},{1,3},{2,0},{3,1},{4,6},{5,7},{6,4},{7,5},{8,10},{9,11},{10,... | collective-permute-start | bytes 884744 | tf_op jit(solution)/shard_map/ppermute | solution.py:26
  257.4 18.5 %collective-permute-start.56 = (bf16[128,1536]{1,0:T(8,128)(2,1)S(1)}, bf16[128,1536]{1,0:T(8,128)(2,1)S(1)}, u32[]{:S(2)}, u32[]{:S(2)}) collective-permute-start(bf16[128,1536]{1,0:T(8,128)(2,1)S(1)} %fusion.11.refs_0_), channel_id=1, source_target_pairs={{0,4},{1,5},{2,6},{3,7},{4,0},{5,1},{6,2},{7,3},{8,12},{9,13},{10,... | collective-permute-start | bytes 1179656 | tf_op jit(solution)/shard_map/ppermute | solution.py:26
  259.1 34.6 %collective-permute-start.53 = (bf16[128,1536]{1,0:T(8,128)(2,1)S(1)}, bf16[128,1536]{1,0:T(8,128)(2,1)S(1)}, u32[]{:S(2)}, u32[]{:S(2)}) collective-permute-start(bf16[128,1536]{1,0:T(8,128)(2,1)S(1)} %fusion.11.refs_0_), channel_id=1, source_target_pairs={{0,1},{1,0},{2,3},{3,2},{4,5},{5,4},{6,7},{7,6},{8,9},{9,8},{10,11... | collective-permute-start | bytes 1179656 | tf_op jit(solution)/shard_map/ppermute | solution.py:26
  268.7 24.3 %collective-permute-start.78 = (bf16[384,384]{1,0:T(8,128)(2,1)S(1)}, bf16[384,384]{1,0:T(8,128)(2,1)S(1)}, u32[]{:S(2)}, u32[]{:S(2)}) collective-permute-start(bf16[384,384]{1,0:T(8,128)(2,1)S(1)} %copy-done.10), channel_id=1, source_target_pairs={{0,8},{1,9},{2,10},{3,11},{4,12},{5,13},{6,14},{7,15},{8,0},{9,1},... | collective-permute-start | bytes 884744 | tf_op jit(solution)/shard_map/ppermute | solution.py:26
  273.1 20.5 %collective-permute-start.80 = (bf16[384,384]{1,0:T(8,128)(2,1)S(1)}, bf16[384,384]{1,0:T(8,128)(2,1)S(1)}, u32[]{:S(2)}, u32[]{:S(2)}) collective-permute-start(bf16[384,384]{1,0:T(8,128)(2,1)S(1)} %copy-done.35), channel_id=1, source_target_pairs={{0,12},{1,13},{2,14},{3,15},{4,8},{5,9},{6,10},{7,11},{8,4},{9,5},... | collective-permute-start | bytes 884744 | tf_op jit(solution)/shard_map/ppermute | solution.py:26
  275.9 18.4 %collective-permute-start.58 = (bf16[128,1536]{1,0:T(8,128)(2,1)S(1)}, bf16[128,1536]{1,0:T(8,128)(2,1)S(1)}, u32[]{:S(2)}, u32[]{:S(2)}) collective-permute-start(bf16[128,1536]{1,0:T(8,128)(2,1)S(1)} %collective-permute-done.56.refs_4_), channel_id=1, source_target_pairs={{0,1},{1,0},{2,3},{3,2},{4,5},{5,4},{6,7},{7,6},{8,9},{9,8},{10,11... | collective-permute-start | bytes 1179656 | tf_op jit(solution)/shard_map/ppermute | solution.py:26
  299.8 20.9 %collective-permute-start.79 = (bf16[384,384]{1,0:T(8,128)(2,1)S(1)}, bf16[384,384]{1,0:T(8,128)(2,1)S(1)}, u32[]{:S(2)}, u32[]{:S(2)}) collective-permute-start(bf16[384,384]{1,0:T(8,128)(2,1)S(1)} %collective-permute-done.78.refs_12_), channel_id=1, source_target_pairs={{0,2},{1,3},{2,0},{3,1},{4,6},{5,7},{6,4},{7,5},{8,10},{9,11},{10,... | collective-permute-start | bytes 884744 | tf_op jit(solution)/shard_map/ppermute | solution.py:26
  300.5 20.3 %collective-permute-start.81 = (bf16[384,384]{1,0:T(8,128)(2,1)S(1)}, bf16[384,384]{1,0:T(8,128)(2,1)S(1)}, u32[]{:S(2)}, u32[]{:S(2)}) collective-permute-start(bf16[384,384]{1,0:T(8,128)(2,1)S(1)} %collective-permute-done.80.refs_14_), channel_id=1, source_target_pairs={{0,2},{1,3},{2,0},{3,1},{4,6},{5,7},{6,4},{7,5},{8,10},{9,11},{10,... | collective-permute-start | bytes 884744 | tf_op jit(solution)/shard_map/ppermute | solution.py:26
  338.5 18.5 %collective-permute-start.83 = (bf16[128,1536]{1,0:T(8,128)(2,1)S(1)}, bf16[128,1536]{1,0:T(8,128)(2,1)S(1)}, u32[]{:S(2)}, u32[]{:S(2)}) collective-permute-start(bf16[128,1536]{1,0:T(8,128)(2,1)S(1)} %get-tuple-element.128), channel_id=1, source_target_pairs={{0,1},{1,0},{2,3},{3,2},{4,5},{5,4},{6,7},{7,6},{8,9},{9,8},{10,11... | collective-permute-start | bytes 1179656 | tf_op jit(solution)/shard_map/ppermute | solution.py:26
  (140 other events, 2337.3 us)

commit v2 on v1

--- a/solution.py
+++ b/solution.py
@@ -99,24 +99,27 @@
 
 def modulate(plan, wc, mod_ref, xv, xm):
     slots, slot_len, cols = plan
-    feat = cols * wc
-    for slot in range(slots):
-        rows = pl.ds(slot * slot_len, slot_len)
-        total = jnp.zeros((slot_len, 1), jnp.float32)
-        squares = jnp.zeros((slot_len, 1), jnp.float32)
-        for col in range(cols):
-            part = xv[col, rows, :].astype(jnp.float32)
-            total += jnp.sum(part, axis=-1, keepdims=True)
-            squares += jnp.sum(part * part, axis=-1, keepdims=True)
-        mean = total / feat
-        var = squares / feat - mean * mean
-        inverse = lax.rsqrt(var + 1e-06)
-        for col in range(cols):
-            span = pl.ds(col * wc, wc)
-            part = xv[col, rows, :].astype(jnp.float32)
-            shift = mod_ref[slot, 0:1, span]
-            scale = mod_ref[slot, 1:2, span]
-            xm[rows, span] = ((part - mean) * inverse * (1.0 + scale) + shift).astype(jnp.bfloat16)
+    feat, tile = cols * wc, 16
+    for slot in range(slots):
+
+        def some_rows(step, carry, slot=slot):
+            rows = pl.ds(pl.multiple_of(slot * slot_len + step * tile, tile), tile)
+            parts = [xv[col, rows, :].astype(jnp.float32) for col in range(cols)]
+            total = sum(jnp.sum(part, axis=-1, keepdims=True) for part in parts)
+            squares = sum(jnp.sum(part * part, axis=-1, keepdims=True) for part in parts)
+            mean = total / feat
+            var = squares / feat - mean * mean
+            inverse = lax.rsqrt(var + 1e-06)
+            for col in range(cols):
+                span = pl.ds(col * wc, wc)
+                part = xv[col, rows, :].astype(jnp.float32)
+                shift = mod_ref[slot, 0:1, span]
+                scale = mod_ref[slot, 1:2, span]
+                part = (part - mean) * inverse * (1.0 + scale) + shift
+                xm[rows, span] = part.astype(jnp.bfloat16)
+            return carry
+
+        lax.fori_loop(0, slot_len // tile, some_rows, 0, unroll=2)
 
 
 def modulate_kernel(plan, wc, mod_ref, *refs):
@@ -132,7 +135,7 @@
     x_ref, refs = refs[0], refs[1:]
     w_refs, refs = (refs[:n_w], refs[n_w : 2 * n_w]), refs[2 * n_w :]
     kv_refs, refs = refs[:slots], refs[slots:]
-    weights_ref, xm, wv, kvv, x_sem, w_sem, kv_sem = refs
+    weights_ref, xm, wv, raw_ref, kvv, x_sem, w_sem, kv_sem = refs
     x_copies = [pltpu.make_async_copy(x_ref, xm, x_sem.at[0])]
     x_copies[0].start()
     copies = load_rows(w_refs[0], wv.at[0], w_sem, 0, kr)
@@ -150,14 +153,15 @@
         mean = jnp.mean(block * block, axis=-1, keepdims=True)
         return (block * lax.rsqrt(mean + 1e-06)).astype(jnp.bfloat16)
 
+    for t in range(2):
+        raw_ref[t] = jnp.dot(xm[...], wv[t], preferred_element_type=jnp.float32)
     for slot in range(slots):
         rows = pl.ds(slot * slot_len, slot_len)
-        raw = [jnp.dot(xm[rows, :], wv[t], preferred_element_type=jnp.float32) for t in range(2)]
         fresh, valid = fresh_and_valid(ends_ref, slot, slot_len)
         for head in range(bw // HD):
             lanes = slice(head * HD, (head + 1) * HD)
-            query = normed(raw[0][:, lanes])
-            kvv[slot, 0:slot_len, lanes] = normed(raw[1][:, lanes])
+            query = normed(raw_ref[0, rows, lanes])
+            kvv[slot, 0:slot_len, lanes] = normed(raw_ref[1, rows, lanes])
             both = lax.dot_general(
                 query, kvv[slot, :, lanes], contract, preferred_element_type=jnp.float32
             )
@@ -193,10 +197,9 @@
     o_copies = load_rows(o_refs, ov, w_sem, n_w, None)
     for copy in [x_copy] + copies:
         copy.wait()
-    for slot in range(slots):
-        rows = pl.ds(slot * slot_len, slot_len)
-        raw = jnp.dot(xm[rows, :], wv[...], preferred_element_type=jnp.float32)
-        kvv[slot, 0:slot_len, :] = raw.astype(jnp.bfloat16)
+    raw = jnp.dot(xm[...], wv[...], preferred_element_type=jnp.float32).astype(jnp.bfloat16)
+    for slot in range(slots):
+        kvv[slot, 0:slot_len, :] = raw[slot * slot_len : (slot + 1) * slot_len]
     for copy in late:
         copy.wait()
     for slot in range(slots):
@@ -207,19 +210,20 @@
             att[rows, lanes] = mixed.astype(jnp.bfloat16)
     for copy in o_copies:
         copy.wait()
-    for side, out_ref in ((1 - s, pass_ref), (s, keep_ref)):
-        blocks = []
+    blocks = []
+    for side in (1 - s, s):
         for slot in range(slots):
             row = pl.multiple_of(slot * slot_len + side * half, half)
             blocks.append(att[pl.ds(row, half), :])
-        lhs = jnp.concatenate(blocks, axis=0)
-        for place in range(n_w):
-            row = lax.rem(c * (n_w // cols) + place, n_w)
-            part = jnp.dot(lhs, ov[row], preferred_element_type=jnp.float32).astype(jnp.bfloat16)
+    lhs = jnp.concatenate(blocks, axis=0)
+    for place in range(n_w):
+        row = lax.rem(c * (n_w // cols) + place, n_w)
+        part = jnp.dot(lhs, ov[row], preferred_element_type=jnp.float32).astype(jnp.bfloat16)
+        lanes = slice(place * nr, (place + 1) * nr)
+        for k, out_ref in enumerate((pass_ref, keep_ref)):
             for slot in range(slots):
-                out_ref[slot, :, place * nr : (place + 1) * nr] = part[
-                    slot * half : (slot + 1) * half
-                ]
+                first = (k * slots + slot) * half
+                out_ref[slot, :, lanes] = part[first : first + half]
 
 
 def mod_kernel(slots, feats_ref, weight_ref, out_ref):
@@ -230,23 +234,25 @@
 
 
 GATES = {
-    "V0.4": ("Q0.4",),
-    "V0.6": ("Q0.6",),
-    "O0.4": ("K0.4",),
-    "O0.6": ("K0.6",),
-    "Q1.4": ("V0.4",),
-    "Q1.6": ("V0.6",),
-    "K1.4": ("O0.4",),
-    "K1.6": ("O0.6",),
-    "V1.4": ("Q1.4",),
-    "V1.6": ("Q1.6",),
-    "O1.4": ("K1.4",),
-    "O1.6": ("K1.6",),
+    "K0.4": ("Q0.4",),
+    "K0.6": ("Q0.6",),
+    "V0.4": ("K0.4",),
+    "V0.6": ("K0.6",),
+    "O0.4": ("V0.4",),
+    "O0.6": ("V0.6",),
+    "Q1.4": ("O0.4", "Q0.3",),
+    "Q1.6": ("O0.6",),
+    "K1.4": ("Q1.4",),
+    "K1.6": ("Q1.6",),
+    "V1.4": ("K1.4",),
+    "V1.6": ("K1.6",),
+    "O1.4": ("V1.4",),
+    "O1.6": ("V1.6",),
     "O0.2": ("Q0.2",),
-    "Q1.2": ("K0.2",),
-    "K1.2": ("S0.2",),
+    "Q1.2": ("S0.2",),
+    "K1.2": ("K0.2",),
     "V1.2": ("V0.2",),
-    "O1.2": ("O0.2",),
+    "O1.2": ("O0.2", "O0.5",),
     "S1.2": ("Q1.2",),
     "K0.1": ("Q0.1",),
     "K0.3": ("Q0.3",),
@@ -284,7 +290,8 @@
     "p0": ("Q1.4", "Q1.6",),
     "r0.0.1": ("K1.4",),
     "g.2.0": ("K1.6",),
-    "k0": ("Q1.2",),
+    "O1.0": ("V1.3",),
+    "x.0.0c": ("aV",),
 }
 TREE = ("x", "r0", "g", )
 
@@ -450,6 +457,7 @@
             scratch_shapes=[
                 pltpu.VMEM((slots * slot_len, feat), jnp.bfloat16),
                 pltpu.VMEM((2, feat, bw), jnp.bfloat16),
+                pltpu.VMEM((2, slots * slot_len, bw), jnp.float32),
                 pltpu.VMEM((slots, 2 * slot_len, bw), jnp.bfloat16),
                 pltpu.SemaphoreType.DMA((1,)),
                 pltpu.SemaphoreType.DMA((2 * rows,)),

time: 366 us -> 345 us (0.943); the launches traced: 362 us -> 345 us
  starting transfers between devices: 95.9 us -> 89 us
  Pallas kernels: 64.2 us -> 57.6 us
  waiting for transfers between devices: 165 us -> 159 us
    pallas_call x2, Pallas kernels: 29.1 us -> 20 us  [scores(): pl.pallas_call(functools.partial(scores_kernel, (slots, slot_len, rows, k...]
    ppermute x87, starting transfers between devices: 95.9 us -> 89 us  [send_to(): return lax.ppermute(array, AXES, pairs)]
    ppermute x87, waiting for transfers between devices: 165 us -> 159 us  [send_to(): return lax.ppermute(array, AXES, pairs)]
    unnamed x170 -> x174, local copies, waits for them, and re-layouts: 8.29 us -> 6.79 us
  transfers between devices with their start and end apart: 87 -> 87, of which waited for: 37 -> 38; matrix products, arithmetic and copies ran while one was open for 5% -> 7% of each run, Pallas kernels for 15% -> 14%
where the time goes in v2:
time: 345 us
  waiting for transfers between devices  159 us (46%)
  starting transfers between devices  89 us (26%)
  Pallas kernels  57.6 us (17%)
  other arithmetic  22.4 us (6%)
  local copies, waits for them, and re-layouts  15.2 us (4%)
    ppermute x87, waiting for transfers between devices, send_to(): return lax.ppermute(array, AXES, pairs)  159 us
    ppermute x87, starting transfers between devices, send_to(): return lax.ppermute(array, AXES, pairs)  89 us
    pallas_call x2, Pallas kernels, scores(): pl.pallas_call(functools.partial(scores_kernel, (slots, slot_len, rows, k...  20 us
    pallas_call x2, Pallas kernels, mix(): pl.pallas_call(functools.partial(mix_kernel, plan), out_shape=(shape, sha...  18.7 us
    pallas_call x2, Pallas kernels, modulated(): pl.pallas_call(functools.partial(modulate_kernel, (slots, slot_len, cols)...  15.2 us
    select_n x5, other arithmetic, block_of(): block = jnp.where(s == layer, cut(kind, s * wide + at, bw), other)  10.5 us
  transfers between devices with their start and end apart: 87, of which 38 were waited for; matrix products, arithmetic and copies ran while one was open for 7% of the time, Pallas kernels for 14%

profile of v2, /device:TPU:0, one launch (start us, length us, event | category | flops | bytes accessed | tf_op | source)
XLA Modules:
  0.0 344.9 jit_solution(11192618976326368494)
XLA Ops:
  19.6 7.0 %collective-permute-done.12.refs_3_ = bf16[384,384]{1,0:T(8,128)(2,1)S(1)} collective-permute-done((bf16[384,384]{1,0:T(8,128)(2,1)S(1)}, bf16[384,384]{1,0:T(8,128)(2,1)S(1)}, u32[]{:S(2)}, u32[]{:S(2)}) %collective-permute-start.12) | collective-permute-done | bytes 294944 | tf_op jit(solution)/shard_map/ppermute | solution.py:26
  26.9 3.9 %collective-permute-start.2 = (bf16[384,384]{1,0:T(8,128)(2,1)S(1)}, bf16[384,384]{1,0:T(8,128)(2,1)}, u32[]{:S(2)}, u32[]{:S(2)}) collective-permute-start(bf16[384,384]{1,0:T(8,128)(2,1)S(1)} %get-tuple-element.151), channel_id=1, source_target_pairs={{0,12},{1,13},{2,14},{3,15},{4,8},{5,9},{6,10},{7,11},{8,4},{9,5},... | collective-permute-start | bytes 884744 | tf_op jit(solution)/shard_map/ppermute | solution.py:26
  35.8 6.1 %collective-permute-done.16.refs_6_ = bf16[384,384]{1,0:T(8,128)(2,1)S(1)} collective-permute-done((bf16[384,384]{1,0:T(8,128)(2,1)S(1)}, bf16[384,384]{1,0:T(8,128)(2,1)S(1)}, u32[]{:S(2)}, u32[]{:S(2)}) %collective-permute-start.16) | collective-permute-done | bytes 294944 | tf_op jit(solution)/shard_map/ppermute | solution.py:26
  41.9 3.7 %collective-permute-start.20 = (bf16[384,384]{1,0:T(8,128)(2,1)}, bf16[384,384]{1,0:T(8,128)(2,1)}, u32[]{:S(2)}, u32[]{:S(2)}) collective-permute-start(bf16[384,384]{1,0:T(8,128)(2,1)} %get-tuple-element.73.refs_9_), channel_id=1, source_target_pairs={{0,8},{1,9},{2,10},{3,11},{4,12},{5,13},{6,14},{7,15},{8,0},{9,1},... | collective-permute-start | bytes 884744 | tf_op jit(solution)/shard_map/ppermute | solution.py:26
  48.2 5.1 %collective-permute-start.25 = (bf16[384,384]{1,0:T(8,128)(2,1)}, bf16[384,384]{1,0:T(8,128)(2,1)}, u32[]{:S(2)}, u32[]{:S(2)}) collective-permute-start(bf16[384,384]{1,0:T(8,128)(2,1)} %get-tuple-element.82), channel_id=1, source_target_pairs={{0,4},{1,5},{2,6},{3,7},{4,0},{5,1},{6,2},{7,3},{8,12},{9,13},{10,... | collective-permute-start | bytes 884744 | tf_op jit(solution)/shard_map/ppermute | solution.py:26
  59.7 8.1 %collective-permute-done.25.refs_2_ = bf16[384,384]{1,0:T(8,128)(2,1)} collective-permute-done((bf16[384,384]{1,0:T(8,128)(2,1)}, bf16[384,384]{1,0:T(8,128)(2,1)}, u32[]{:S(2)}, u32[]{:S(2)}) %collective-permute-start.25) | collective-permute-done | bytes 294944 | tf_op jit(solution)/shard_map/ppermute | solution.py:26
  67.8 3.7 %collective-permute-start.23 = (bf16[384,384]{1,0:T(8,128)(2,1)}, bf16[384,384]{1,0:T(8,128)(2,1)S(1)}, u32[]{:S(2)}, u32[]{:S(2)}) collective-permute-start(bf16[384,384]{1,0:T(8,128)(2,1)} %collective-permute-done.20.refs_13_), channel_id=1, source_target_pairs={{0,2},{1,3},{2,0},{3,1},{4,6},{5,7},{6,4},{7,5},{8,10},{9,11},{10,... | collective-permute-start | bytes 884744 | tf_op jit(solution)/shard_map/ppermute | solution.py:26
  74.4 11.5 %collective-permute-done.26.refs_3_ = bf16[384,384]{1,0:T(8,128)(2,1)S(1)} collective-permute-done((bf16[384,384]{1,0:T(8,128)(2,1)}, bf16[384,384]{1,0:T(8,128)(2,1)S(1)}, u32[]{:S(2)}, u32[]{:S(2)}) %collective-permute-start.26) | collective-permute-done | bytes 294944 | tf_op jit(solution)/shard_map/ppermute | solution.py:26
  98.9 5.3 %collective-permute-done.29.refs_18_.refs_17_ = bf16[2,256,384]{2,1,0:T(8,128)(2,1)S(1)} collective-permute-done((bf16[2,256,384]{2,1,0:T(8,128)(2,1)S(1)}, bf16[2,256,384]{2,1,0:T(8,128)(2,1)S(1)}, u32[]{:S(2)}, u32[]{:S(2)}) %collective-permute-start.29) | collective-permute-done | bytes 393248 | tf_op jit(solution)/shard_map/ppermute | solution.py:26
  104.7 9.9 %collective-permute-done.7.refs_4_ = bf16[128,1536]{1,0:T(8,128)(2,1)S(1)} collective-permute-done((bf16[128,1536]{1,0:T(8,128)(2,1)S(1)}, bf16[128,1536]{1,0:T(8,128)(2,1)S(1)}, u32[]{:S(2)}, u32[]{:S(2)}) %collective-permute-start.7) | collective-permute-done | bytes 393248 | tf_op jit(solution)/shard_map/ppermute | solution.py:26
  123.0 3.5 %collective-permute-done.37.refs_7_ = bf16[384,384]{1,0:T(8,128)(2,1)S(1)} collective-permute-done((bf16[384,384]{1,0:T(8,128)(2,1)S(1)}, bf16[384,384]{1,0:T(8,128)(2,1)S(1)}, u32[]{:S(2)}, u32[]{:S(2)}) %collective-permute-start.37) | collective-permute-done | bytes 294944 | tf_op jit(solution)/shard_map/ppermute | solution.py:26
  130.6 8.0 %collective-permute-done.38.refs_12_ = bf16[384,384]{1,0:T(8,128)(2,1)S(1)} collective-permute-done((bf16[384,384]{1,0:T(8,128)(2,1)S(1)}, bf16[384,384]{1,0:T(8,128)(2,1)S(1)}, u32[]{:S(2)}, u32[]{:S(2)}) %collective-permute-start.38) | collective-permute-done | bytes 294944 | tf_op jit(solution)/shard_map/ppermute | solution.py:26
  141.0 3.7 %modulation.1 = f32[2,3,3072]{2,1,0:T(4,128)} custom-call(bf16[8,256]{1,0:T(8,128)(2,1)} %fusion.21.feats_ref, bf16[3,256,3072]{2,1,0:T(8,128)(2,1)} %bitcast.107), custom_call_target="tpu_custom_call" | custom-call | tf_op jit(solution)/shard_map/modulation/pallas_call | solution.py:400
  151.0 7.5 %modulate.2.refs_0_.x_ref = bf16[512,3072]{1,0:T(8,128)(2,1)} custom-call(f32[2,3,3072]{2,1,0:T(4,128)} %get-tuple-element.166.mod_ref, bf16[128,1536]{1,0:T(8,128)(2,1)} %copy-done.2, bf16[128,1536]{1,0:T(8,128)(2,1)} %get-tuple-element.163.refs_1_, bf16[128,1536]{1,0:T(8,128)(2,1)} %copy-done.22, bf16[128,1536]{1,0:T(8,128)(2,1)} %copy-done.27, ...), custom_call_target="tpu_custom_call" | custom-call | tf_op jit(solution)/shard_map/modulate/pallas_call | solution.py:435
  158.6 10.0 %scores.2.weights_ref = bf16[2,3,256,512]{3,2,1,0:T(8,128)(2,1)} custom-call(s32[2,4]{1,0:T(2,128)} %bitcast.115, bf16[512,3072]{1,0:T(8,128)(2,1)} %modulate.2.refs_0_.x_ref, bf16[384,384]{1,0:T(8,128)(2,1)} %copy-done.16, bf16[384,384]{1,0:T(8,128)(2,1)} %copy-done.65, bf16[384,384]{1,0:T(8,128)(2,1)} %copy-done.66, bf16[384,384]{1,0:T(8,128)(2,1)} %copy-done.72, ...), custom_call_target="tpu_custom_call" | custom-call | tf_op jit(solution)/shard_map/scores/pallas_call | solution.py:449
  170.1 9.3 %mix.2 = (bf16[2,128,3072]{2,1,0:T(8,128)(2,1)}, bf16[2,128,3072]{2,1,0:T(8,128)(2,1)}) custom-call(bf16[512,3072]{1,0:T(8,128)(2,1)} %modulate.2.refs_0_.x_ref, bf16[2,3,256,512]{3,2,1,0:T(8,128)(2,1)} %scores.2.weights_ref, bf16[384,384]{1,0:T(8,128)(2,1)} %copy-done.11, bf16[384,384]{1,0:T(8,128)(2,1)} %copy-done.37, ...), custom_call_target="tpu_custom_call" | custom-call | tf_op jit(solution)/shard_map/mix/pallas_call | solution.py:479
  186.3 3.6 %collective-permute-done.62.refs_11_ = bf16[384,384]{1,0:T(8,128)(2,1)S(1)} collective-permute-done((bf16[384,384]{1,0:T(8,128)(2,1)}, bf16[384,384]{1,0:T(8,128)(2,1)S(1)}, u32[]{:S(2)}, u32[]{:S(2)}) %collective-permute-start.62) | collective-permute-done | bytes 294944 | tf_op jit(solution)/shard_map/ppermute | solution.py:26
  195.6 4.3 %collective-permute-done.63.refs_12_ = bf16[384,384]{1,0:T(8,128)(2,1)S(1)} collective-permute-done((bf16[384,384]{1,0:T(8,128)(2,1)S(1)}, bf16[384,384]{1,0:T(8,128)(2,1)S(1)}, u32[]{:S(2)}, u32[]{:S(2)}) %collective-permute-start.63) | collective-permute-done | bytes 294944 | tf_op jit(solution)/shard_map/ppermute | solution.py:26
  201.4 4.8 %collective-permute-done.61.refs_6_ = bf16[384,384]{1,0:T(8,128)(2,1)S(1)} collective-permute-done((bf16[384,384]{1,0:T(8,128)(2,1)S(1)}, bf16[384,384]{1,0:T(8,128)(2,1)S(1)}, u32[]{:S(2)}, u32[]{:S(2)}) %collective-permute-start.61) | collective-permute-done | bytes 294944 | tf_op jit(solution)/shard_map/ppermute | solution.py:26
  214.0 4.8 %collective-permute-done.65.refs_1_ = bf16[384,384]{1,0:T(8,128)(2,1)S(1)} collective-permute-done((bf16[384,384]{1,0:T(8,128)(2,1)S(1)}, bf16[384,384]{1,0:T(8,128)(2,1)S(1)}, u32[]{:S(2)}, u32[]{:S(2)}) %collective-permute-start.65) | collective-permute-done | bytes 294944 | tf_op jit(solution)/shard_map/ppermute | solution.py:26
  223.3 4.3 %collective-permute-done.55.refs_15_ = bf16[384,384]{1,0:T(8,128)(2,1)} collective-permute-done((bf16[384,384]{1,0:T(8,128)(2,1)}, bf16[384,384]{1,0:T(8,128)(2,1)}, u32[]{:S(2)}, u32[]{:S(2)}) %collective-permute-start.55) | collective-permute-done | bytes 294944 | tf_op jit(solution)/shard_map/ppermute | solution.py:26
  235.5 10.9 %collective-permute-done.71.refs_4_ = bf16[384,384]{1,0:T(8,128)(2,1)S(1)} collective-permute-done((bf16[384,384]{1,0:T(8,128)(2,1)}, bf16[384,384]{1,0:T(8,128)(2,1)S(1)}, u32[]{:S(2)}, u32[]{:S(2)}) %collective-permute-start.71) | collective-permute-done | bytes 294944 | tf_op jit(solution)/shard_map/ppermute | solution.py:26
  247.7 3.8 %collective-permute-done.75.refs_10_ = bf16[384,384]{1,0:T(8,128)(2,1)S(1)} collective-permute-done((bf16[384,384]{1,0:T(8,128)(2,1)}, bf16[384,384]{1,0:T(8,128)(2,1)S(1)}, u32[]{:S(2)}, u32[]{:S(2)}) %collective-permute-start.75) | collective-permute-done | bytes 294944 | tf_op jit(solution)/shard_map/ppermute | solution.py:26
  255.6 5.5 %collective-permute-done.56.refs_4_ = bf16[128,1536]{1,0:T(8,128)(2,1)S(1)} collective-permute-done((bf16[128,1536]{1,0:T(8,128)(2,1)S(1)}, bf16[128,1536]{1,0:T(8,128)(2,1)S(1)}, u32[]{:S(2)}, u32[]{:S(2)}) %collective-permute-start.56) | collective-permute-done | bytes 393248 | tf_op jit(solution)/shard_map/ppermute | solution.py:26
  262.6 12.9 %collective-permute-done.78.refs_12_ = bf16[384,384]{1,0:T(8,128)(2,1)S(1)} collective-permute-done((bf16[384,384]{1,0:T(8,128)(2,1)S(1)}, bf16[384,384]{1,0:T(8,128)(2,1)S(1)}, u32[]{:S(2)}, u32[]{:S(2)}) %collective-permute-start.78) | collective-permute-done | bytes 294944 | tf_op jit(solution)/shard_map/ppermute | solution.py:26
  277.0 5.3 %collective-permute-done.77.refs_7_ = bf16[384,384]{1,0:T(8,128)(2,1)S(1)} collective-permute-done((bf16[384,384]{1,0:T(8,128)(2,1)S(1)}, bf16[384,384]{1,0:T(8,128)(2,1)S(1)}, u32[]{:S(2)}, u32[]{:S(2)}) %collective-permute-start.77) | collective-permute-done | bytes 294944 | tf_op jit(solution)/shard_map/ppermute | solution.py:26
  285.3 7.7 %modulate.3.refs_0_.x_ref = bf16[512,3072]{1,0:T(8,128)(2,1)} custom-call(f32[2,3,3072]{2,1,0:T(4,128)} %get-tuple-element.165.mod_ref, bf16[128,1536]{1,0:T(8,128)(2,1)} %copy-done, bf16[128,1536]{1,0:T(8,128)(2,1)} %copy-done.6, bf16[128,1536]{1,0:T(8,128)(2,1)} %copy-done.25, bf16[128,1536]{1,0:T(8,128)(2,1)} %copy-done.29, bf16[128,1536]{1,0:T(8,128)(2,1)} %copy-done.24, ...), custom_call_target="tpu_custom_call" | custom-call | tf_op jit(solution)/shard_map/modulate/pallas_call | solution.py:435
  293.7 10.0 %scores.3.weights_ref = bf16[2,3,256,512]{3,2,1,0:T(8,128)(2,1)} custom-call(s32[2,4]{1,0:T(2,128)} %bitcast.116, bf16[512,3072]{1,0:T(8,128)(2,1)} %modulate.3.refs_0_.x_ref, bf16[384,384]{1,0:T(8,128)(2,1)} %get-tuple-element.95.refs_1_, bf16[384,384]{1,0:T(8,128)(2,1)} %copy-done.63, bf16[384,384]{1,0:T(8,128)(2,1)} %copy-done.62, ...), custom_call_target="tpu_custom_call" | custom-call | tf_op jit(solution)/shard_map/scores/pallas_call | solution.py:449
  305.2 9.3 %mix.3 = (bf16[2,128,3072]{2,1,0:T(8,128)(2,1)}, bf16[2,128,3072]{2,1,0:T(8,128)(2,1)}) custom-call(bf16[512,3072]{1,0:T(8,128)(2,1)} %modulate.3.refs_0_.x_ref, bf16[2,3,256,512]{3,2,1,0:T(8,128)(2,1)} %scores.3.weights_ref, bf16[384,384]{1,0:T(8,128)(2,1)} %get-tuple-element.113.refs_0_, bf16[384,384]{1,0:T(8,128)(2,1)} %copy-done.40, ...), custom_call_target="tpu_custom_call" | custom-call | tf_op jit(solution)/shard_map/mix/pallas_call | solution.py:479
  314.7 3.6 %collective-permute-done.82 = bf16[2,128,3072]{2,1,0:T(8,128)(2,1)S(1)} collective-permute-done((bf16[2,128,3072]{2,1,0:T(8,128)(2,1)}, bf16[2,128,3072]{2,1,0:T(8,128)(2,1)S(1)}, u32[]{:S(2)}, u32[]{:S(2)}) %collective-permute-start.82) | collective-permute-done | bytes 1572896 | tf_op jit(solution)/shard_map/ppermute | solution.py:26
  324.3 8.5 %collective-permute-done.85 = bf16[128,1536]{1,0:T(8,128)(2,1)S(1)} collective-permute-done((bf16[128,1536]{1,0:T(8,128)(2,1)S(1)}, bf16[128,1536]{1,0:T(8,128)(2,1)S(1)}, u32[]{:S(2)}, u32[]{:S(2)}) %collective-permute-start.85) | collective-permute-done | bytes 393248 | tf_op jit(solution)/shard_map/ppermute | solution.py:26
  332.8 7.7 %collective-permute-done.84 = bf16[128,1536]{1,0:T(8,128)(2,1)S(1)} collective-permute-done((bf16[128,1536]{1,0:T(8,128)(2,1)S(1)}, bf16[128,1536]{1,0:T(8,128)(2,1)S(1)}, u32[]{:S(2)}, u32[]{:S(2)}) %collective-permute-start.84) | collective-permute-done | bytes 393248 | tf_op jit(solution)/shard_map/ppermute | solution.py:26
  (358 shorter events, 129.6 us)
Async XLA Ops:
  14.7 19.8 %collective-permute-start.21 = (bf16[384,768]{1,0:T(8,128)(2,1)S(1)}, bf16[384,768]{1,0:T(8,128)(2,1)S(1)}, u32[]{:S(2)}, u32[]{:S(2)}) collective-permute-start(bf16[384,768]{1,0:T(8,128)(2,1)S(1)} %dynamic-slice_bitcast_fusion.1), channel_id=1, source_target_pairs={{0,16},{1,17},{2,18},{3,19},{4,20},{5,21},{6,22},{7,23},{8,24},{9,... | collective-permute-start | bytes 1769480 | tf_op jit(solution)/shard_map/ppermute | solution.py:26
  26.9 26.4 %collective-permute-start.31 = (bf16[768,384]{1,0:T(8,128)(2,1)S(1)}, bf16[768,384]{1,0:T(8,128)(2,1)}, u32[]{:S(2)}, u32[]{:S(2)}) collective-permute-start(bf16[768,384]{1,0:T(8,128)(2,1)S(1)} %dynamic-slice_bitcast_fusion), channel_id=1, source_target_pairs={{0,16},{1,17},{2,18},{3,19},{4,20},{5,21},{6,22},{7,23},{8,24},{9,... | collective-permute-start | bytes 1769480 | tf_op jit(solution)/shard_map/ppermute | solution.py:26
  26.9 18.7 %collective-permute-start.2 = (bf16[384,384]{1,0:T(8,128)(2,1)S(1)}, bf16[384,384]{1,0:T(8,128)(2,1)}, u32[]{:S(2)}, u32[]{:S(2)}) collective-permute-start(bf16[384,384]{1,0:T(8,128)(2,1)S(1)} %get-tuple-element.151), channel_id=1, source_target_pairs={{0,12},{1,13},{2,14},{3,15},{4,8},{5,9},{6,10},{7,11},{8,4},{9,5},... | collective-permute-start | bytes 884744 | tf_op jit(solution)/shard_map/ppermute | solution.py:26
  34.5 53.6 %collective-permute-start.28 = (bf16[512,768]{1,0:T(8,128)(2,1)S(1)}, bf16[512,768]{1,0:T(8,128)(2,1)}, u32[]{:S(2)}, u32[]{:S(2)}) collective-permute-start(bf16[512,768]{1,0:T(8,128)(2,1)S(1)} %pad_maximum_fusion), channel_id=1, source_target_pairs={{0,16},{1,17},{2,18},{3,19},{4,20},{5,21},{6,22},{7,23},{8,24},{9,... | collective-permute-start | bytes 2359304 | tf_op jit(solution)/shard_map/ppermute | solution.py:26
  48.2 19.6 %collective-permute-start.25 = (bf16[384,384]{1,0:T(8,128)(2,1)}, bf16[384,384]{1,0:T(8,128)(2,1)}, u32[]{:S(2)}, u32[]{:S(2)}) collective-permute-start(bf16[384,384]{1,0:T(8,128)(2,1)} %get-tuple-element.82), channel_id=1, source_target_pairs={{0,4},{1,5},{2,6},{3,7},{4,0},{5,1},{6,2},{7,3},{8,12},{9,13},{10,... | collective-permute-start | bytes 884744 | tf_op jit(solution)/shard_map/ppermute | solution.py:26
  58.7 32.0 %collective-permute-start.35 = (bf16[384,384]{1,0:T(8,128)(2,1)S(1)}, bf16[384,384]{1,0:T(8,128)(2,1)S(1)}, u32[]{:S(2)}, u32[]{:S(2)}) collective-permute-start(bf16[384,384]{1,0:T(8,128)(2,1)S(1)} %get-tuple-element.89), channel_id=1, source_target_pairs={{0,4},{1,5},{2,6},{3,7},{4,0},{5,1},{6,2},{7,3},{8,12},{9,13},{10,... | collective-permute-start | bytes 884744 | tf_op jit(solution)/shard_map/ppermute | solution.py:26
  67.8 20.2 %collective-permute-start.23 = (bf16[384,384]{1,0:T(8,128)(2,1)}, bf16[384,384]{1,0:T(8,128)(2,1)S(1)}, u32[]{:S(2)}, u32[]{:S(2)}) collective-permute-start(bf16[384,384]{1,0:T(8,128)(2,1)} %collective-permute-done.20.refs_13_), channel_id=1, source_target_pairs={{0,2},{1,3},{2,0},{3,1},{4,6},{5,7},{6,4},{7,5},{8,10},{9,11},{10,... | collective-permute-start | bytes 884744 | tf_op jit(solution)/shard_map/ppermute | solution.py:26
  74.3 20.1 %collective-permute-start.30 = (bf16[384,384]{1,0:T(8,128)(2,1)S(1)}, bf16[384,384]{1,0:T(8,128)(2,1)S(1)}, u32[]{:S(2)}, u32[]{:S(2)}) collective-permute-start(bf16[384,384]{1,0:T(8,128)(2,1)S(1)} %get-tuple-element.79.refs_0_), channel_id=1, source_target_pairs={{0,8},{1,9},{2,10},{3,11},{4,12},{5,13},{6,14},{7,15},{8,0},{9,1},... | collective-permute-start | bytes 884744 | tf_op jit(solution)/shard_map/ppermute | solution.py:26
  90.8 23.8 %collective-permute-start.7 = (bf16[128,1536]{1,0:T(8,128)(2,1)S(1)}, bf16[128,1536]{1,0:T(8,128)(2,1)S(1)}, u32[]{:S(2)}, u32[]{:S(2)}) collective-permute-start(bf16[128,1536]{1,0:T(8,128)(2,1)S(1)} %get-tuple-element.68.refs_0_), channel_id=1, source_target_pairs={{0,4},{1,5},{2,6},{3,7},{4,0},{5,1},{6,2},{7,3},{8,12},{9,13},{10,... | collective-permute-start | bytes 1179656 | tf_op jit(solution)/shard_map/ppermute | solution.py:26
  94.4 21.8 %collective-permute-start.34 = (bf16[384,384]{1,0:T(8,128)(2,1)}, bf16[384,384]{1,0:T(8,128)(2,1)S(1)}, u32[]{:S(2)}, u32[]{:S(2)}) collective-permute-start(bf16[384,384]{1,0:T(8,128)(2,1)} %get-tuple-element.82), channel_id=1, source_target_pairs={{0,12},{1,13},{2,14},{3,15},{4,8},{5,9},{6,10},{7,11},{8,4},{9,5},... | collective-permute-start | bytes 884744 | tf_op jit(solution)/shard_map/ppermute | solution.py:26
  94.4 21.8 %collective-permute-start.36 = (bf16[384,384]{1,0:T(8,128)(2,1)S(1)}, bf16[384,384]{1,0:T(8,128)(2,1)S(1)}, u32[]{:S(2)}, u32[]{:S(2)}) collective-permute-start(bf16[384,384]{1,0:T(8,128)(2,1)S(1)} %collective-permute-done.35.refs_10_), channel_id=1, source_target_pairs={{0,2},{1,3},{2,0},{3,1},{4,6},{5,7},{6,4},{7,5},{8,10},{9,11},{10,... | collective-permute-start | bytes 884744 | tf_op jit(solution)/shard_map/ppermute | solution.py:26
  97.5 22.2 %collective-permute-start.33 = (bf16[384,384]{1,0:T(8,128)(2,1)S(1)}, bf16[384,384]{1,0:T(8,128)(2,1)S(1)}, u32[]{:S(2)}, u32[]{:S(2)}) collective-permute-start(bf16[384,384]{1,0:T(8,128)(2,1)S(1)} %collective-permute-done.30.refs_4_), channel_id=1, source_target_pairs={{0,2},{1,3},{2,0},{3,1},{4,6},{5,7},{6,4},{7,5},{8,10},{9,11},{10,... | collective-permute-start | bytes 884744 | tf_op jit(solution)/shard_map/ppermute | solution.py:26
  119.8 18.9 %collective-permute-start.38 = (bf16[384,384]{1,0:T(8,128)(2,1)S(1)}, bf16[384,384]{1,0:T(8,128)(2,1)S(1)}, u32[]{:S(2)}, u32[]{:S(2)}) collective-permute-start(bf16[384,384]{1,0:T(8,128)(2,1)S(1)} %get-tuple-element.86.refs_8_), channel_id=1, source_target_pairs={{0,8},{1,9},{2,10},{3,11},{4,12},{5,13},{6,14},{7,15},{8,0},{9,1},... | collective-permute-start | bytes 884744 | tf_op jit(solution)/shard_map/ppermute | solution.py:26
  121.8 26.1 %collective-permute-start.8 = (bf16[128,1536]{1,0:T(8,128)(2,1)S(1)}, bf16[128,1536]{1,0:T(8,128)(2,1)S(1)}, u32[]{:S(2)}, u32[]{:S(2)}) collective-permute-start(bf16[128,1536]{1,0:T(8,128)(2,1)S(1)} %collective-permute-done.7.refs_4_), channel_id=1, source_target_pairs={{0,16},{1,17},{2,18},{3,19},{4,20},{5,21},{6,22},{7,23},{8,24},{9,... | collective-permute-start | bytes 1179656 | tf_op jit(solution)/shard_map/ppermute | solution.py:26
  123.0 23.4 %collective-permute-start.6 = (bf16[128,1536]{1,0:T(8,128)(2,1)S(1)}, bf16[128,1536]{1,0:T(8,128)(2,1)S(1)}, u32[]{:S(2)}, u32[]{:S(2)}) collective-permute-start(bf16[128,1536]{1,0:T(8,128)(2,1)S(1)} %collective-permute-done.5.refs_2_), channel_id=1, source_target_pairs={{0,16},{1,17},{2,18},{3,19},{4,20},{5,21},{6,22},{7,23},{8,24},{9,... | collective-permute-start | bytes 1179656 | tf_op jit(solution)/shard_map/ppermute | solution.py:26
  145.5 33.9 %collective-permute-start.45 = (bf16[384,384]{1,0:T(8,128)(2,1)S(1)}, bf16[384,384]{1,0:T(8,128)(2,1)S(1)}, u32[]{:S(2)}, u32[]{:S(2)}) collective-permute-start(bf16[384,384]{1,0:T(8,128)(2,1)S(1)} %copy-done.14), channel_id=1, source_target_pairs={{0,8},{1,9},{2,10},{3,11},{4,12},{5,13},{6,14},{7,15},{8,0},{9,1},... | collective-permute-start | bytes 884744 | tf_op jit(solution)/shard_map/ppermute | solution.py:26
  146.4 33.0 %collective-permute-start.46 = (bf16[384,384]{1,0:T(8,128)(2,1)S(1)}, bf16[384,384]{1,0:T(8,128)(2,1)S(1)}, u32[]{:S(2)}, u32[]{:S(2)}) collective-permute-start(bf16[384,384]{1,0:T(8,128)(2,1)S(1)} %copy-done.36), channel_id=1, source_target_pairs={{0,12},{1,13},{2,14},{3,15},{4,8},{5,9},{6,10},{7,11},{8,4},{9,5},... | collective-permute-start | bytes 884744 | tf_op jit(solution)/shard_map/ppermute | solution.py:26
  146.5 22.2 %collective-permute-start.40 = (bf16[384,384]{1,0:T(8,128)(2,1)S(1)}, bf16[384,384]{1,0:T(8,128)(2,1)S(1)}, u32[]{:S(2)}, u32[]{:S(2)}) collective-permute-start(bf16[384,384]{1,0:T(8,128)(2,1)S(1)} %collective-permute-done.38.refs_12_), channel_id=1, source_target_pairs={{0,2},{1,3},{2,0},{3,1},{4,6},{5,7},{6,4},{7,5},{8,10},{9,11},{10,... | collective-permute-start | bytes 884744 | tf_op jit(solution)/shard_map/ppermute | solution.py:26
  147.9 20.8 %collective-permute-start.44 = (bf16[384,384]{1,0:T(8,128)(2,1)S(1)}, bf16[384,384]{1,0:T(8,128)(2,1)S(1)}, u32[]{:S(2)}, u32[]{:S(2)}) collective-permute-start(bf16[384,384]{1,0:T(8,128)(2,1)S(1)} %collective-permute-done.41.refs_14_), channel_id=1, source_target_pairs={{0,2},{1,3},{2,0},{3,1},{4,6},{5,7},{6,4},{7,5},{8,10},{9,11},{10,... | collective-permute-start | bytes 884744 | tf_op jit(solution)/shard_map/ppermute | solution.py:26
  185.8 22.8 %collective-permute-start.50 = (bf16[128,1536]{1,0:T(8,128)(2,1)S(1)}, bf16[128,1536]{1,0:T(8,128)(2,1)S(1)}, u32[]{:S(2)}, u32[]{:S(2)}) collective-permute-start(bf16[128,1536]{1,0:T(8,128)(2,1)S(1)} %get-tuple-element.136), channel_id=1, source_target_pairs={{0,1},{1,0},{2,3},{3,2},{4,5},{5,4},{6,7},{7,6},{8,9},{9,8},{10,11... | collective-permute-start | bytes 1179656 | tf_op jit(solution)/shard_map/ppermute | solution.py:26
  208.1 24.0 %collective-permute-start.49 = (bf16[128,1536]{1,0:T(8,128)(2,1)}, bf16[128,1536]{1,0:T(8,128)(2,1)}, u32[]{:S(2)}, u32[]{:S(2)}) collective-permute-start(bf16[128,1536]{1,0:T(8,128)(2,1)} %get-tuple-element.99), channel_id=1, source_target_pairs={{0,1},{1,0},{2,3},{3,2},{4,5},{5,4},{6,7},{7,6},{8,9},{9,8},{10,11... | collective-permute-start | bytes 1179656 | tf_op jit(solution)/shard_map/ppermute | solution.py:26
  209.5 24.0 %collective-permute-start.51 = (bf16[128,1536]{1,0:T(8,128)(2,1)}, bf16[128,1536]{1,0:T(8,128)(2,1)}, u32[]{:S(2)}, u32[]{:S(2)}) collective-permute-start(bf16[128,1536]{1,0:T(8,128)(2,1)} %fusion.6), channel_id=1, source_target_pairs={{0,4},{1,5},{2,6},{3,7},{4,0},{5,1},{6,2},{7,3},{8,12},{9,13},{10,... | collective-permute-start | bytes 1179656 | tf_op jit(solution)/shard_map/ppermute | solution.py:26
  227.6 18.8 %collective-permute-start.71 = (bf16[384,384]{1,0:T(8,128)(2,1)}, bf16[384,384]{1,0:T(8,128)(2,1)S(1)}, u32[]{:S(2)}, u32[]{:S(2)}) collective-permute-start(bf16[384,384]{1,0:T(8,128)(2,1)} %get-tuple-element.113.refs_0_), channel_id=1, source_target_pairs={{0,8},{1,9},{2,10},{3,11},{4,12},{5,13},{6,14},{7,15},{8,0},{9,1},... | collective-permute-start | bytes 884744 | tf_op jit(solution)/shard_map/ppermute | solution.py:26
  227.6 25.7 %collective-permute-start.74 = (bf16[384,384]{1,0:T(8,128)(2,1)}, bf16[384,384]{1,0:T(8,128)(2,1)S(1)}, u32[]{:S(2)}, u32[]{:S(2)}) collective-permute-start(bf16[384,384]{1,0:T(8,128)(2,1)} %get-tuple-element.117), channel_id=1, source_target_pairs={{0,12},{1,13},{2,14},{3,15},{4,8},{5,9},{6,10},{7,11},{8,4},{9,5},... | collective-permute-start | bytes 884744 | tf_op jit(solution)/shard_map/ppermute | solution.py:26
  230.5 21.1 %collective-permute-start.75 = (bf16[384,384]{1,0:T(8,128)(2,1)}, bf16[384,384]{1,0:T(8,128)(2,1)S(1)}, u32[]{:S(2)}, u32[]{:S(2)}) collective-permute-start(bf16[384,384]{1,0:T(8,128)(2,1)} %get-tuple-element.123), channel_id=1, source_target_pairs={{0,4},{1,5},{2,6},{3,7},{4,0},{5,1},{6,2},{7,3},{8,12},{9,13},{10,... | collective-permute-start | bytes 884744 | tf_op jit(solution)/shard_map/ppermute | solution.py:26
  232.0 20.6 %collective-permute-start.69 = (bf16[384,384]{1,0:T(8,128)(2,1)}, bf16[384,384]{1,0:T(8,128)(2,1)S(1)}, u32[]{:S(2)}, u32[]{:S(2)}) collective-permute-start(bf16[384,384]{1,0:T(8,128)(2,1)} %collective-permute-done.55.refs_15_), channel_id=1, source_target_pairs={{0,2},{1,3},{2,0},{3,1},{4,6},{5,7},{6,4},{7,5},{8,10},{9,11},{10,... | collective-permute-start | bytes 884744 | tf_op jit(solution)/shard_map/ppermute | solution.py:26
  233.5 20.5 %collective-permute-start.72 = (bf16[384,384]{1,0:T(8,128)(2,1)}, bf16[384,384]{1,0:T(8,128)(2,1)S(1)}, u32[]{:S(2)}, u32[]{:S(2)}) collective-permute-start(bf16[384,384]{1,0:T(8,128)(2,1)} %get-tuple-element.121.refs_8_), channel_id=1, source_target_pairs={{0,2},{1,3},{2,0},{3,1},{4,6},{5,7},{6,4},{7,5},{8,10},{9,11},{10,... | collective-permute-start | bytes 884744 | tf_op jit(solution)/shard_map/ppermute | solution.py:26
  251.6 24.4 %collective-permute-start.53 = (bf16[128,1536]{1,0:T(8,128)(2,1)S(1)}, bf16[128,1536]{1,0:T(8,128)(2,1)S(1)}, u32[]{:S(2)}, u32[]{:S(2)}) collective-permute-start(bf16[128,1536]{1,0:T(8,128)(2,1)S(1)} %fusion.11.refs_0_), channel_id=1, source_target_pairs={{0,1},{1,0},{2,3},{3,2},{4,5},{5,4},{6,7},{7,6},{8,9},{9,8},{10,11... | collective-permute-start | bytes 1179656 | tf_op jit(solution)/shard_map/ppermute | solution.py:26
  253.3 22.2 %collective-permute-start.78 = (bf16[384,384]{1,0:T(8,128)(2,1)S(1)}, bf16[384,384]{1,0:T(8,128)(2,1)S(1)}, u32[]{:S(2)}, u32[]{:S(2)}) collective-permute-start(bf16[384,384]{1,0:T(8,128)(2,1)S(1)} %copy-done.10), channel_id=1, source_target_pairs={{0,8},{1,9},{2,10},{3,11},{4,12},{5,13},{6,14},{7,15},{8,0},{9,1},... | collective-permute-start | bytes 884744 | tf_op jit(solution)/shard_map/ppermute | solution.py:26
  254.1 21.8 %collective-permute-start.80 = (bf16[384,384]{1,0:T(8,128)(2,1)S(1)}, bf16[384,384]{1,0:T(8,128)(2,1)S(1)}, u32[]{:S(2)}, u32[]{:S(2)}) collective-permute-start(bf16[384,384]{1,0:T(8,128)(2,1)S(1)} %copy-done.35), channel_id=1, source_target_pairs={{0,12},{1,13},{2,14},{3,15},{4,8},{5,9},{6,10},{7,11},{8,4},{9,5},... | collective-permute-start | bytes 884744 | tf_op jit(solution)/shard_map/ppermute | solution.py:26
  282.3 21.5 %collective-permute-start.79 = (bf16[384,384]{1,0:T(8,128)(2,1)S(1)}, bf16[384,384]{1,0:T(8,128)(2,1)S(1)}, u32[]{:S(2)}, u32[]{:S(2)}) collective-permute-start(bf16[384,384]{1,0:T(8,128)(2,1)S(1)} %collective-permute-done.78.refs_12_), channel_id=1, source_target_pairs={{0,2},{1,3},{2,0},{3,1},{4,6},{5,7},{6,4},{7,5},{8,10},{9,11},{10,... | collective-permute-start | bytes 884744 | tf_op jit(solution)/shard_map/ppermute | solution.py:26
  282.7 21.1 %collective-permute-start.81 = (bf16[384,384]{1,0:T(8,128)(2,1)S(1)}, bf16[384,384]{1,0:T(8,128)(2,1)S(1)}, u32[]{:S(2)}, u32[]{:S(2)}) collective-permute-start(bf16[384,384]{1,0:T(8,128)(2,1)S(1)} %collective-permute-done.80.refs_14_), channel_id=1, source_target_pairs={{0,2},{1,3},{2,0},{3,1},{4,6},{5,7},{6,4},{7,5},{8,10},{9,11},{10,... | collective-permute-start | bytes 884744 | tf_op jit(solution)/shard_map/ppermute | solution.py:26
  (142 other events, 2361.2 us)

commit v3 on v2

--- a/solution.py
+++ b/solution.py
@@ -97,37 +97,50 @@
     return copies
 
 
-def modulate(plan, wc, mod_ref, xv, xm):
+def modulate_kernel(plan, wc, mod_ref, *refs):
+    n_x = len(refs) - 5
+    x_refs, (xm, xv, stats, one_plus, sem) = refs[:n_x], refs[n_x:]
     slots, slot_len, cols = plan
-    feat, tile = cols * wc, 16
+    feat, tile, lane = cols * wc, 16, 128
+    copies = load_x(plan, x_refs, xv, sem)
+    one_plus[...] = 1.0 + mod_ref[:, 1:2, :]
+    for copy in copies:
+        copy.wait()
+
+    def add_up(step, carry):
+        rows = pl.ds(pl.multiple_of(step * tile, tile), tile)
+        total = jnp.zeros((tile, lane), jnp.float32)
+        squares = jnp.zeros((tile, lane), jnp.float32)
+        for col in range(cols):
+            for first in range(0, wc, lane):
+                part = xv[col, rows, first : first + lane].astype(jnp.float32)
+                total += part
+                squares += part * part
+        stats[0, rows, :] = total
+        stats[1, rows, :] = squares
+        return carry
+
+    steps = slots * slot_len // tile
+    lax.fori_loop(0, steps, add_up, 0, unroll=4)
+    mean = jnp.sum(stats[0], axis=-1, keepdims=True) / feat
+    var = jnp.sum(stats[1], axis=-1, keepdims=True) / feat - mean * mean
+    shape = (slots * slot_len, lane)
+    stats[0] = jnp.broadcast_to(mean, shape)
+    stats[1] = jnp.broadcast_to(lax.rsqrt(var + 1e-06), shape)
     for slot in range(slots):
 
-        def some_rows(step, carry, slot=slot):
+        def write(step, carry, slot=slot):
             rows = pl.ds(pl.multiple_of(slot * slot_len + step * tile, tile), tile)
-            parts = [xv[col, rows, :].astype(jnp.float32) for col in range(cols)]
-            total = sum(jnp.sum(part, axis=-1, keepdims=True) for part in parts)
-            squares = sum(jnp.sum(part * part, axis=-1, keepdims=True) for part in parts)
-            mean = total / feat
-            var = squares / feat - mean * mean
-            inverse = lax.rsqrt(var + 1e-06)
+            mean, inverse = stats[0, rows, :], stats[1, rows, :]
             for col in range(cols):
-                span = pl.ds(col * wc, wc)
-                part = xv[col, rows, :].astype(jnp.float32)
-                shift = mod_ref[slot, 0:1, span]
-                scale = mod_ref[slot, 1:2, span]
-                part = (part - mean) * inverse * (1.0 + scale) + shift
-                xm[rows, span] = part.astype(jnp.bfloat16)
+                for first in range(0, wc, lane):
+                    span = slice(col * wc + first, col * wc + first + lane)
+                    part = xv[col, rows, first : first + lane].astype(jnp.float32)
+                    part = (part - mean) * inverse * one_plus[slot, :, span]
+                    xm[rows, span] = (part + mod_ref[slot, 0:1, span]).astype(jnp.bfloat16)
             return carry
 
-        lax.fori_loop(0, slot_len // tile, some_rows, 0, unroll=2)
-
-
-def modulate_kernel(plan, wc, mod_ref, *refs):
-    n_x = len(refs) - 3
-    x_refs, (xm, xv, sem) = refs[:n_x], refs[n_x:]
-    for copy in load_x(plan, x_refs, xv, sem):
-        copy.wait()
-    modulate(plan, wc, mod_ref, xv, xm)
+        lax.fori_loop(0, slot_len // tile, write, 0, unroll=2)
 
 
 def scores_kernel(plan, ends_ref, *refs):
@@ -135,7 +148,7 @@
     x_ref, refs = refs[0], refs[1:]
     w_refs, refs = (refs[:n_w], refs[n_w : 2 * n_w]), refs[2 * n_w :]
     kv_refs, refs = refs[:slots], refs[slots:]
-    weights_ref, xm, wv, raw_ref, kvv, x_sem, w_sem, kv_sem = refs
+    weights_ref, xm, wv, raw_ref, queries, kvv, x_sem, w_sem, kv_sem = refs
     x_copies = [pltpu.make_async_copy(x_ref, xm, x_sem.at[0])]
     x_copies[0].start()
     copies = load_rows(w_refs[0], wv.at[0], w_sem, 0, kr)
@@ -155,15 +168,22 @@
 
     for t in range(2):
         raw_ref[t] = jnp.dot(xm[...], wv[t], preferred_element_type=jnp.float32)
+    for head in range(bw // HD):
+        lanes = slice(head * HD, (head + 1) * HD)
+        queries[:, lanes] = normed(raw_ref[0, :, lanes])
+        keys = normed(raw_ref[1, :, lanes])
+        for slot in range(slots):
+            kvv[slot, 0:slot_len, lanes] = keys[slot * slot_len : (slot + 1) * slot_len]
     for slot in range(slots):
         rows = pl.ds(slot * slot_len, slot_len)
         fresh, valid = fresh_and_valid(ends_ref, slot, slot_len)
         for head in range(bw // HD):
             lanes = slice(head * HD, (head + 1) * HD)
-            query = normed(raw_ref[0, rows, lanes])
-            kvv[slot, 0:slot_len, lanes] = normed(raw_ref[1, rows, lanes])
             both = lax.dot_general(
-                query, kvv[slot, :, lanes], contract, preferred_element_type=jnp.float32
+                queries[rows, lanes],
+                kvv[slot, :, lanes],
+                contract,
+                preferred_element_type=jnp.float32,
             )
             scores = jnp.where(fresh, both[:, :slot_len], both[:, slot_len:])
             weights = jnp.where(valid, jnp.exp(scores * (1.0 / math.sqrt(HD))), 0.0)
@@ -240,7 +260,7 @@
     "V0.6": ("K0.6",),
     "O0.4": ("V0.4",),
     "O0.6": ("V0.6",),
-    "Q1.4": ("O0.4", "Q0.3",),
+    "Q1.4": ("O0.4",),
     "Q1.6": ("O0.6",),
     "K1.4": ("Q1.4",),
     "K1.6": ("Q1.6",),
@@ -285,13 +305,14 @@
     "O1.5": ("V1.5",),
     "O1.7": ("V1.7",),
     "n": ("aQ",),
-    "x.0.0": ("Q0.4",),
-    "m": ("Q0.6",),
+    "m": ("Q0.6", "aV",),
     "p0": ("Q1.4", "Q1.6",),
     "r0.0.1": ("K1.4",),
     "g.2.0": ("K1.6",),
     "O1.0": ("V1.3",),
     "x.0.0c": ("aV",),
+    "v0": ("n",),
+    "V0.2": ("Q0.6",),
 }
 TREE = ("x", "r0", "g", )
 
@@ -439,6 +460,8 @@
             out_specs=vmem_spec(),
             scratch_shapes=[
                 pltpu.VMEM((cols, slots * slot_len, wc), jnp.bfloat16),
+                pltpu.VMEM((2, slots * slot_len, 128), jnp.float32),
+                pltpu.VMEM((slots, 1, feat), jnp.float32),
                 pltpu.SemaphoreType.DMA((len(pieces),)),
             ],
             compiler_params=pltpu.CompilerParams(vmem_limit_bytes=VMEM_LIMIT),
@@ -458,6 +481,7 @@
                 pltpu.VMEM((slots * slot_len, feat), jnp.bfloat16),
                 pltpu.VMEM((2, feat, bw), jnp.bfloat16),
                 pltpu.VMEM((2, slots * slot_len, bw), jnp.float32),
+                pltpu.VMEM((slots * slot_len, bw), jnp.bfloat16),
                 pltpu.VMEM((slots, 2 * slot_len, bw), jnp.bfloat16),
                 pltpu.SemaphoreType.DMA((1,)),
                 pltpu.SemaphoreType.DMA((2 * rows,)),

time: 345 us -> 337 us (0.977)
  waiting for transfers between devices: 159 us -> 142 us
  starting transfers between devices: 89 us -> 98.2 us
    ppermute x87, waiting for transfers between devices: 159 us -> 142 us  [send_to(): return lax.ppermute(array, AXES, pairs)]
    ppermute x87, starting transfers between devices: 89 us -> 98.2 us  [send_to(): return lax.ppermute(array, AXES, pairs)]
  transfers between devices with their start and end apart: 87 -> 87, of which waited for: 38 -> 37; matrix products, arithmetic and copies ran while one was open for 7% -> 7% of each run, Pallas kernels for 14% -> 14%
where the time goes in v3:
time: 337 us; the launch traced here: 336 us
  waiting for transfers between devices  142 us (42%)
  starting transfers between devices  98.2 us (29%)
  Pallas kernels  56.9 us (17%)
  other arithmetic  22.4 us (7%)
  local copies, waits for them, and re-layouts  15.2 us (5%)
    ppermute x87, waiting for transfers between devices, send_to(): return lax.ppermute(array, AXES, pairs)  142 us
    ppermute x87, starting transfers between devices, send_to(): return lax.ppermute(array, AXES, pairs)  98.2 us
    pallas_call x2, Pallas kernels, scores(): pl.pallas_call(functools.partial(scores_kernel, (slots, slot_len, rows, k...  20.1 us
    pallas_call x2, Pallas kernels, mix(): pl.pallas_call(functools.partial(mix_kernel, plan), out_shape=(shape, sha...  18.7 us
    pallas_call x2, Pallas kernels, modulated(): pl.pallas_call(functools.partial(modulate_kernel, (slots, slot_len, cols)...  14.4 us
    select_n x5, other arithmetic, block_of(): block = jnp.where(s == layer, cut(kind, s * wide + at, bw), other)  10.5 us
    unnamed x174, local copies, waits for them, and re-layouts  6.78 us
  transfers between devices with their start and end apart: 87, of which 37 were waited for; matrix products, arithmetic and copies ran while one was open for 7% of the time, Pallas kernels for 14%

profile of v3, /device:TPU:0, one launch (start us, length us, event | category | flops | bytes accessed | tf_op | source)
XLA Modules:
  0.0 336.2 jit_solution(2941120112293269183)
XLA Ops:
  19.6 7.0 %collective-permute-done.12.refs_3_ = bf16[384,384]{1,0:T(8,128)(2,1)S(1)} collective-permute-done((bf16[384,384]{1,0:T(8,128)(2,1)S(1)}, bf16[384,384]{1,0:T(8,128)(2,1)S(1)}, u32[]{:S(2)}, u32[]{:S(2)}) %collective-permute-start.12) | collective-permute-done | bytes 294944 | tf_op jit(solution)/shard_map/ppermute | solution.py:26
  26.9 3.9 %collective-permute-start.2 = (bf16[384,384]{1,0:T(8,128)(2,1)S(1)}, bf16[384,384]{1,0:T(8,128)(2,1)}, u32[]{:S(2)}, u32[]{:S(2)}) collective-permute-start(bf16[384,384]{1,0:T(8,128)(2,1)S(1)} %get-tuple-element.153), channel_id=1, source_target_pairs={{0,12},{1,13},{2,14},{3,15},{4,8},{5,9},{6,10},{7,11},{8,4},{9,5},... | collective-permute-start | bytes 884744 | tf_op jit(solution)/shard_map/ppermute | solution.py:26
  35.8 4.7 %collective-permute-done.2.refs_7_ = bf16[384,384]{1,0:T(8,128)(2,1)} collective-permute-done((bf16[384,384]{1,0:T(8,128)(2,1)S(1)}, bf16[384,384]{1,0:T(8,128)(2,1)}, u32[]{:S(2)}, u32[]{:S(2)}) %collective-permute-start.2) | collective-permute-done | bytes 294944 | tf_op jit(solution)/shard_map/ppermute | solution.py:26
  40.5 4.6 %collective-permute-start.21 = (bf16[384,384]{1,0:T(8,128)(2,1)}, bf16[384,384]{1,0:T(8,128)(2,1)}, u32[]{:S(2)}, u32[]{:S(2)}) collective-permute-start(bf16[384,384]{1,0:T(8,128)(2,1)} %get-tuple-element.73.refs_9_), channel_id=1, source_target_pairs={{0,8},{1,9},{2,10},{3,11},{4,12},{5,13},{6,14},{7,15},{8,0},{9,1},... | collective-permute-start | bytes 884744 | tf_op jit(solution)/shard_map/ppermute | solution.py:26
  52.3 5.0 %collective-permute-done.21.refs_13_ = bf16[384,384]{1,0:T(8,128)(2,1)} collective-permute-done((bf16[384,384]{1,0:T(8,128)(2,1)}, bf16[384,384]{1,0:T(8,128)(2,1)}, u32[]{:S(2)}, u32[]{:S(2)}) %collective-permute-start.21) | collective-permute-done | bytes 294944 | tf_op jit(solution)/shard_map/ppermute | solution.py:26
  57.3 3.5 %collective-permute-start.24 = (bf16[384,384]{1,0:T(8,128)(2,1)}, bf16[384,384]{1,0:T(8,128)(2,1)S(1)}, u32[]{:S(2)}, u32[]{:S(2)}) collective-permute-start(bf16[384,384]{1,0:T(8,128)(2,1)} %get-tuple-element.76), channel_id=1, source_target_pairs={{0,12},{1,13},{2,14},{3,15},{4,8},{5,9},{6,10},{7,11},{8,4},{9,5},... | collective-permute-start | bytes 884744 | tf_op jit(solution)/shard_map/ppermute | solution.py:26
  65.0 4.3 %collective-permute-done.24.refs_15_ = bf16[384,384]{1,0:T(8,128)(2,1)S(1)} collective-permute-done((bf16[384,384]{1,0:T(8,128)(2,1)}, bf16[384,384]{1,0:T(8,128)(2,1)S(1)}, u32[]{:S(2)}, u32[]{:S(2)}) %collective-permute-start.24) | collective-permute-done | bytes 294944 | tf_op jit(solution)/shard_map/ppermute | solution.py:26
  69.3 3.9 %collective-permute-start.7 = (bf16[128,1536]{1,0:T(8,128)(2,1)S(1)}, bf16[128,1536]{1,0:T(8,128)(2,1)S(1)}, u32[]{:S(2)}, u32[]{:S(2)}) collective-permute-start(bf16[128,1536]{1,0:T(8,128)(2,1)S(1)} %get-tuple-element.166.refs_0_), channel_id=1, source_target_pairs={{0,4},{1,5},{2,6},{3,7},{4,0},{5,1},{6,2},{7,3},{8,12},{9,13},{10,... | collective-permute-start | bytes 1179656 | tf_op jit(solution)/shard_map/ppermute | solution.py:26
  82.3 4.0 %collective-permute-done.27.refs_16_ = bf16[384,384]{1,0:T(8,128)(2,1)S(1)} collective-permute-done((bf16[384,384]{1,0:T(8,128)(2,1)S(1)}, bf16[384,384]{1,0:T(8,128)(2,1)S(1)}, u32[]{:S(2)}, u32[]{:S(2)}) %collective-permute-start.27) | collective-permute-done | bytes 294944 | tf_op jit(solution)/shard_map/ppermute | solution.py:26
  86.3 3.5 %collective-permute-start.34 = (bf16[384,384]{1,0:T(8,128)(2,1)}, bf16[384,384]{1,0:T(8,128)(2,1)S(1)}, u32[]{:S(2)}, u32[]{:S(2)}) collective-permute-start(bf16[384,384]{1,0:T(8,128)(2,1)} %get-tuple-element.84), channel_id=1, source_target_pairs={{0,12},{1,13},{2,14},{3,15},{4,8},{5,9},{6,10},{7,11},{8,4},{9,5},... | collective-permute-start | bytes 884744 | tf_op jit(solution)/shard_map/ppermute | solution.py:26
  109.8 7.9 %collective-permute-done.42.refs_3_ = bf16[384,384]{1,0:T(8,128)(2,1)S(1)} collective-permute-done((bf16[384,384]{1,0:T(8,128)(2,1)S(1)}, bf16[384,384]{1,0:T(8,128)(2,1)S(1)}, u32[]{:S(2)}, u32[]{:S(2)}) %collective-permute-start.42) | collective-permute-done | bytes 294944 | tf_op jit(solution)/shard_map/ppermute | solution.py:26
  120.9 3.7 %modulation.1 = f32[2,3,3072]{2,1,0:T(4,128)} custom-call(bf16[8,256]{1,0:T(8,128)(2,1)} %fusion.21.feats_ref, bf16[3,256,3072]{2,1,0:T(8,128)(2,1)} %bitcast.107), custom_call_target="tpu_custom_call" | custom-call | tf_op jit(solution)/shard_map/modulation/pallas_call | solution.py:421
  124.7 4.3 %collective-permute-done.41.refs_14_ = bf16[384,384]{1,0:T(8,128)(2,1)S(1)} collective-permute-done((bf16[384,384]{1,0:T(8,128)(2,1)S(1)}, bf16[384,384]{1,0:T(8,128)(2,1)S(1)}, u32[]{:S(2)}, u32[]{:S(2)}) %collective-permute-start.41) | collective-permute-done | bytes 294944 | tf_op jit(solution)/shard_map/ppermute | solution.py:26
  129.6 3.9 %collective-permute-done.43.refs_4_ = bf16[384,384]{1,0:T(8,128)(2,1)S(1)} collective-permute-done((bf16[384,384]{1,0:T(8,128)(2,1)S(1)}, bf16[384,384]{1,0:T(8,128)(2,1)S(1)}, u32[]{:S(2)}, u32[]{:S(2)}) %collective-permute-start.43) | collective-permute-done | bytes 294944 | tf_op jit(solution)/shard_map/ppermute | solution.py:26
  133.6 3.8 %collective-permute-start.45 = (bf16[384,384]{1,0:T(8,128)(2,1)S(1)}, bf16[384,384]{1,0:T(8,128)(2,1)S(1)}, u32[]{:S(2)}, u32[]{:S(2)}) collective-permute-start(bf16[384,384]{1,0:T(8,128)(2,1)S(1)} %copy-done.14), channel_id=1, source_target_pairs={{0,8},{1,9},{2,10},{3,11},{4,12},{5,13},{6,14},{7,15},{8,0},{9,1},... | collective-permute-start | bytes 884744 | tf_op jit(solution)/shard_map/ppermute | solution.py:26
  144.2 7.1 %modulate.2.refs_0_.x_ref = bf16[512,3072]{1,0:T(8,128)(2,1)} custom-call(f32[2,3,3072]{2,1,0:T(4,128)} %get-tuple-element.168.mod_ref, bf16[128,1536]{1,0:T(8,128)(2,1)} %copy-done.2, bf16[128,1536]{1,0:T(8,128)(2,1)} %get-tuple-element.165.refs_1_, bf16[128,1536]{1,0:T(8,128)(2,1)} %copy-done.22, bf16[128,1536]{1,0:T(8,128)(2,1)} %copy-done.27, ...), custom_call_target="tpu_custom_call" | custom-call | tf_op jit(solution)/shard_map/modulate/pallas_call | solution.py:456
  151.3 10.1 %scores.2.weights_ref = bf16[2,3,256,512]{3,2,1,0:T(8,128)(2,1)} custom-call(s32[2,4]{1,0:T(2,128)} %bitcast.115, bf16[512,3072]{1,0:T(8,128)(2,1)} %modulate.2.refs_0_.x_ref, bf16[384,384]{1,0:T(8,128)(2,1)} %copy-done.16, bf16[384,384]{1,0:T(8,128)(2,1)} %copy-done.65, bf16[384,384]{1,0:T(8,128)(2,1)} %copy-done.66, bf16[384,384]{1,0:T(8,128)(2,1)} %copy-done.72, ...), custom_call_target="tpu_custom_call" | custom-call | tf_op jit(solution)/shard_map/scores/pallas_call | solution.py:472
  162.9 9.3 %mix.2 = (bf16[2,128,3072]{2,1,0:T(8,128)(2,1)}, bf16[2,128,3072]{2,1,0:T(8,128)(2,1)}) custom-call(bf16[512,3072]{1,0:T(8,128)(2,1)} %modulate.2.refs_0_.x_ref, bf16[2,3,256,512]{3,2,1,0:T(8,128)(2,1)} %scores.2.weights_ref, bf16[384,384]{1,0:T(8,128)(2,1)} %copy-done.11, bf16[384,384]{1,0:T(8,128)(2,1)} %copy-done.37, ...), custom_call_target="tpu_custom_call" | custom-call | tf_op jit(solution)/shard_map/mix/pallas_call | solution.py:503
  186.3 5.7 %collective-permute-done.63.refs_12_ = bf16[384,384]{1,0:T(8,128)(2,1)S(1)} collective-permute-done((bf16[384,384]{1,0:T(8,128)(2,1)S(1)}, bf16[384,384]{1,0:T(8,128)(2,1)S(1)}, u32[]{:S(2)}, u32[]{:S(2)}) %collective-permute-start.63) | collective-permute-done | bytes 294944 | tf_op jit(solution)/shard_map/ppermute | solution.py:26
  192.5 5.8 %collective-permute-done.61.refs_6_ = bf16[384,384]{1,0:T(8,128)(2,1)S(1)} collective-permute-done((bf16[384,384]{1,0:T(8,128)(2,1)S(1)}, bf16[384,384]{1,0:T(8,128)(2,1)S(1)}, u32[]{:S(2)}, u32[]{:S(2)}) %collective-permute-start.61) | collective-permute-done | bytes 294944 | tf_op jit(solution)/shard_map/ppermute | solution.py:26
  206.1 4.8 %collective-permute-done.65.refs_1_ = bf16[384,384]{1,0:T(8,128)(2,1)S(1)} collective-permute-done((bf16[384,384]{1,0:T(8,128)(2,1)S(1)}, bf16[384,384]{1,0:T(8,128)(2,1)S(1)}, u32[]{:S(2)}, u32[]{:S(2)}) %collective-permute-start.65) | collective-permute-done | bytes 294944 | tf_op jit(solution)/shard_map/ppermute | solution.py:26
  214.4 4.0 %collective-permute-done.55.refs_15_ = bf16[384,384]{1,0:T(8,128)(2,1)} collective-permute-done((bf16[384,384]{1,0:T(8,128)(2,1)}, bf16[384,384]{1,0:T(8,128)(2,1)}, u32[]{:S(2)}, u32[]{:S(2)}) %collective-permute-start.55) | collective-permute-done | bytes 294944 | tf_op jit(solution)/shard_map/ppermute | solution.py:26
  226.3 14.3 %collective-permute-done.71.refs_4_ = bf16[384,384]{1,0:T(8,128)(2,1)S(1)} collective-permute-done((bf16[384,384]{1,0:T(8,128)(2,1)}, bf16[384,384]{1,0:T(8,128)(2,1)S(1)}, u32[]{:S(2)}, u32[]{:S(2)}) %collective-permute-start.71) | collective-permute-done | bytes 294944 | tf_op jit(solution)/shard_map/ppermute | solution.py:26
  248.1 4.5 %collective-permute-done.56.refs_4_ = bf16[128,1536]{1,0:T(8,128)(2,1)S(1)} collective-permute-done((bf16[128,1536]{1,0:T(8,128)(2,1)S(1)}, bf16[128,1536]{1,0:T(8,128)(2,1)S(1)}, u32[]{:S(2)}, u32[]{:S(2)}) %collective-permute-start.56) | collective-permute-done | bytes 393248 | tf_op jit(solution)/shard_map/ppermute | solution.py:26
  255.4 12.0 %collective-permute-done.78.refs_12_ = bf16[384,384]{1,0:T(8,128)(2,1)S(1)} collective-permute-done((bf16[384,384]{1,0:T(8,128)(2,1)S(1)}, bf16[384,384]{1,0:T(8,128)(2,1)S(1)}, u32[]{:S(2)}, u32[]{:S(2)}) %collective-permute-start.78) | collective-permute-done | bytes 294944 | tf_op jit(solution)/shard_map/ppermute | solution.py:26
  270.2 3.9 %collective-permute-done.77.refs_7_ = bf16[384,384]{1,0:T(8,128)(2,1)S(1)} collective-permute-done((bf16[384,384]{1,0:T(8,128)(2,1)S(1)}, bf16[384,384]{1,0:T(8,128)(2,1)S(1)}, u32[]{:S(2)}, u32[]{:S(2)}) %collective-permute-start.77) | collective-permute-done | bytes 294944 | tf_op jit(solution)/shard_map/ppermute | solution.py:26
  277.1 7.3 %modulate.3.refs_0_.x_ref = bf16[512,3072]{1,0:T(8,128)(2,1)} custom-call(f32[2,3,3072]{2,1,0:T(4,128)} %get-tuple-element.167.mod_ref, bf16[128,1536]{1,0:T(8,128)(2,1)} %copy-done, bf16[128,1536]{1,0:T(8,128)(2,1)} %copy-done.6, bf16[128,1536]{1,0:T(8,128)(2,1)} %copy-done.25, bf16[128,1536]{1,0:T(8,128)(2,1)} %copy-done.29, bf16[128,1536]{1,0:T(8,128)(2,1)} %copy-done.24, ...), custom_call_target="tpu_custom_call" | custom-call | tf_op jit(solution)/shard_map/modulate/pallas_call | solution.py:456
  285.2 10.0 %scores.3.weights_ref = bf16[2,3,256,512]{3,2,1,0:T(8,128)(2,1)} custom-call(s32[2,4]{1,0:T(2,128)} %bitcast.116, bf16[512,3072]{1,0:T(8,128)(2,1)} %modulate.3.refs_0_.x_ref, bf16[384,384]{1,0:T(8,128)(2,1)} %get-tuple-element.97.refs_1_, bf16[384,384]{1,0:T(8,128)(2,1)} %copy-done.63, bf16[384,384]{1,0:T(8,128)(2,1)} %copy-done.62, ...), custom_call_target="tpu_custom_call" | custom-call | tf_op jit(solution)/shard_map/scores/pallas_call | solution.py:472
  296.8 9.3 %mix.3 = (bf16[2,128,3072]{2,1,0:T(8,128)(2,1)}, bf16[2,128,3072]{2,1,0:T(8,128)(2,1)}) custom-call(bf16[512,3072]{1,0:T(8,128)(2,1)} %modulate.3.refs_0_.x_ref, bf16[2,3,256,512]{3,2,1,0:T(8,128)(2,1)} %scores.3.weights_ref, bf16[384,384]{1,0:T(8,128)(2,1)} %get-tuple-element.115.refs_0_, bf16[384,384]{1,0:T(8,128)(2,1)} %copy-done.40, ...), custom_call_target="tpu_custom_call" | custom-call | tf_op jit(solution)/shard_map/mix/pallas_call | solution.py:503
  306.2 3.6 %collective-permute-done.82 = bf16[2,128,3072]{2,1,0:T(8,128)(2,1)S(1)} collective-permute-done((bf16[2,128,3072]{2,1,0:T(8,128)(2,1)}, bf16[2,128,3072]{2,1,0:T(8,128)(2,1)S(1)}, u32[]{:S(2)}, u32[]{:S(2)}) %collective-permute-start.82) | collective-permute-done | bytes 1572896 | tf_op jit(solution)/shard_map/ppermute | solution.py:26
  315.8 8.6 %collective-permute-done.85 = bf16[128,1536]{1,0:T(8,128)(2,1)S(1)} collective-permute-done((bf16[128,1536]{1,0:T(8,128)(2,1)S(1)}, bf16[128,1536]{1,0:T(8,128)(2,1)S(1)}, u32[]{:S(2)}, u32[]{:S(2)}) %collective-permute-start.85) | collective-permute-done | bytes 393248 | tf_op jit(solution)/shard_map/ppermute | solution.py:26
  324.4 6.9 %collective-permute-done.84 = bf16[128,1536]{1,0:T(8,128)(2,1)S(1)} collective-permute-done((bf16[128,1536]{1,0:T(8,128)(2,1)S(1)}, bf16[128,1536]{1,0:T(8,128)(2,1)S(1)}, u32[]{:S(2)}, u32[]{:S(2)}) %collective-permute-start.84) | collective-permute-done | bytes 393248 | tf_op jit(solution)/shard_map/ppermute | solution.py:26
  (358 shorter events, 139.3 us)
Async XLA Ops:
  14.7 19.8 %collective-permute-start.3 = (bf16[384,768]{1,0:T(8,128)(2,1)S(1)}, bf16[384,768]{1,0:T(8,128)(2,1)S(1)}, u32[]{:S(2)}, u32[]{:S(2)}) collective-permute-start(bf16[384,768]{1,0:T(8,128)(2,1)S(1)} %dynamic-slice_bitcast_fusion.2), channel_id=1, source_target_pairs={{0,16},{1,17},{2,18},{3,19},{4,20},{5,21},{6,22},{7,23},{8,24},{9,... | collective-permute-start | bytes 1769480 | tf_op jit(solution)/shard_map/ppermute | solution.py:26
  26.9 21.5 %collective-permute-start.31 = (bf16[768,384]{1,0:T(8,128)(2,1)S(1)}, bf16[768,384]{1,0:T(8,128)(2,1)}, u32[]{:S(2)}, u32[]{:S(2)}) collective-permute-start(bf16[768,384]{1,0:T(8,128)(2,1)S(1)} %dynamic-slice_bitcast_fusion), channel_id=1, source_target_pairs={{0,16},{1,17},{2,18},{3,19},{4,20},{5,21},{6,22},{7,23},{8,24},{9,... | collective-permute-start | bytes 1769480 | tf_op jit(solution)/shard_map/ppermute | solution.py:26
  34.5 42.1 %collective-permute-start.28 = (bf16[512,768]{1,0:T(8,128)(2,1)S(1)}, bf16[512,768]{1,0:T(8,128)(2,1)}, u32[]{:S(2)}, u32[]{:S(2)}) collective-permute-start(bf16[512,768]{1,0:T(8,128)(2,1)S(1)} %pad_maximum_fusion), channel_id=1, source_target_pairs={{0,16},{1,17},{2,18},{3,19},{4,20},{5,21},{6,22},{7,23},{8,24},{9,... | collective-permute-start | bytes 2359304 | tf_op jit(solution)/shard_map/ppermute | solution.py:26
  40.5 16.7 %collective-permute-start.21 = (bf16[384,384]{1,0:T(8,128)(2,1)}, bf16[384,384]{1,0:T(8,128)(2,1)}, u32[]{:S(2)}, u32[]{:S(2)}) collective-permute-start(bf16[384,384]{1,0:T(8,128)(2,1)} %get-tuple-element.73.refs_9_), channel_id=1, source_target_pairs={{0,8},{1,9},{2,10},{3,11},{4,12},{5,13},{6,14},{7,15},{8,0},{9,1},... | collective-permute-start | bytes 884744 | tf_op jit(solution)/shard_map/ppermute | solution.py:26
  60.8 20.2 %collective-permute-start.35 = (bf16[384,384]{1,0:T(8,128)(2,1)S(1)}, bf16[384,384]{1,0:T(8,128)(2,1)S(1)}, u32[]{:S(2)}, u32[]{:S(2)}) collective-permute-start(bf16[384,384]{1,0:T(8,128)(2,1)S(1)} %get-tuple-element.91), channel_id=1, source_target_pairs={{0,4},{1,5},{2,6},{3,7},{4,0},{5,1},{6,2},{7,3},{8,12},{9,13},{10,... | collective-permute-start | bytes 884744 | tf_op jit(solution)/shard_map/ppermute | solution.py:26
  69.3 25.4 %collective-permute-start.7 = (bf16[128,1536]{1,0:T(8,128)(2,1)S(1)}, bf16[128,1536]{1,0:T(8,128)(2,1)S(1)}, u32[]{:S(2)}, u32[]{:S(2)}) collective-permute-start(bf16[128,1536]{1,0:T(8,128)(2,1)S(1)} %get-tuple-element.166.refs_0_), channel_id=1, source_target_pairs={{0,4},{1,5},{2,6},{3,7},{4,0},{5,1},{6,2},{7,3},{8,12},{9,13},{10,... | collective-permute-start | bytes 1179656 | tf_op jit(solution)/shard_map/ppermute | solution.py:26
  76.6 16.6 %collective-permute-start.32 = (bf16[384,384]{1,0:T(8,128)(2,1)S(1)}, bf16[384,384]{1,0:T(8,128)(2,1)S(1)}, u32[]{:S(2)}, u32[]{:S(2)}) collective-permute-start(bf16[384,384]{1,0:T(8,128)(2,1)S(1)} %get-tuple-element.88.refs_8_), channel_id=1, source_target_pairs={{0,2},{1,3},{2,0},{3,1},{4,6},{5,7},{6,4},{7,5},{8,10},{9,11},{10,... | collective-permute-start | bytes 884744 | tf_op jit(solution)/shard_map/ppermute | solution.py:26
  81.0 18.1 %collective-permute-start.29 = (bf16[2,256,384]{2,1,0:T(8,128)(2,1)S(1)}, bf16[2,256,384]{2,1,0:T(8,128)(2,1)S(1)}, u32[]{:S(2)}, u32[]{:S(2)}) collective-permute-start(bf16[2,256,384]{2,1,0:T(8,128)(2,1)S(1)} %bitcast.114), channel_id=1, source_target_pairs={{0,4},{1,5},{2,6},{3,7},{4,0},{5,1},{6,2},{7,3},{8,12},{9,13},{10,... | collective-permute-start | bytes 1179656 | tf_op jit(solution)/shard_map/ppermute | solution.py:26
  86.3 17.6 %collective-permute-start.34 = (bf16[384,384]{1,0:T(8,128)(2,1)}, bf16[384,384]{1,0:T(8,128)(2,1)S(1)}, u32[]{:S(2)}, u32[]{:S(2)}) collective-permute-start(bf16[384,384]{1,0:T(8,128)(2,1)} %get-tuple-element.84), channel_id=1, source_target_pairs={{0,12},{1,13},{2,14},{3,15},{4,8},{5,9},{6,10},{7,11},{8,4},{9,5},... | collective-permute-start | bytes 884744 | tf_op jit(solution)/shard_map/ppermute | solution.py:26
  99.1 19.0 %collective-permute-start.9 = (bf16[128,1536]{1,0:T(8,128)(2,1)S(1)}, bf16[128,1536]{1,0:T(8,128)(2,1)S(1)}, u32[]{:S(2)}, u32[]{:S(2)}) collective-permute-start(bf16[128,1536]{1,0:T(8,128)(2,1)S(1)} %collective-permute-done.7.refs_4_), channel_id=1, source_target_pairs={{0,1},{1,0},{2,3},{3,2},{4,5},{5,4},{6,7},{7,6},{8,9},{9,8},{10,11... | collective-permute-start | bytes 1179656 | tf_op jit(solution)/shard_map/ppermute | solution.py:26
  109.8 29.9 %collective-permute-start.8 = (bf16[128,1536]{1,0:T(8,128)(2,1)S(1)}, bf16[128,1536]{1,0:T(8,128)(2,1)S(1)}, u32[]{:S(2)}, u32[]{:S(2)}) collective-permute-start(bf16[128,1536]{1,0:T(8,128)(2,1)S(1)} %collective-permute-done.7.refs_4_), channel_id=1, source_target_pairs={{0,16},{1,17},{2,18},{3,19},{4,20},{5,21},{6,22},{7,23},{8,24},{9,... | collective-permute-start | bytes 1179656 | tf_op jit(solution)/shard_map/ppermute | solution.py:26
  117.7 19.6 %collective-permute-start.6 = (bf16[128,1536]{1,0:T(8,128)(2,1)S(1)}, bf16[128,1536]{1,0:T(8,128)(2,1)S(1)}, u32[]{:S(2)}, u32[]{:S(2)}) collective-permute-start(bf16[128,1536]{1,0:T(8,128)(2,1)S(1)} %collective-permute-done.5.refs_2_), channel_id=1, source_target_pairs={{0,16},{1,17},{2,18},{3,19},{4,20},{5,21},{6,22},{7,23},{8,24},{9,... | collective-permute-start | bytes 1179656 | tf_op jit(solution)/shard_map/ppermute | solution.py:26
  133.6 38.7 %collective-permute-start.45 = (bf16[384,384]{1,0:T(8,128)(2,1)S(1)}, bf16[384,384]{1,0:T(8,128)(2,1)S(1)}, u32[]{:S(2)}, u32[]{:S(2)}) collective-permute-start(bf16[384,384]{1,0:T(8,128)(2,1)S(1)} %copy-done.14), channel_id=1, source_target_pairs={{0,8},{1,9},{2,10},{3,11},{4,12},{5,13},{6,14},{7,15},{8,0},{9,1},... | collective-permute-start | bytes 884744 | tf_op jit(solution)/shard_map/ppermute | solution.py:26
  137.3 34.9 %collective-permute-start.46 = (bf16[384,384]{1,0:T(8,128)(2,1)S(1)}, bf16[384,384]{1,0:T(8,128)(2,1)S(1)}, u32[]{:S(2)}, u32[]{:S(2)}) collective-permute-start(bf16[384,384]{1,0:T(8,128)(2,1)S(1)} %copy-done.36), channel_id=1, source_target_pairs={{0,12},{1,13},{2,14},{3,15},{4,8},{5,9},{6,10},{7,11},{8,4},{9,5},... | collective-permute-start | bytes 884744 | tf_op jit(solution)/shard_map/ppermute | solution.py:26
  139.7 21.8 %collective-permute-start.40 = (bf16[384,384]{1,0:T(8,128)(2,1)S(1)}, bf16[384,384]{1,0:T(8,128)(2,1)S(1)}, u32[]{:S(2)}, u32[]{:S(2)}) collective-permute-start(bf16[384,384]{1,0:T(8,128)(2,1)S(1)} %collective-permute-done.38.refs_12_), channel_id=1, source_target_pairs={{0,2},{1,3},{2,0},{3,1},{4,6},{5,7},{6,4},{7,5},{8,10},{9,11},{10,... | collective-permute-start | bytes 884744 | tf_op jit(solution)/shard_map/ppermute | solution.py:26
  140.3 21.2 %collective-permute-start.44 = (bf16[384,384]{1,0:T(8,128)(2,1)S(1)}, bf16[384,384]{1,0:T(8,128)(2,1)S(1)}, u32[]{:S(2)}, u32[]{:S(2)}) collective-permute-start(bf16[384,384]{1,0:T(8,128)(2,1)S(1)} %collective-permute-done.41.refs_14_), channel_id=1, source_target_pairs={{0,2},{1,3},{2,0},{3,1},{4,6},{5,7},{6,4},{7,5},{8,10},{9,11},{10,... | collective-permute-start | bytes 884744 | tf_op jit(solution)/shard_map/ppermute | solution.py:26
  178.1 22.8 %collective-permute-start.50 = (bf16[128,1536]{1,0:T(8,128)(2,1)S(1)}, bf16[128,1536]{1,0:T(8,128)(2,1)S(1)}, u32[]{:S(2)}, u32[]{:S(2)}) collective-permute-start(bf16[128,1536]{1,0:T(8,128)(2,1)S(1)} %get-tuple-element.138), channel_id=1, source_target_pairs={{0,1},{1,0},{2,3},{3,2},{4,5},{5,4},{6,7},{7,6},{8,9},{9,8},{10,11... | collective-permute-start | bytes 1179656 | tf_op jit(solution)/shard_map/ppermute | solution.py:26
  199.4 23.4 %collective-permute-start.49 = (bf16[128,1536]{1,0:T(8,128)(2,1)}, bf16[128,1536]{1,0:T(8,128)(2,1)}, u32[]{:S(2)}, u32[]{:S(2)}) collective-permute-start(bf16[128,1536]{1,0:T(8,128)(2,1)} %get-tuple-element.101), channel_id=1, source_target_pairs={{0,1},{1,0},{2,3},{3,2},{4,5},{5,4},{6,7},{7,6},{8,9},{9,8},{10,11... | collective-permute-start | bytes 1179656 | tf_op jit(solution)/shard_map/ppermute | solution.py:26
  201.8 21.5 %collective-permute-start.51 = (bf16[128,1536]{1,0:T(8,128)(2,1)}, bf16[128,1536]{1,0:T(8,128)(2,1)}, u32[]{:S(2)}, u32[]{:S(2)}) collective-permute-start(bf16[128,1536]{1,0:T(8,128)(2,1)} %fusion.6), channel_id=1, source_target_pairs={{0,4},{1,5},{2,6},{3,7},{4,0},{5,1},{6,2},{7,3},{8,12},{9,13},{10,... | collective-permute-start | bytes 1179656 | tf_op jit(solution)/shard_map/ppermute | solution.py:26
  218.3 22.2 %collective-permute-start.71 = (bf16[384,384]{1,0:T(8,128)(2,1)}, bf16[384,384]{1,0:T(8,128)(2,1)S(1)}, u32[]{:S(2)}, u32[]{:S(2)}) collective-permute-start(bf16[384,384]{1,0:T(8,128)(2,1)} %get-tuple-element.115.refs_0_), channel_id=1, source_target_pairs={{0,8},{1,9},{2,10},{3,11},{4,12},{5,13},{6,14},{7,15},{8,0},{9,1},... | collective-permute-start | bytes 884744 | tf_op jit(solution)/shard_map/ppermute | solution.py:26
  218.3 26.7 %collective-permute-start.74 = (bf16[384,384]{1,0:T(8,128)(2,1)}, bf16[384,384]{1,0:T(8,128)(2,1)S(1)}, u32[]{:S(2)}, u32[]{:S(2)}) collective-permute-start(bf16[384,384]{1,0:T(8,128)(2,1)} %get-tuple-element.119), channel_id=1, source_target_pairs={{0,12},{1,13},{2,14},{3,15},{4,8},{5,9},{6,10},{7,11},{8,4},{9,5},... | collective-permute-start | bytes 884744 | tf_op jit(solution)/shard_map/ppermute | solution.py:26
  222.3 19.7 %collective-permute-start.75 = (bf16[384,384]{1,0:T(8,128)(2,1)}, bf16[384,384]{1,0:T(8,128)(2,1)S(1)}, u32[]{:S(2)}, u32[]{:S(2)}) collective-permute-start(bf16[384,384]{1,0:T(8,128)(2,1)} %get-tuple-element.125), channel_id=1, source_target_pairs={{0,4},{1,5},{2,6},{3,7},{4,0},{5,1},{6,2},{7,3},{8,12},{9,13},{10,... | collective-permute-start | bytes 884744 | tf_op jit(solution)/shard_map/ppermute | solution.py:26
  222.8 21.6 %collective-permute-start.69 = (bf16[384,384]{1,0:T(8,128)(2,1)}, bf16[384,384]{1,0:T(8,128)(2,1)S(1)}, u32[]{:S(2)}, u32[]{:S(2)}) collective-permute-start(bf16[384,384]{1,0:T(8,128)(2,1)} %collective-permute-done.55.refs_15_), channel_id=1, source_target_pairs={{0,2},{1,3},{2,0},{3,1},{4,6},{5,7},{6,4},{7,5},{8,10},{9,11},{10,... | collective-permute-start | bytes 884744 | tf_op jit(solution)/shard_map/ppermute | solution.py:26
  223.3 22.2 %collective-permute-start.72 = (bf16[384,384]{1,0:T(8,128)(2,1)}, bf16[384,384]{1,0:T(8,128)(2,1)S(1)}, u32[]{:S(2)}, u32[]{:S(2)}) collective-permute-start(bf16[384,384]{1,0:T(8,128)(2,1)} %get-tuple-element.123.refs_8_), channel_id=1, source_target_pairs={{0,2},{1,3},{2,0},{3,1},{4,6},{5,7},{6,4},{7,5},{8,10},{9,11},{10,... | collective-permute-start | bytes 884744 | tf_op jit(solution)/shard_map/ppermute | solution.py:26
  242.0 27.3 %collective-permute-start.53 = (bf16[128,1536]{1,0:T(8,128)(2,1)S(1)}, bf16[128,1536]{1,0:T(8,128)(2,1)S(1)}, u32[]{:S(2)}, u32[]{:S(2)}) collective-permute-start(bf16[128,1536]{1,0:T(8,128)(2,1)S(1)} %fusion.11.refs_0_), channel_id=1, source_target_pairs={{0,1},{1,0},{2,3},{3,2},{4,5},{5,4},{6,7},{7,6},{8,9},{9,8},{10,11... | collective-permute-start | bytes 1179656 | tf_op jit(solution)/shard_map/ppermute | solution.py:26
  245.1 22.3 %collective-permute-start.78 = (bf16[384,384]{1,0:T(8,128)(2,1)S(1)}, bf16[384,384]{1,0:T(8,128)(2,1)S(1)}, u32[]{:S(2)}, u32[]{:S(2)}) collective-permute-start(bf16[384,384]{1,0:T(8,128)(2,1)S(1)} %copy-done.10), channel_id=1, source_target_pairs={{0,8},{1,9},{2,10},{3,11},{4,12},{5,13},{6,14},{7,15},{8,0},{9,1},... | collective-permute-start | bytes 884744 | tf_op jit(solution)/shard_map/ppermute | solution.py:26
  245.6 23.6 %collective-permute-start.80 = (bf16[384,384]{1,0:T(8,128)(2,1)S(1)}, bf16[384,384]{1,0:T(8,128)(2,1)S(1)}, u32[]{:S(2)}, u32[]{:S(2)}) collective-permute-start(bf16[384,384]{1,0:T(8,128)(2,1)S(1)} %copy-done.35), channel_id=1, source_target_pairs={{0,12},{1,13},{2,14},{3,15},{4,8},{5,9},{6,10},{7,11},{8,4},{9,5},... | collective-permute-start | bytes 884744 | tf_op jit(solution)/shard_map/ppermute | solution.py:26
  252.6 17.2 %collective-permute-start.58 = (bf16[128,1536]{1,0:T(8,128)(2,1)S(1)}, bf16[128,1536]{1,0:T(8,128)(2,1)S(1)}, u32[]{:S(2)}, u32[]{:S(2)}) collective-permute-start(bf16[128,1536]{1,0:T(8,128)(2,1)S(1)} %collective-permute-done.56.refs_4_), channel_id=1, source_target_pairs={{0,1},{1,0},{2,3},{3,2},{4,5},{5,4},{6,7},{7,6},{8,9},{9,8},{10,11... | collective-permute-start | bytes 1179656 | tf_op jit(solution)/shard_map/ppermute | solution.py:26
  274.2 21.2 %collective-permute-start.79 = (bf16[384,384]{1,0:T(8,128)(2,1)S(1)}, bf16[384,384]{1,0:T(8,128)(2,1)S(1)}, u32[]{:S(2)}, u32[]{:S(2)}) collective-permute-start(bf16[384,384]{1,0:T(8,128)(2,1)S(1)} %collective-permute-done.78.refs_12_), channel_id=1, source_target_pairs={{0,2},{1,3},{2,0},{3,1},{4,6},{5,7},{6,4},{7,5},{8,10},{9,11},{10,... | collective-permute-start | bytes 884744 | tf_op jit(solution)/shard_map/ppermute | solution.py:26
  276.0 19.4 %collective-permute-start.81 = (bf16[384,384]{1,0:T(8,128)(2,1)S(1)}, bf16[384,384]{1,0:T(8,128)(2,1)S(1)}, u32[]{:S(2)}, u32[]{:S(2)}) collective-permute-start(bf16[384,384]{1,0:T(8,128)(2,1)S(1)} %collective-permute-done.80.refs_14_), channel_id=1, source_target_pairs={{0,2},{1,3},{2,0},{3,1},{4,6},{5,7},{6,4},{7,5},{8,10},{9,11},{10,... | collective-permute-start | bytes 884744 | tf_op jit(solution)/shard_map/ppermute | solution.py:26
  313.5 17.8 %collective-permute-start.84 = (bf16[128,1536]{1,0:T(8,128)(2,1)S(1)}, bf16[128,1536]{1,0:T(8,128)(2,1)S(1)}, u32[]{:S(2)}, u32[]{:S(2)}) collective-permute-start(bf16[128,1536]{1,0:T(8,128)(2,1)S(1)} %get-tuple-element.136), channel_id=1, source_target_pairs={{0,4},{1,5},{2,6},{3,7},{4,0},{5,1},{6,2},{7,3},{8,12},{9,13},{10,... | collective-permute-start | bytes 1179656 | tf_op jit(solution)/shard_map/ppermute | solution.py:26
  313.6 18.3 %collective-permute-start.83 = (bf16[128,1536]{1,0:T(8,128)(2,1)S(1)}, bf16[128,1536]{1,0:T(8,128)(2,1)S(1)}, u32[]{:S(2)}, u32[]{:S(2)}) collective-permute-start(bf16[128,1536]{1,0:T(8,128)(2,1)S(1)} %get-tuple-element.134), channel_id=1, source_target_pairs={{0,1},{1,0},{2,3},{3,2},{4,5},{5,4},{6,7},{7,6},{8,9},{9,8},{10,11... | collective-permute-start | bytes 1179656 | tf_op jit(solution)/shard_map/ppermute | solution.py:26
  (142 other events, 2196.7 us)

commit v4 on v3

--- a/solution.py
+++ b/solution.py
@@ -97,15 +97,9 @@
     return copies
 
 
-def modulate_kernel(plan, wc, mod_ref, *refs):
-    n_x = len(refs) - 5
-    x_refs, (xm, xv, stats, one_plus, sem) = refs[:n_x], refs[n_x:]
+def modulate(plan, wc, mod_ref, xv, stats, one_plus, xm):
     slots, slot_len, cols = plan
     feat, tile, lane = cols * wc, 16, 128
-    copies = load_x(plan, x_refs, xv, sem)
-    one_plus[...] = 1.0 + mod_ref[:, 1:2, :]
-    for copy in copies:
-        copy.wait()
 
     def add_up(step, carry):
         rows = pl.ds(pl.multiple_of(step * tile, tile), tile)
@@ -143,107 +137,93 @@
         lax.fori_loop(0, slot_len // tile, write, 0, unroll=2)
 
 
-def scores_kernel(plan, ends_ref, *refs):
-    slots, slot_len, n_w, kr, bw = plan
-    x_ref, refs = refs[0], refs[1:]
-    w_refs, refs = (refs[:n_w], refs[n_w : 2 * n_w]), refs[2 * n_w :]
+def layer_kernel(plan, ends_ref, mod_ref, *refs):
+    slots, slot_len, cols, n_x, n_w, kr, nr, bw, wc = plan
+    x_refs, refs = refs[:n_x], refs[n_x:]
+    w_refs, refs = [refs[t * n_w : (t + 1) * n_w] for t in range(4)], refs[4 * n_w :]
     kv_refs, refs = refs[:slots], refs[slots:]
-    weights_ref, xm, wv, raw_ref, queries, kvv, x_sem, w_sem, kv_sem = refs
-    x_copies = [pltpu.make_async_copy(x_ref, xm, x_sem.at[0])]
-    x_copies[0].start()
-    copies = load_rows(w_refs[0], wv.at[0], w_sem, 0, kr)
-    copies += load_rows(w_refs[1], wv.at[1], w_sem, n_w, kr)
+    keep_ref, pass_ref, xv, stats, one_plus, xm, wv, ov, raw, queries, keys, values, att, out = refs[:14]
+    x_sem, w_sem, kv_sem, out_sem = refs[14:]
+    s, c = lax.axis_index("section"), lax.axis_index("col")
+    half, lanes_of = slot_len // 2, [slice(h * HD, (h + 1) * HD) for h in range(bw // HD)]
+    x_copies = load_x((slots, slot_len, cols), x_refs, xv, x_sem)
+    copies = [load_rows(w_refs[t], wv.at[t], w_sem, t * n_w, kr) for t in range(2)]
+    kv_copies = []
     for slot in range(slots):
-        one = kv_refs[slot].at[0]
-        target = kvv.at[slot, pl.ds(slot_len, slot_len), :]
-        copies.append(pltpu.make_async_copy(one, target, kv_sem.at[slot]))
-        copies[-1].start()
-    for copy in x_copies + copies:
+        for t, target in enumerate((keys, values)):
+            place = target.at[slot, pl.ds(slot_len, slot_len), :]
+            kv_copies.append(
+                pltpu.make_async_copy(kv_refs[slot].at[t], place, kv_sem.at[2 * slot + t])
+            )
+            kv_copies[-1].start()
+    copies.append(load_rows(w_refs[2], wv.at[2], w_sem, 2 * n_w, kr))
+    copies.append(load_rows(w_refs[3], ov, w_sem, 3 * n_w, None))
+    one_plus[...] = 1.0 + mod_ref[:, 1:2, :]
+    for copy in x_copies:
         copy.wait()
-    contract = (((1,), (1,)), ((), ()))
+    modulate((slots, slot_len, cols), wc, mod_ref, xv, stats, one_plus, xm)
+    for t in range(2):
+        for copy in copies[t]:
+            copy.wait()
+        raw[t] = jnp.dot(xm[...], wv[t], preferred_element_type=jnp.float32)
+    for copy in kv_copies + copies[2]:
+        copy.wait()
 
     def normed(block):
         mean = jnp.mean(block * block, axis=-1, keepdims=True)
         return (block * lax.rsqrt(mean + 1e-06)).astype(jnp.bfloat16)
 
-    for t in range(2):
-        raw_ref[t] = jnp.dot(xm[...], wv[t], preferred_element_type=jnp.float32)
-    for head in range(bw // HD):
-        lanes = slice(head * HD, (head + 1) * HD)
-        queries[:, lanes] = normed(raw_ref[0, :, lanes])
-        keys = normed(raw_ref[1, :, lanes])
+    for lanes in lanes_of:
+        queries[:, lanes] = normed(raw[0, :, lanes])
+        fresh_keys = normed(raw[1, :, lanes])
         for slot in range(slots):
-            kvv[slot, 0:slot_len, lanes] = keys[slot * slot_len : (slot + 1) * slot_len]
+            keys[slot, 0:slot_len, lanes] = fresh_keys[slot * slot_len : (slot + 1) * slot_len]
+    fresh_values = jnp.dot(xm[...], wv[2], preferred_element_type=jnp.float32).astype(jnp.bfloat16)
+    for slot in range(slots):
+        values[slot, 0:slot_len, :] = fresh_values[slot * slot_len : (slot + 1) * slot_len]
+    contract = (((1,), (1,)), ((), ()))
     for slot in range(slots):
         rows = pl.ds(slot * slot_len, slot_len)
         fresh, valid = fresh_and_valid(ends_ref, slot, slot_len)
-        for head in range(bw // HD):
-            lanes = slice(head * HD, (head + 1) * HD)
+        for lanes in lanes_of:
             both = lax.dot_general(
                 queries[rows, lanes],
-                kvv[slot, :, lanes],
+                keys[slot, :, lanes],
                 contract,
                 preferred_element_type=jnp.float32,
             )
             scores = jnp.where(fresh, both[:, :slot_len], both[:, slot_len:])
             weights = jnp.where(valid, jnp.exp(scores * (1.0 / math.sqrt(HD))), 0.0)
             weights = weights * (1.0 / jnp.sum(weights, axis=-1, keepdims=True))
-            weights_ref[slot, head, :, 0:slot_len] = jnp.where(fresh, weights, 0.0).astype(
-                jnp.bfloat16
+            both = jnp.concatenate(
+                [
+                    jnp.where(fresh, weights, 0.0).astype(jnp.bfloat16),
+                    jnp.where(fresh, 0.0, weights).astype(jnp.bfloat16),
+                ],
+                axis=1,
             )
-            weights_ref[slot, head, :, slot_len:] = jnp.where(fresh, 0.0, weights).astype(
-                jnp.bfloat16
-            )
-
-
-def mix_kernel(plan, x_ref, weights_ref, *refs):
-    slots, slot_len, cols, n_w, kr, nr, bw, wc = plan
-    v_refs, o_refs, refs = refs[:n_w], refs[n_w : 2 * n_w], refs[2 * n_w :]
-    kv_refs, refs = refs[:slots], refs[slots:]
-    keep_ref, pass_ref, xm, pv, wv, ov, kvv, att, x_sem, w_sem, kv_sem = refs
-    s, c = lax.axis_index("section"), lax.axis_index("col")
-    half = slot_len // 2
-    x_copy = pltpu.make_async_copy(x_ref, xm, x_sem.at[0])
-    x_copy.start()
-    copies = load_rows(v_refs, wv, w_sem, 0, kr)
-    p_copy = pltpu.make_async_copy(weights_ref, pv, x_sem.at[1])
-    p_copy.start()
-    late = [p_copy]
-    for slot in range(slots):
-        one = kv_refs[slot].at[1]
-        target = kvv.at[slot, pl.ds(slot_len, slot_len), :]
-        late.append(pltpu.make_async_copy(one, target, kv_sem.at[slot]))
-        late[-1].start()
-    o_copies = load_rows(o_refs, ov, w_sem, n_w, None)
-    for copy in [x_copy] + copies:
+            mixed = jnp.dot(both, values[slot, :, lanes], preferred_element_type=jnp.float32)
+            att[rows, lanes] = mixed.astype(jnp.bfloat16)
+    for copy in copies[3]:
         copy.wait()
-    raw = jnp.dot(xm[...], wv[...], preferred_element_type=jnp.float32).astype(jnp.bfloat16)
-    for slot in range(slots):
-        kvv[slot, 0:slot_len, :] = raw[slot * slot_len : (slot + 1) * slot_len]
-    for copy in late:
-        copy.wait()
-    for slot in range(slots):
-        rows = pl.ds(slot * slot_len, slot_len)
-        for head in range(bw // HD):
-            lanes = slice(head * HD, (head + 1) * HD)
-            mixed = jnp.dot(pv[slot, head], kvv[slot, :, lanes], preferred_element_type=jnp.float32)
-            att[rows, lanes] = mixed.astype(jnp.bfloat16)
-    for copy in o_copies:
-        copy.wait()
-    blocks = []
-    for side in (1 - s, s):
+    out_copies = []
+    for k, (side, out_ref) in enumerate(((1 - s, pass_ref), (s, keep_ref))):
+        blocks = []
         for slot in range(slots):
             row = pl.multiple_of(slot * slot_len + side * half, half)
             blocks.append(att[pl.ds(row, half), :])
-    lhs = jnp.concatenate(blocks, axis=0)
-    for place in range(n_w):
-        row = lax.rem(c * (n_w // cols) + place, n_w)
-        part = jnp.dot(lhs, ov[row], preferred_element_type=jnp.float32).astype(jnp.bfloat16)
-        lanes = slice(place * nr, (place + 1) * nr)
-        for k, out_ref in enumerate((pass_ref, keep_ref)):
+        lhs = jnp.concatenate(blocks, axis=0)
+        for place in range(n_w):
+            row = lax.rem(c * (n_w // cols) + place, n_w)
+            part = jnp.dot(lhs, ov[row], preferred_element_type=jnp.float32).astype(jnp.bfloat16)
             for slot in range(slots):
-                first = (k * slots + slot) * half
-                out_ref[slot, :, lanes] = part[first : first + half]
+                out[k, slot, :, place * nr : (place + 1) * nr] = part[
+                    slot * half : (slot + 1) * half
+                ]
+        out_copies.append(pltpu.make_async_copy(out.at[k], out_ref, out_sem.at[k]))
+        out_copies[-1].start()
+    for copy in out_copies:
+        copy.wait()
 
 
 def mod_kernel(slots, feats_ref, weight_ref, out_ref):
@@ -278,7 +258,7 @@
     "K0.3": ("Q0.3",),
     "Q0.5": ("K0.1",),
     "Q0.7": ("K0.3",),
-    "V0.1": ("Q0.5",),
+    "V0.1": ("Q0.5", "O0.2",),
     "V0.3": ("Q0.7",),
     "K0.5": ("V0.1",),
     "K0.7": ("V0.3",),
@@ -304,15 +284,15 @@
     "V1.7": ("O1.3",),
     "O1.5": ("V1.5",),
     "O1.7": ("V1.7",),
-    "n": ("aQ",),
+    "n": ("aQ", "O0.2",),
     "m": ("Q0.6", "aV",),
     "p0": ("Q1.4", "Q1.6",),
     "r0.0.1": ("K1.4",),
-    "g.2.0": ("K1.6",),
     "O1.0": ("V1.3",),
     "x.0.0c": ("aV",),
-    "v0": ("n",),
     "V0.2": ("Q0.6",),
+    "v0": ("aQ",),
+    "l1": ("O1.6",),
 }
 TREE = ("x", "r0", "g", )
 
@@ -450,79 +430,42 @@
     def x_pieces(kind):
         return [get(f"{kind}.{di}.{dc}" + end) for di, dc in places for end in ("", "c")]
 
-    def modulated(layer):
+    def heads_of(layer):
         pieces = x_pieces("xg"[layer])
-        shape = (slots * slot_len, feat)
+        plan = (slots, slot_len, cols, len(pieces), rows, kr, nr, bw, wc)
+        shape = jax.ShapeDtypeStruct((slots, half, feat), jnp.bfloat16)
+        every = slots * slot_len
         return pl.pallas_call(
-            functools.partial(modulate_kernel, (slots, slot_len, cols), wc),
-            out_shape=jax.ShapeDtypeStruct(shape, jnp.bfloat16),
-            in_specs=[vmem_spec()] + [any_spec()] * len(pieces),
-            out_specs=vmem_spec(),
+            functools.partial(layer_kernel, plan),
+            out_shape=(shape, shape),
+            in_specs=[pl.BlockSpec(memory_space=pltpu.SMEM), vmem_spec()]
+            + [any_spec()] * (len(pieces) + 4 * rows + slots),
+            out_specs=(any_spec(), any_spec()),
             scratch_shapes=[
-                pltpu.VMEM((cols, slots * slot_len, wc), jnp.bfloat16),
-                pltpu.VMEM((2, slots * slot_len, 128), jnp.float32),
+                pltpu.VMEM((cols, every, wc), jnp.bfloat16),
+                pltpu.VMEM((2, every, 128), jnp.float32),
                 pltpu.VMEM((slots, 1, feat), jnp.float32),
+                pltpu.VMEM((every, feat), jnp.bfloat16),
+                pltpu.VMEM((3, feat, bw), jnp.bfloat16),
+                pltpu.VMEM((rows, bw, nr), jnp.bfloat16),
+                pltpu.VMEM((2, every, bw), jnp.float32),
+                pltpu.VMEM((every, bw), jnp.bfloat16),
+                pltpu.VMEM((slots, 2 * slot_len, bw), jnp.bfloat16),
+                pltpu.VMEM((slots, 2 * slot_len, bw), jnp.bfloat16),
+                pltpu.VMEM((every, bw), jnp.bfloat16),
+                pltpu.VMEM((2, slots, half, feat), jnp.bfloat16),
                 pltpu.SemaphoreType.DMA((len(pieces),)),
+                pltpu.SemaphoreType.DMA((4 * rows,)),
+                pltpu.SemaphoreType.DMA((2 * slots,)),
+                pltpu.SemaphoreType.DMA((2,)),
             ],
             compiler_params=pltpu.CompilerParams(vmem_limit_bytes=VMEM_LIMIT),
-            name="modulate",
-        )(gated(get("m")[layer], f"l{layer}"), *pieces)
-
-    def scores(layer):
-        return pl.pallas_call(
-            functools.partial(scores_kernel, (slots, slot_len, rows, kr, bw)),
-            out_shape=jax.ShapeDtypeStruct(
-                (slots, bw // HD, slot_len, 2 * slot_len), jnp.bfloat16
-            ),
-            in_specs=[pl.BlockSpec(memory_space=pltpu.SMEM)]
-            + [any_spec()] * (1 + 2 * rows + slots),
-            out_specs=vmem_spec(),
-            scratch_shapes=[
-                pltpu.VMEM((slots * slot_len, feat), jnp.bfloat16),
-                pltpu.VMEM((2, feat, bw), jnp.bfloat16),
-                pltpu.VMEM((2, slots * slot_len, bw), jnp.float32),
-                pltpu.VMEM((slots * slot_len, bw), jnp.bfloat16),
-                pltpu.VMEM((slots, 2 * slot_len, bw), jnp.bfloat16),
-                pltpu.SemaphoreType.DMA((1,)),
-                pltpu.SemaphoreType.DMA((2 * rows,)),
-                pltpu.SemaphoreType.DMA((slots,)),
-            ],
-            compiler_params=pltpu.CompilerParams(vmem_limit_bytes=VMEM_LIMIT),
-            name="scores",
+            name="layer",
         )(
-            gated(get("n")[:, :NP], f"k{layer}"),
-            get(f"l{layer}"),
-            *of_rows("Q", layer),
-            *of_rows("K", layer),
-            *stale_of(layer),
-        )
-
-    def mix(layer):
-        plan = (slots, slot_len, cols, rows, kr, nr, bw, wc)
-        shape = jax.ShapeDtypeStruct((slots, half, feat), jnp.bfloat16)
-        return pl.pallas_call(
-            functools.partial(mix_kernel, plan),
-            out_shape=(shape, shape),
-            in_specs=[any_spec()] * (2 + 2 * rows + slots),
-            out_specs=(vmem_spec(), vmem_spec()),
-            scratch_shapes=[
-                pltpu.VMEM((slots * slot_len, feat), jnp.bfloat16),
-                pltpu.VMEM((slots, bw // HD, slot_len, 2 * slot_len), jnp.bfloat16),
-                pltpu.VMEM((feat, bw), jnp.bfloat16),
-                pltpu.VMEM((rows, bw, nr), jnp.bfloat16),
-                pltpu.VMEM((slots, 2 * slot_len, bw), jnp.bfloat16),
-                pltpu.VMEM((slots * slot_len, bw), jnp.bfloat16),
-                pltpu.SemaphoreType.DMA((2,)),
-                pltpu.SemaphoreType.DMA((2 * rows,)),
-                pltpu.SemaphoreType.DMA((slots,)),
-            ],
-            compiler_params=pltpu.CompilerParams(vmem_limit_bytes=VMEM_LIMIT),
-            name="mix",
-        )(
-            get(f"l{layer}"),
-            gated(get(f"k{layer}"), f"v{layer}"),
-            *of_rows("V", layer),
-            *of_rows("O", layer),
+            gated(get("n")[:, :NP], f"v{layer}"),
+            get("m")[layer],
+            *pieces,
+            *[one for kind in "QKVO" for one in of_rows(kind, layer)],
             *stale_of(layer),
         )
 
@@ -549,9 +492,7 @@
         return send(name, get(f"u{layer}.{di}").astype(jnp.bfloat16), di, 0)
 
     for layer in range(2):
-        step(f"l{layer}")(functools.partial(modulated, layer))
-        step(f"k{layer}")(functools.partial(scores, layer))
-        step(f"v{layer}")(functools.partial(mix, layer))
+        step(f"v{layer}")(functools.partial(heads_of, layer))
         step(f"p{layer}")(lambda layer=layer: swap(f"p{layer}", get(f"v{layer}")[1]))
         step(f"t{layer}")(functools.partial(parts, layer))
         for di, dc in places:

time: 337 us -> 338 us (level)
  waiting for transfers between devices: 142 us -> 172 us
  Pallas kernels: 56.9 us -> 42.3 us
  starting transfers between devices: 98.2 us -> 85 us
    ppermute x87, waiting for transfers between devices: 142 us -> 172 us  [send_to(): return lax.ppermute(array, AXES, pairs)]
    pallas_call x6 -> x2, Pallas kernels: 53.2 us -> 38.6 us  [heads_of(): pl.pallas_call(functools.partial(layer_kernel, plan), out_shape=(shape, s...]
    ppermute x87, starting transfers between devices: 98.2 us -> 85 us  [send_to(): return lax.ppermute(array, AXES, pairs)]
    unnamed x174 -> x190, local copies, waits for them, and re-layouts: 6.78 us -> 4.46 us
  transfers between devices with their start and end apart: 87 -> 87, of which waited for: 37 -> 44; matrix products, arithmetic and copies ran while one was open for 7% -> 8% of each run, Pallas kernels for 14% -> 7%
where the time goes in v4:
time: 338 us
  waiting for transfers between devices  172 us (51%)
  starting transfers between devices  85 us (25%)
  Pallas kernels  42.3 us (13%)
  other arithmetic  22 us (7%)
  local copies, waits for them, and re-layouts  15 us (4%)
    ppermute x87, waiting for transfers between devices, send_to(): return lax.ppermute(array, AXES, pairs)  172 us
    ppermute x87, starting transfers between devices, send_to(): return lax.ppermute(array, AXES, pairs)  85 us
    pallas_call x2, Pallas kernels, heads_of(): pl.pallas_call(functools.partial(layer_kernel, plan), out_shape=(shape, s...  38.6 us
    select_n x5, other arithmetic, block_of(): block = jnp.where(s == layer, cut(kind, s * wide + at, bw), other)  10 us
  transfers between devices with their start and end apart: 87, of which 44 were waited for; matrix products, arithmetic and copies ran while one was open for 8% of the time, Pallas kernels for 7%

profile of v4, /device:TPU:0, one launch (start us, length us, event | category | flops | bytes accessed | tf_op | source)
XLA Modules:
  0.0 337.5 jit_solution(6609380382791414112)
XLA Ops:
  21.4 4.4 %collective-permute-done.2.refs_10_ = bf16[384,384]{1,0:T(8,128)(2,1)S(1)} collective-permute-done((bf16[384,384]{1,0:T(8,128)(2,1)S(1)}, bf16[384,384]{1,0:T(8,128)(2,1)S(1)}, u32[]{:S(2)}, u32[]{:S(2)}) %collective-permute-start.2) | collective-permute-done | bytes 294944 | tf_op jit(solution)/shard_map/ppermute | solution.py:26
  36.8 4.7 %collective-permute-done.5.refs_14_ = bf16[384,384]{1,0:T(8,128)(2,1)} collective-permute-done((bf16[384,384]{1,0:T(8,128)(2,1)S(1)}, bf16[384,384]{1,0:T(8,128)(2,1)}, u32[]{:S(2)}, u32[]{:S(2)}) %collective-permute-start.5) | collective-permute-done | bytes 294944 | tf_op jit(solution)/shard_map/ppermute | solution.py:26
  44.3 4.1 %collective-permute-done.3.refs_34_ = bf16[384,384]{1,0:T(8,128)(2,1)S(1)} collective-permute-done((bf16[384,384]{1,0:T(8,128)(2,1)S(1)}, bf16[384,384]{1,0:T(8,128)(2,1)S(1)}, u32[]{:S(2)}, u32[]{:S(2)}) %collective-permute-start.3) | collective-permute-done | bytes 294944 | tf_op jit(solution)/shard_map/ppermute | solution.py:26
  51.3 7.2 %collective-permute-done.23.refs_20_ = bf16[384,384]{1,0:T(8,128)(2,1)S(1)} collective-permute-done((bf16[384,384]{1,0:T(8,128)(2,1)S(1)}, bf16[384,384]{1,0:T(8,128)(2,1)S(1)}, u32[]{:S(2)}, u32[]{:S(2)}) %collective-permute-start.23) | collective-permute-done | bytes 294944 | tf_op jit(solution)/shard_map/ppermute | solution.py:26
  58.5 3.5 %collective-permute-start.26 = (bf16[384,384]{1,0:T(8,128)(2,1)}, bf16[384,384]{1,0:T(8,128)(2,1)S(1)}, u32[]{:S(2)}, u32[]{:S(2)}) collective-permute-start(bf16[384,384]{1,0:T(8,128)(2,1)} %copy-done.78), channel_id=1, source_target_pairs={{0,12},{1,13},{2,14},{3,15},{4,8},{5,9},{6,10},{7,11},{8,4},{9,5},... | collective-permute-start | bytes 884744 | tf_op jit(solution)/shard_map/ppermute | solution.py:26
  67.5 2.9 collective-permute-done.26.refs_22_
  70.4 4.0 %collective-permute-start.30 = (bf16[384,384]{1,0:T(8,128)(2,1)S(1)}, bf16[384,384]{1,0:T(8,128)(2,1)S(1)}, u32[]{:S(2)}, u32[]{:S(2)}) collective-permute-start(bf16[384,384]{1,0:T(8,128)(2,1)S(1)} %get-tuple-element.81.refs_24_), channel_id=1, source_target_pairs={{0,8},{1,9},{2,10},{3,11},{4,12},{5,13},{6,14},{7,15},{8,0},{9,1},... | collective-permute-start | bytes 884744 | tf_op jit(solution)/shard_map/ppermute | solution.py:26
  81.7 5.1 %collective-permute-done.29.refs_23_ = bf16[384,384]{1,0:T(8,128)(2,1)S(1)} collective-permute-done((bf16[384,384]{1,0:T(8,128)(2,1)S(1)}, bf16[384,384]{1,0:T(8,128)(2,1)S(1)}, u32[]{:S(2)}, u32[]{:S(2)}) %collective-permute-start.29) | collective-permute-done | bytes 294944 | tf_op jit(solution)/shard_map/ppermute | solution.py:26
  88.6 4.3 %collective-permute-done.31.refs_33_ = bf16[384,384]{1,0:T(8,128)(2,1)S(1)} collective-permute-done((bf16[384,384]{1,0:T(8,128)(2,1)S(1)}, bf16[384,384]{1,0:T(8,128)(2,1)S(1)}, u32[]{:S(2)}, u32[]{:S(2)}) %collective-permute-start.31) | collective-permute-done | bytes 294944 | tf_op jit(solution)/shard_map/ppermute | solution.py:26
  95.8 4.7 %collective-permute-done.41.refs_41_ = bf16[2,256,384]{2,1,0:T(8,128)(2,1)S(1)} collective-permute-done((bf16[2,256,384]{2,1,0:T(8,128)(2,1)S(1)}, bf16[2,256,384]{2,1,0:T(8,128)(2,1)S(1)}, u32[]{:S(2)}, u32[]{:S(2)}) %collective-permute-start.41) | collective-permute-done | bytes 393248 | tf_op jit(solution)/shard_map/ppermute | solution.py:26
  106.6 4.5 %collective-permute-done.42.refs_10_ = bf16[384,384]{1,0:T(8,128)(2,1)S(1)} collective-permute-done((bf16[384,384]{1,0:T(8,128)(2,1)S(1)}, bf16[384,384]{1,0:T(8,128)(2,1)S(1)}, u32[]{:S(2)}, u32[]{:S(2)}) %collective-permute-start.42) | collective-permute-done | bytes 294944 | tf_op jit(solution)/shard_map/ppermute | solution.py:26
  116.8 10.0 %collective-permute-done.36.refs_36_ = bf16[384,384]{1,0:T(8,128)(2,1)S(1)} collective-permute-done((bf16[384,384]{1,0:T(8,128)(2,1)S(1)}, bf16[384,384]{1,0:T(8,128)(2,1)S(1)}, u32[]{:S(2)}, u32[]{:S(2)}) %collective-permute-start.36) | collective-permute-done | bytes 294944 | tf_op jit(solution)/shard_map/ppermute | solution.py:26
  129.2 3.7 %modulation.1 = f32[2,3,3072]{2,1,0:T(4,128)} custom-call(bf16[8,256]{1,0:T(8,128)(2,1)} %fusion.21.feats_ref, bf16[3,256,3072]{2,1,0:T(8,128)(2,1)} %bitcast.107), custom_call_target="tpu_custom_call" | custom-call | tf_op jit(solution)/shard_map/modulation/pallas_call | solution.py:401
  138.8 6.3 %collective-permute-done.38.refs_37_ = bf16[384,384]{1,0:T(8,128)(2,1)S(1)} collective-permute-done((bf16[384,384]{1,0:T(8,128)(2,1)S(1)}, bf16[384,384]{1,0:T(8,128)(2,1)S(1)}, u32[]{:S(2)}, u32[]{:S(2)}) %collective-permute-start.38) | collective-permute-done | bytes 294944 | tf_op jit(solution)/shard_map/ppermute | solution.py:26
  145.1 4.6 %collective-permute-done.44.refs_39_ = bf16[384,384]{1,0:T(8,128)(2,1)S(1)} collective-permute-done((bf16[384,384]{1,0:T(8,128)(2,1)S(1)}, bf16[384,384]{1,0:T(8,128)(2,1)S(1)}, u32[]{:S(2)}, u32[]{:S(2)}) %collective-permute-start.44) | collective-permute-done | bytes 294944 | tf_op jit(solution)/shard_map/ppermute | solution.py:26
  150.4 19.2 %layer.2 = (bf16[2,128,3072]{2,1,0:T(8,128)(2,1)}, bf16[2,128,3072]{2,1,0:T(8,128)(2,1)}) custom-call(s32[2,4]{1,0:T(2,128)} %bitcast.113, f32[2,3,3072]{2,1,0:T(4,128)} %get-tuple-element.166.mod_ref, bf16[128,1536]{1,0:T(8,128)(2,1)} %copy-done.2, bf16[128,1536]{1,0:T(8,128)(2,1)} %get-tuple-element.163.refs_1_, bf16[128,1536]{1,0:T(8,128)(2,1)} %copy-done.21, ...), custom_call_target="tpu_custom_call" | custom-call | tf_op jit(solution)/shard_map/layer/pallas_call | solution.py:438
  176.5 3.5 %collective-permute-done.61.refs_18_ = bf16[384,384]{1,0:T(8,128)(2,1)S(1)} collective-permute-done((bf16[384,384]{1,0:T(8,128)(2,1)}, bf16[384,384]{1,0:T(8,128)(2,1)S(1)}, u32[]{:S(2)}, u32[]{:S(2)}) %collective-permute-start.61) | collective-permute-done | bytes 294944 | tf_op jit(solution)/shard_map/ppermute | solution.py:26
  185.1 4.8 %collective-permute-done.62.refs_19_ = bf16[384,384]{1,0:T(8,128)(2,1)S(1)} collective-permute-done((bf16[384,384]{1,0:T(8,128)(2,1)S(1)}, bf16[384,384]{1,0:T(8,128)(2,1)S(1)}, u32[]{:S(2)}, u32[]{:S(2)}) %collective-permute-start.62) | collective-permute-done | bytes 294944 | tf_op jit(solution)/shard_map/ppermute | solution.py:26
  190.6 5.6 %collective-permute-done.60.refs_13_ = bf16[384,384]{1,0:T(8,128)(2,1)S(1)} collective-permute-done((bf16[384,384]{1,0:T(8,128)(2,1)S(1)}, bf16[384,384]{1,0:T(8,128)(2,1)S(1)}, u32[]{:S(2)}, u32[]{:S(2)}) %collective-permute-start.60) | collective-permute-done | bytes 294944 | tf_op jit(solution)/shard_map/ppermute | solution.py:26
  203.3 5.6 %collective-permute-done.64.refs_25_ = bf16[384,384]{1,0:T(8,128)(2,1)S(1)} collective-permute-done((bf16[384,384]{1,0:T(8,128)(2,1)S(1)}, bf16[384,384]{1,0:T(8,128)(2,1)S(1)}, u32[]{:S(2)}, u32[]{:S(2)}) %collective-permute-start.64) | collective-permute-done | bytes 294944 | tf_op jit(solution)/shard_map/ppermute | solution.py:26
  212.6 4.8 %collective-permute-done.66.refs_22_ = bf16[384,384]{1,0:T(8,128)(2,1)} collective-permute-done((bf16[384,384]{1,0:T(8,128)(2,1)}, bf16[384,384]{1,0:T(8,128)(2,1)}, u32[]{:S(2)}, u32[]{:S(2)}) %collective-permute-start.66) | collective-permute-done | bytes 294944 | tf_op jit(solution)/shard_map/ppermute | solution.py:26
  225.5 14.8 %collective-permute-done.74.refs_34_ = bf16[384,384]{1,0:T(8,128)(2,1)S(1)} collective-permute-done((bf16[384,384]{1,0:T(8,128)(2,1)}, bf16[384,384]{1,0:T(8,128)(2,1)S(1)}, u32[]{:S(2)}, u32[]{:S(2)}) %collective-permute-start.74) | collective-permute-done | bytes 294944 | tf_op jit(solution)/shard_map/ppermute | solution.py:26
  244.6 5.7 %collective-permute-done.75.refs_35_ = bf16[384,384]{1,0:T(8,128)(2,1)S(1)} collective-permute-done((bf16[384,384]{1,0:T(8,128)(2,1)S(1)}, bf16[384,384]{1,0:T(8,128)(2,1)S(1)}, u32[]{:S(2)}, u32[]{:S(2)}) %collective-permute-start.75) | collective-permute-done | bytes 294944 | tf_op jit(solution)/shard_map/ppermute | solution.py:26
  251.4 7.2 %collective-permute-done.55.refs_4_ = bf16[128,1536]{1,0:T(8,128)(2,1)S(1)} collective-permute-done((bf16[128,1536]{1,0:T(8,128)(2,1)S(1)}, bf16[128,1536]{1,0:T(8,128)(2,1)S(1)}, u32[]{:S(2)}, u32[]{:S(2)}) %collective-permute-start.55) | collective-permute-done | bytes 393248 | tf_op jit(solution)/shard_map/ppermute | solution.py:26
  259.8 4.1 %collective-permute-done.77.refs_36_ = bf16[384,384]{1,0:T(8,128)(2,1)S(1)} collective-permute-done((bf16[384,384]{1,0:T(8,128)(2,1)S(1)}, bf16[384,384]{1,0:T(8,128)(2,1)S(1)}, u32[]{:S(2)}, u32[]{:S(2)}) %collective-permute-start.77) | collective-permute-done | bytes 294944 | tf_op jit(solution)/shard_map/ppermute | solution.py:26
  266.0 6.5 %collective-permute-done.79.refs_38_ = bf16[384,384]{1,0:T(8,128)(2,1)S(1)} collective-permute-done((bf16[384,384]{1,0:T(8,128)(2,1)S(1)}, bf16[384,384]{1,0:T(8,128)(2,1)S(1)}, u32[]{:S(2)}, u32[]{:S(2)}) %collective-permute-start.79) | collective-permute-done | bytes 294944 | tf_op jit(solution)/shard_map/ppermute | solution.py:26
  278.0 5.5 %collective-permute-done.80.refs_39_ = bf16[384,384]{1,0:T(8,128)(2,1)S(1)} collective-permute-done((bf16[384,384]{1,0:T(8,128)(2,1)S(1)}, bf16[384,384]{1,0:T(8,128)(2,1)S(1)}, u32[]{:S(2)}, u32[]{:S(2)}) %collective-permute-start.80) | collective-permute-done | bytes 294944 | tf_op jit(solution)/shard_map/ppermute | solution.py:26
  284.8 19.4 %layer.3 = (bf16[2,128,3072]{2,1,0:T(8,128)(2,1)}, bf16[2,128,3072]{2,1,0:T(8,128)(2,1)}) custom-call(s32[2,4]{1,0:T(2,128)} %bitcast.114, f32[2,3,3072]{2,1,0:T(4,128)} %get-tuple-element.165.mod_ref, bf16[128,1536]{1,0:T(8,128)(2,1)} %copy-done, bf16[128,1536]{1,0:T(8,128)(2,1)} %copy-done.4, bf16[128,1536]{1,0:T(8,128)(2,1)} %copy-done.27, ...), custom_call_target="tpu_custom_call" | custom-call | tf_op jit(solution)/shard_map/layer/pallas_call | solution.py:438
  304.3 3.6 %collective-permute-done.82 = bf16[2,128,3072]{2,1,0:T(8,128)(2,1)S(1)} collective-permute-done((bf16[2,128,3072]{2,1,0:T(8,128)(2,1)}, bf16[2,128,3072]{2,1,0:T(8,128)(2,1)S(1)}, u32[]{:S(2)}, u32[]{:S(2)}) %collective-permute-start.82) | collective-permute-done | bytes 1572896 | tf_op jit(solution)/shard_map/ppermute | solution.py:26
  309.6 5.9 %collective-permute-start.85 = (bf16[128,1536]{1,0:T(8,128)(2,1)S(1)}, bf16[128,1536]{1,0:T(8,128)(2,1)S(1)}, u32[]{:S(2)}, u32[]{:S(2)}) collective-permute-start(bf16[128,1536]{1,0:T(8,128)(2,1)S(1)} %get-tuple-element.133), channel_id=1, source_target_pairs={{0,5},{1,4},{2,7},{3,6},{4,1},{5,0},{6,3},{7,2},{8,13},{9,12},{10,... | collective-permute-start | bytes 1179656 | tf_op jit(solution)/shard_map/ppermute | solution.py:26
  317.2 8.2 %collective-permute-done.85 = bf16[128,1536]{1,0:T(8,128)(2,1)S(1)} collective-permute-done((bf16[128,1536]{1,0:T(8,128)(2,1)S(1)}, bf16[128,1536]{1,0:T(8,128)(2,1)S(1)}, u32[]{:S(2)}, u32[]{:S(2)}) %collective-permute-start.85) | collective-permute-done | bytes 393248 | tf_op jit(solution)/shard_map/ppermute | solution.py:26
  325.4 7.4 %collective-permute-done.84 = bf16[128,1536]{1,0:T(8,128)(2,1)S(1)} collective-permute-done((bf16[128,1536]{1,0:T(8,128)(2,1)S(1)}, bf16[128,1536]{1,0:T(8,128)(2,1)S(1)}, u32[]{:S(2)}, u32[]{:S(2)}) %collective-permute-start.84) | collective-permute-done | bytes 393248 | tf_op jit(solution)/shard_map/ppermute | solution.py:26
  (370 shorter events, 130.1 us)
Async XLA Ops:
  12.1 23.5 %collective-permute-start.6 = (bf16[384,768]{1,0:T(8,128)(2,1)S(1)}, bf16[384,768]{1,0:T(8,128)(2,1)S(1)}, u32[]{:S(2)}, u32[]{:S(2)}) collective-permute-start(bf16[384,768]{1,0:T(8,128)(2,1)S(1)} %dynamic-slice_bitcast_fusion.1), channel_id=1, source_target_pairs={{0,16},{1,17},{2,18},{3,19},{4,20},{5,21},{6,22},{7,23},{8,24},{9,... | collective-permute-start | bytes 1769480 | tf_op jit(solution)/shard_map/ppermute | solution.py:26
  12.2 16.8 %collective-permute-start.16 = (bf16[384,384]{1,0:T(8,128)(2,1)S(1)}, bf16[384,384]{1,0:T(8,128)(2,1)S(1)}, u32[]{:S(2)}, u32[]{:S(2)}) collective-permute-start(bf16[384,384]{1,0:T(8,128)(2,1)S(1)} %get-tuple-element.150.refs_8_), channel_id=1, source_target_pairs={{0,8},{1,9},{2,10},{3,11},{4,12},{5,13},{6,14},{7,15},{8,0},{9,1},... | collective-permute-start | bytes 884744 | tf_op jit(solution)/shard_map/ppermute | solution.py:26
  31.5 17.0 %collective-permute-start.3 = (bf16[384,384]{1,0:T(8,128)(2,1)S(1)}, bf16[384,384]{1,0:T(8,128)(2,1)S(1)}, u32[]{:S(2)}, u32[]{:S(2)}) collective-permute-start(bf16[384,384]{1,0:T(8,128)(2,1)S(1)} %get-tuple-element.90), channel_id=1, source_target_pairs={{0,4},{1,5},{2,6},{3,7},{4,0},{5,1},{6,2},{7,3},{8,12},{9,13},{10,... | collective-permute-start | bytes 884744 | tf_op jit(solution)/shard_map/ppermute | solution.py:26
  35.7 43.3 %collective-permute-start.40 = (bf16[512,768]{1,0:T(8,128)(2,1)S(1)}, bf16[512,768]{1,0:T(8,128)(2,1)}, u32[]{:S(2)}, u32[]{:S(2)}) collective-permute-start(bf16[512,768]{1,0:T(8,128)(2,1)S(1)} %pad_maximum_fusion), channel_id=1, source_target_pairs={{0,16},{1,17},{2,18},{3,19},{4,20},{5,21},{6,22},{7,23},{8,24},{9,... | collective-permute-start | bytes 2359304 | tf_op jit(solution)/shard_map/ppermute | solution.py:26
  41.5 16.9 %collective-permute-start.23 = (bf16[384,384]{1,0:T(8,128)(2,1)S(1)}, bf16[384,384]{1,0:T(8,128)(2,1)S(1)}, u32[]{:S(2)}, u32[]{:S(2)}) collective-permute-start(bf16[384,384]{1,0:T(8,128)(2,1)S(1)} %get-tuple-element.74.refs_16_), channel_id=1, source_target_pairs={{0,8},{1,9},{2,10},{3,11},{4,12},{5,13},{6,14},{7,15},{8,0},{9,1},... | collective-permute-start | bytes 884744 | tf_op jit(solution)/shard_map/ppermute | solution.py:26
  66.0 28.2 %collective-permute-start.10 = (bf16[128,1536]{1,0:T(8,128)(2,1)S(1)}, bf16[128,1536]{1,0:T(8,128)(2,1)S(1)}, u32[]{:S(2)}, u32[]{:S(2)}) collective-permute-start(bf16[128,1536]{1,0:T(8,128)(2,1)S(1)} %get-tuple-element.164.refs_0_), channel_id=1, source_target_pairs={{0,4},{1,5},{2,6},{3,7},{4,0},{5,1},{6,2},{7,3},{8,12},{9,13},{10,... | collective-permute-start | bytes 1179656 | tf_op jit(solution)/shard_map/ppermute | solution.py:26
  70.4 18.2 %collective-permute-start.30 = (bf16[384,384]{1,0:T(8,128)(2,1)S(1)}, bf16[384,384]{1,0:T(8,128)(2,1)S(1)}, u32[]{:S(2)}, u32[]{:S(2)}) collective-permute-start(bf16[384,384]{1,0:T(8,128)(2,1)S(1)} %get-tuple-element.81.refs_24_), channel_id=1, source_target_pairs={{0,8},{1,9},{2,10},{3,11},{4,12},{5,13},{6,14},{7,15},{8,0},{9,1},... | collective-permute-start | bytes 884744 | tf_op jit(solution)/shard_map/ppermute | solution.py:26
  81.7 18.8 %collective-permute-start.41 = (bf16[2,256,384]{2,1,0:T(8,128)(2,1)S(1)}, bf16[2,256,384]{2,1,0:T(8,128)(2,1)S(1)}, u32[]{:S(2)}, u32[]{:S(2)}) collective-permute-start(bf16[2,256,384]{2,1,0:T(8,128)(2,1)S(1)} %bitcast.112), channel_id=1, source_target_pairs={{0,4},{1,5},{2,6},{3,7},{4,0},{5,1},{6,2},{7,3},{8,12},{9,13},{10,... | collective-permute-start | bytes 1179656 | tf_op jit(solution)/shard_map/ppermute | solution.py:26
  105.7 21.1 %collective-permute-start.36 = (bf16[384,384]{1,0:T(8,128)(2,1)S(1)}, bf16[384,384]{1,0:T(8,128)(2,1)S(1)}, u32[]{:S(2)}, u32[]{:S(2)}) collective-permute-start(bf16[384,384]{1,0:T(8,128)(2,1)S(1)} %get-tuple-element.87.refs_32_), channel_id=1, source_target_pairs={{0,8},{1,9},{2,10},{3,11},{4,12},{5,13},{6,14},{7,15},{8,0},{9,1},... | collective-permute-start | bytes 884744 | tf_op jit(solution)/shard_map/ppermute | solution.py:26
  106.6 28.5 %collective-permute-start.11 = (bf16[128,1536]{1,0:T(8,128)(2,1)S(1)}, bf16[128,1536]{1,0:T(8,128)(2,1)S(1)}, u32[]{:S(2)}, u32[]{:S(2)}) collective-permute-start(bf16[128,1536]{1,0:T(8,128)(2,1)S(1)} %collective-permute-done.10.refs_4_), channel_id=1, source_target_pairs={{0,16},{1,17},{2,18},{3,19},{4,20},{5,21},{6,22},{7,23},{8,24},{9,... | collective-permute-start | bytes 1179656 | tf_op jit(solution)/shard_map/ppermute | solution.py:26
  111.2 22.5 %collective-permute-start.9 = (bf16[128,1536]{1,0:T(8,128)(2,1)S(1)}, bf16[128,1536]{1,0:T(8,128)(2,1)S(1)}, u32[]{:S(2)}, u32[]{:S(2)}) collective-permute-start(bf16[128,1536]{1,0:T(8,128)(2,1)S(1)} %collective-permute-done.8.refs_2_), channel_id=1, source_target_pairs={{0,16},{1,17},{2,18},{3,19},{4,20},{5,21},{6,22},{7,23},{8,24},{9,... | collective-permute-start | bytes 1179656 | tf_op jit(solution)/shard_map/ppermute | solution.py:26
  112.5 20.5 %collective-permute-start.39 = (bf16[384,384]{1,0:T(8,128)(2,1)S(1)}, bf16[384,384]{1,0:T(8,128)(2,1)S(1)}, u32[]{:S(2)}, u32[]{:S(2)}) collective-permute-start(bf16[384,384]{1,0:T(8,128)(2,1)S(1)} %copy-done.55), channel_id=1, source_target_pairs={{0,12},{1,13},{2,14},{3,15},{4,8},{5,9},{6,10},{7,11},{8,4},{9,5},... | collective-permute-start | bytes 884744 | tf_op jit(solution)/shard_map/ppermute | solution.py:26
  114.8 18.3 %collective-permute-start.37 = (bf16[384,384]{1,0:T(8,128)(2,1)S(1)}, bf16[384,384]{1,0:T(8,128)(2,1)S(1)}, u32[]{:S(2)}, u32[]{:S(2)}) collective-permute-start(bf16[384,384]{1,0:T(8,128)(2,1)S(1)} %copy-done.7), channel_id=1, source_target_pairs={{0,2},{1,3},{2,0},{3,1},{4,6},{5,7},{6,4},{7,5},{8,10},{9,11},{10,... | collective-permute-start | bytes 884744 | tf_op jit(solution)/shard_map/ppermute | solution.py:26
  133.7 35.9 %collective-permute-start.45 = (bf16[384,384]{1,0:T(8,128)(2,1)S(1)}, bf16[384,384]{1,0:T(8,128)(2,1)S(1)}, u32[]{:S(2)}, u32[]{:S(2)}) collective-permute-start(bf16[384,384]{1,0:T(8,128)(2,1)S(1)} %copy-done.7), channel_id=1, source_target_pairs={{0,8},{1,9},{2,10},{3,11},{4,12},{5,13},{6,14},{7,15},{8,0},{9,1},... | collective-permute-start | bytes 884744 | tf_op jit(solution)/shard_map/ppermute | solution.py:26
  133.7 35.9 %collective-permute-start.46 = (bf16[384,384]{1,0:T(8,128)(2,1)S(1)}, bf16[384,384]{1,0:T(8,128)(2,1)S(1)}, u32[]{:S(2)}, u32[]{:S(2)}) collective-permute-start(bf16[384,384]{1,0:T(8,128)(2,1)S(1)} %copy-done.37), channel_id=1, source_target_pairs={{0,12},{1,13},{2,14},{3,15},{4,8},{5,9},{6,10},{7,11},{8,4},{9,5},... | collective-permute-start | bytes 884744 | tf_op jit(solution)/shard_map/ppermute | solution.py:26
  175.5 22.7 %collective-permute-start.50 = (bf16[128,1536]{1,0:T(8,128)(2,1)S(1)}, bf16[128,1536]{1,0:T(8,128)(2,1)S(1)}, u32[]{:S(2)}, u32[]{:S(2)}) collective-permute-start(bf16[128,1536]{1,0:T(8,128)(2,1)S(1)} %get-tuple-element.136), channel_id=1, source_target_pairs={{0,1},{1,0},{2,3},{3,2},{4,5},{5,4},{6,7},{7,6},{8,9},{9,8},{10,11... | collective-permute-start | bytes 1179656 | tf_op jit(solution)/shard_map/ppermute | solution.py:26
  183.5 16.3 %collective-permute-start.67 = (bf16[384,384]{1,0:T(8,128)(2,1)S(1)}, bf16[384,384]{1,0:T(8,128)(2,1)}, u32[]{:S(2)}, u32[]{:S(2)}) collective-permute-start(bf16[384,384]{1,0:T(8,128)(2,1)S(1)} %copy-done.35), channel_id=1, source_target_pairs={{0,4},{1,5},{2,6},{3,7},{4,0},{5,1},{6,2},{7,3},{8,12},{9,13},{10,... | collective-permute-start | bytes 884744 | tf_op jit(solution)/shard_map/ppermute | solution.py:26
  197.6 24.5 %collective-permute-start.49 = (bf16[128,1536]{1,0:T(8,128)(2,1)}, bf16[128,1536]{1,0:T(8,128)(2,1)}, u32[]{:S(2)}, u32[]{:S(2)}) collective-permute-start(bf16[128,1536]{1,0:T(8,128)(2,1)} %get-tuple-element.100), channel_id=1, source_target_pairs={{0,1},{1,0},{2,3},{3,2},{4,5},{5,4},{6,7},{7,6},{8,9},{9,8},{10,11... | collective-permute-start | bytes 1179656 | tf_op jit(solution)/shard_map/ppermute | solution.py:26
  199.1 23.3 %collective-permute-start.51 = (bf16[128,1536]{1,0:T(8,128)(2,1)}, bf16[128,1536]{1,0:T(8,128)(2,1)}, u32[]{:S(2)}, u32[]{:S(2)}) collective-permute-start(bf16[128,1536]{1,0:T(8,128)(2,1)} %fusion.6), channel_id=1, source_target_pairs={{0,4},{1,5},{2,6},{3,7},{4,0},{5,1},{6,2},{7,3},{8,12},{9,13},{10,... | collective-permute-start | bytes 1179656 | tf_op jit(solution)/shard_map/ppermute | solution.py:26
  199.8 17.5 %collective-permute-start.66 = (bf16[384,384]{1,0:T(8,128)(2,1)}, bf16[384,384]{1,0:T(8,128)(2,1)}, u32[]{:S(2)}, u32[]{:S(2)}) collective-permute-start(bf16[384,384]{1,0:T(8,128)(2,1)} %get-tuple-element.108), channel_id=1, source_target_pairs={{0,12},{1,13},{2,14},{3,15},{4,8},{5,9},{6,10},{7,11},{8,4},{9,5},... | collective-permute-start | bytes 884744 | tf_op jit(solution)/shard_map/ppermute | solution.py:26
  217.3 23.1 %collective-permute-start.70 = (bf16[384,384]{1,0:T(8,128)(2,1)}, bf16[384,384]{1,0:T(8,128)(2,1)S(1)}, u32[]{:S(2)}, u32[]{:S(2)}) collective-permute-start(bf16[384,384]{1,0:T(8,128)(2,1)} %get-tuple-element.112.refs_24_), channel_id=1, source_target_pairs={{0,8},{1,9},{2,10},{3,11},{4,12},{5,13},{6,14},{7,15},{8,0},{9,1},... | collective-permute-start | bytes 884744 | tf_op jit(solution)/shard_map/ppermute | solution.py:26
  217.3 25.7 %collective-permute-start.73 = (bf16[384,384]{1,0:T(8,128)(2,1)}, bf16[384,384]{1,0:T(8,128)(2,1)S(1)}, u32[]{:S(2)}, u32[]{:S(2)}) collective-permute-start(bf16[384,384]{1,0:T(8,128)(2,1)} %get-tuple-element.116), channel_id=1, source_target_pairs={{0,12},{1,13},{2,14},{3,15},{4,8},{5,9},{6,10},{7,11},{8,4},{9,5},... | collective-permute-start | bytes 884744 | tf_op jit(solution)/shard_map/ppermute | solution.py:26
  220.5 19.8 %collective-permute-start.74 = (bf16[384,384]{1,0:T(8,128)(2,1)}, bf16[384,384]{1,0:T(8,128)(2,1)S(1)}, u32[]{:S(2)}, u32[]{:S(2)}) collective-permute-start(bf16[384,384]{1,0:T(8,128)(2,1)} %get-tuple-element.122), channel_id=1, source_target_pairs={{0,4},{1,5},{2,6},{3,7},{4,0},{5,1},{6,2},{7,3},{8,12},{9,13},{10,... | collective-permute-start | bytes 884744 | tf_op jit(solution)/shard_map/ppermute | solution.py:26
  222.0 18.3 %collective-permute-start.69 = (bf16[384,384]{1,0:T(8,128)(2,1)}, bf16[384,384]{1,0:T(8,128)(2,1)S(1)}, u32[]{:S(2)}, u32[]{:S(2)}) collective-permute-start(bf16[384,384]{1,0:T(8,128)(2,1)} %collective-permute-done.66.refs_22_), channel_id=1, source_target_pairs={{0,2},{1,3},{2,0},{3,1},{4,6},{5,7},{6,4},{7,5},{8,10},{9,11},{10,... | collective-permute-start | bytes 884744 | tf_op jit(solution)/shard_map/ppermute | solution.py:26
  222.3 20.1 %collective-permute-start.71 = (bf16[384,384]{1,0:T(8,128)(2,1)}, bf16[384,384]{1,0:T(8,128)(2,1)S(1)}, u32[]{:S(2)}, u32[]{:S(2)}) collective-permute-start(bf16[384,384]{1,0:T(8,128)(2,1)} %get-tuple-element.120.refs_32_), channel_id=1, source_target_pairs={{0,2},{1,3},{2,0},{3,1},{4,6},{5,7},{6,4},{7,5},{8,10},{9,11},{10,... | collective-permute-start | bytes 884744 | tf_op jit(solution)/shard_map/ppermute | solution.py:26
  240.3 18.4 %collective-permute-start.55 = (bf16[128,1536]{1,0:T(8,128)(2,1)S(1)}, bf16[128,1536]{1,0:T(8,128)(2,1)S(1)}, u32[]{:S(2)}, u32[]{:S(2)}) collective-permute-start(bf16[128,1536]{1,0:T(8,128)(2,1)S(1)} %fusion.11.refs_0_), channel_id=1, source_target_pairs={{0,4},{1,5},{2,6},{3,7},{4,0},{5,1},{6,2},{7,3},{8,12},{9,13},{10,... | collective-permute-start | bytes 1179656 | tf_op jit(solution)/shard_map/ppermute | solution.py:26
  240.5 24.6 %collective-permute-start.81 = (bf16[2,256,384]{2,1,0:T(8,128)(2,1)S(1)}, bf16[2,256,384]{2,1,0:T(8,128)(2,1)S(1)}, u32[]{:S(2)}, u32[]{:S(2)}) collective-permute-start(bf16[2,256,384]{2,1,0:T(8,128)(2,1)S(1)} %bitcast.111), channel_id=1, source_target_pairs={{0,4},{1,5},{2,6},{3,7},{4,0},{5,1},{6,2},{7,3},{8,12},{9,13},{10,... | collective-permute-start | bytes 1179656 | tf_op jit(solution)/shard_map/ppermute | solution.py:26
  242.5 21.4 %collective-permute-start.77 = (bf16[384,384]{1,0:T(8,128)(2,1)S(1)}, bf16[384,384]{1,0:T(8,128)(2,1)S(1)}, u32[]{:S(2)}, u32[]{:S(2)}) collective-permute-start(bf16[384,384]{1,0:T(8,128)(2,1)S(1)} %copy-done.9), channel_id=1, source_target_pairs={{0,8},{1,9},{2,10},{3,11},{4,12},{5,13},{6,14},{7,15},{8,0},{9,1},... | collective-permute-start | bytes 884744 | tf_op jit(solution)/shard_map/ppermute | solution.py:26
  243.0 20.9 %collective-permute-start.72 = (bf16[384,384]{1,0:T(8,128)(2,1)S(1)}, bf16[384,384]{1,0:T(8,128)(2,1)S(1)}, u32[]{:S(2)}, u32[]{:S(2)}) collective-permute-start(bf16[384,384]{1,0:T(8,128)(2,1)S(1)} %collective-permute-done.70.refs_28_), channel_id=1, source_target_pairs={{0,2},{1,3},{2,0},{3,1},{4,6},{5,7},{6,4},{7,5},{8,10},{9,11},{10,... | collective-permute-start | bytes 884744 | tf_op jit(solution)/shard_map/ppermute | solution.py:26
  250.3 23.2 %collective-permute-start.53 = (bf16[128,1536]{1,0:T(8,128)(2,1)S(1)}, bf16[128,1536]{1,0:T(8,128)(2,1)S(1)}, u32[]{:S(2)}, u32[]{:S(2)}) collective-permute-start(bf16[128,1536]{1,0:T(8,128)(2,1)S(1)} %fusion.11.refs_0_), channel_id=1, source_target_pairs={{0,1},{1,0},{2,3},{3,2},{4,5},{5,4},{6,7},{7,6},{8,9},{9,8},{10,11... | collective-permute-start | bytes 1179656 | tf_op jit(solution)/shard_map/ppermute | solution.py:26
  315.5 17.3 %collective-permute-start.84 = (bf16[128,1536]{1,0:T(8,128)(2,1)S(1)}, bf16[128,1536]{1,0:T(8,128)(2,1)S(1)}, u32[]{:S(2)}, u32[]{:S(2)}) collective-permute-start(bf16[128,1536]{1,0:T(8,128)(2,1)S(1)} %get-tuple-element.134), channel_id=1, source_target_pairs={{0,4},{1,5},{2,6},{3,7},{4,0},{5,1},{6,2},{7,3},{8,12},{9,13},{10,... | collective-permute-start | bytes 1179656 | tf_op jit(solution)/shard_map/ppermute | solution.py:26
  315.5 17.8 %collective-permute-start.83 = (bf16[128,1536]{1,0:T(8,128)(2,1)S(1)}, bf16[128,1536]{1,0:T(8,128)(2,1)S(1)}, u32[]{:S(2)}, u32[]{:S(2)}) collective-permute-start(bf16[128,1536]{1,0:T(8,128)(2,1)S(1)} %get-tuple-element.132), channel_id=1, source_target_pairs={{0,1},{1,0},{2,3},{3,2},{4,5},{5,4},{6,7},{7,6},{8,9},{9,8},{10,11... | collective-permute-start | bytes 1179656 | tf_op jit(solution)/shard_map/ppermute | solution.py:26
  (150 other events, 2518.3 us)

commit v5 on v4

--- a/solution.py
+++ b/solution.py
@@ -146,8 +146,14 @@
     x_sem, w_sem, kv_sem, out_sem = refs[14:]
     s, c = lax.axis_index("section"), lax.axis_index("col")
     half, lanes_of = slot_len // 2, [slice(h * HD, (h + 1) * HD) for h in range(bw // HD)]
-    x_copies = load_x((slots, slot_len, cols), x_refs, xv, x_sem)
+    one_plus[...] = 1.0 + mod_ref[:, 1:2, :]
+    for copy in load_x((slots, slot_len, cols), x_refs, xv, x_sem):
+        copy.wait()
     copies = [load_rows(w_refs[t], wv.at[t], w_sem, t * n_w, kr) for t in range(2)]
+    modulate((slots, slot_len, cols), wc, mod_ref, xv, stats, one_plus, xm)
+    for copy in copies[0] + copies[1]:
+        copy.wait()
+    copies.append(load_rows(w_refs[2], wv.at[2], w_sem, 2 * n_w, kr))
     kv_copies = []
     for slot in range(slots):
         for t, target in enumerate((keys, values)):
@@ -156,15 +162,8 @@
                 pltpu.make_async_copy(kv_refs[slot].at[t], place, kv_sem.at[2 * slot + t])
             )
             kv_copies[-1].start()
-    copies.append(load_rows(w_refs[2], wv.at[2], w_sem, 2 * n_w, kr))
     copies.append(load_rows(w_refs[3], ov, w_sem, 3 * n_w, None))
-    one_plus[...] = 1.0 + mod_ref[:, 1:2, :]
-    for copy in x_copies:
-        copy.wait()
-    modulate((slots, slot_len, cols), wc, mod_ref, xv, stats, one_plus, xm)
     for t in range(2):
-        for copy in copies[t]:
-            copy.wait()
         raw[t] = jnp.dot(xm[...], wv[t], preferred_element_type=jnp.float32)
     for copy in kv_copies + copies[2]:
         copy.wait()
@@ -271,10 +270,10 @@
     "O0.5": ("Q1.1",),
     "O0.7": ("Q1.3",),
     "K1.1": ("O0.5",),
-    "K1.3": ("O0.7",),
+    "K1.3": ("O0.7", "Q0.1",),
     "Q1.5": ("K1.1",),
     "Q1.7": ("K1.3",),
-    "V1.1": ("Q1.5",),
+    "V1.1": ("Q1.5", "V1.4",),
     "V1.3": ("Q1.7",),
     "K1.5": ("V1.1",),
     "K1.7": ("V1.3",),
@@ -293,6 +292,7 @@
     "V0.2": ("Q0.6",),
     "v0": ("aQ",),
     "l1": ("O1.6",),
+    "x.0.1": ("Q1.1",),
 }
 TREE = ("x", "r0", "g", )
 

time: 338 us -> 328 us (0.970)
  waiting for transfers between devices: 172 us -> 151 us
  starting transfers between devices: 85 us -> 103 us
  Pallas kernels: 42.3 us -> 36.5 us
    ppermute x87, waiting for transfers between devices: 172 us -> 151 us  [send_to(): return lax.ppermute(array, AXES, pairs)]
    ppermute x87, starting transfers between devices: 85 us -> 103 us  [send_to(): return lax.ppermute(array, AXES, pairs)]
    pallas_call x2, Pallas kernels: 38.6 us -> 32.8 us  [heads_of(): pl.pallas_call(functools.partial(layer_kernel, plan), out_shape=(shape, s...]
  transfers between devices with their start and end apart: 87 -> 87, of which waited for: 44 -> 39; matrix products, arithmetic and copies ran while one was open for 8% -> 7% of each run, Pallas kernels for 7% -> 6%
where the time goes in v5:
time: 328 us; the launch traced here: 327 us
  waiting for transfers between devices  151 us (46%)
  starting transfers between devices  103 us (31%)
  Pallas kernels  36.5 us (11%)
  other arithmetic  22.2 us (7%)
  local copies, waits for them, and re-layouts  12.3 us (4%)
    ppermute x87, waiting for transfers between devices, send_to(): return lax.ppermute(array, AXES, pairs)  151 us
    ppermute x87, starting transfers between devices, send_to(): return lax.ppermute(array, AXES, pairs)  103 us
    pallas_call x2, Pallas kernels, heads_of(): pl.pallas_call(functools.partial(layer_kernel, plan), out_shape=(shape, s...  32.8 us
    select_n x5, other arithmetic, block_of(): block = jnp.where(s == layer, cut(kind, s * wide + at, bw), other)  10.2 us
  transfers between devices with their start and end apart: 87, of which 39 were waited for; matrix products, arithmetic and copies ran while one was open for 7% of the time, Pallas kernels for 6%

profile of v5, /device:TPU:0, one launch (start us, length us, event | category | flops | bytes accessed | tf_op | source)
XLA Modules:
  0.0 327.1 jit_solution(4944146839429902849)
XLA Ops:
  21.4 4.4 %collective-permute-done.2.refs_10_ = bf16[384,384]{1,0:T(8,128)(2,1)S(1)} collective-permute-done((bf16[384,384]{1,0:T(8,128)(2,1)S(1)}, bf16[384,384]{1,0:T(8,128)(2,1)S(1)}, u32[]{:S(2)}, u32[]{:S(2)}) %collective-permute-start.2) | collective-permute-done | bytes 294944 | tf_op jit(solution)/shard_map/ppermute | solution.py:26
  36.1 9.9 %collective-permute-done.3.refs_34_ = bf16[384,384]{1,0:T(8,128)(2,1)S(1)} collective-permute-done((bf16[384,384]{1,0:T(8,128)(2,1)S(1)}, bf16[384,384]{1,0:T(8,128)(2,1)S(1)}, u32[]{:S(2)}, u32[]{:S(2)}) %collective-permute-start.3) | collective-permute-done | bytes 294944 | tf_op jit(solution)/shard_map/ppermute | solution.py:26
  51.1 10.3 %collective-permute-done.10.refs_20_ = bf16[384,384]{1,0:T(8,128)(2,1)S(1)} collective-permute-done((bf16[384,384]{1,0:T(8,128)(2,1)S(1)}, bf16[384,384]{1,0:T(8,128)(2,1)S(1)}, u32[]{:S(2)}, u32[]{:S(2)}) %collective-permute-start.10) | collective-permute-done | bytes 294944 | tf_op jit(solution)/shard_map/ppermute | solution.py:26
  61.8 2.8 collective-permute-start.30
  67.0 4.4 %collective-permute-done.16.refs_21_ = bf16[384,384]{1,0:T(8,128)(2,1)} collective-permute-done((bf16[384,384]{1,0:T(8,128)(2,1)S(1)}, bf16[384,384]{1,0:T(8,128)(2,1)}, u32[]{:S(2)}, u32[]{:S(2)}) %collective-permute-start.16) | collective-permute-done | bytes 294944 | tf_op jit(solution)/shard_map/ppermute | solution.py:26
  84.4 4.8 %collective-permute-done.11.refs_28_ = bf16[384,384]{1,0:T(8,128)(2,1)S(1)} collective-permute-done((bf16[384,384]{1,0:T(8,128)(2,1)S(1)}, bf16[384,384]{1,0:T(8,128)(2,1)S(1)}, u32[]{:S(2)}, u32[]{:S(2)}) %collective-permute-start.11) | collective-permute-done | bytes 294944 | tf_op jit(solution)/shard_map/ppermute | solution.py:26
  93.7 3.3 %collective-permute-done.41.refs_41_ = bf16[2,256,384]{2,1,0:T(8,128)(2,1)S(1)} collective-permute-done((bf16[2,256,384]{2,1,0:T(8,128)(2,1)S(1)}, bf16[2,256,384]{2,1,0:T(8,128)(2,1)S(1)}, u32[]{:S(2)}, u32[]{:S(2)}) %collective-permute-start.41) | collective-permute-done | bytes 393248 | tf_op jit(solution)/shard_map/ppermute | solution.py:26
  99.4 2.7 collective-permute-done.34.refs_30_
  107.1 5.9 %collective-permute-done.19.refs_9_ = bf16[384,384]{1,0:T(8,128)(2,1)} collective-permute-done((bf16[384,384]{1,0:T(8,128)(2,1)S(1)}, bf16[384,384]{1,0:T(8,128)(2,1)}, u32[]{:S(2)}, u32[]{:S(2)}) %collective-permute-start.19) | collective-permute-done | bytes 294944 | tf_op jit(solution)/shard_map/ppermute | solution.py:26
  113.0 3.1 collective-permute-start.39
  119.9 3.7 %modulation.1 = f32[2,3,3072]{2,1,0:T(4,128)} custom-call(bf16[8,256]{1,0:T(8,128)(2,1)} %fusion.21.feats_ref, bf16[3,256,3072]{2,1,0:T(8,128)(2,1)} %bitcast.107), custom_call_target="tpu_custom_call" | custom-call | tf_op jit(solution)/shard_map/modulation/pallas_call | solution.py:401
  126.5 5.4 %collective-permute-start.45 = (bf16[384,384]{1,0:T(8,128)(2,1)S(1)}, bf16[384,384]{1,0:T(8,128)(2,1)S(1)}, u32[]{:S(2)}, u32[]{:S(2)}) collective-permute-start(bf16[384,384]{1,0:T(8,128)(2,1)S(1)} %copy-done.7), channel_id=1, source_target_pairs={{0,8},{1,9},{2,10},{3,11},{4,12},{5,13},{6,14},{7,15},{8,0},{9,1},... | collective-permute-start | bytes 884744 | tf_op jit(solution)/shard_map/ppermute | solution.py:26
  137.4 6.2 %collective-permute-done.38.refs_37_ = bf16[384,384]{1,0:T(8,128)(2,1)S(1)} collective-permute-done((bf16[384,384]{1,0:T(8,128)(2,1)S(1)}, bf16[384,384]{1,0:T(8,128)(2,1)S(1)}, u32[]{:S(2)}, u32[]{:S(2)}) %collective-permute-start.38) | collective-permute-done | bytes 294944 | tf_op jit(solution)/shard_map/ppermute | solution.py:26
  143.5 5.2 %collective-permute-done.44.refs_39_ = bf16[384,384]{1,0:T(8,128)(2,1)S(1)} collective-permute-done((bf16[384,384]{1,0:T(8,128)(2,1)S(1)}, bf16[384,384]{1,0:T(8,128)(2,1)S(1)}, u32[]{:S(2)}, u32[]{:S(2)}) %collective-permute-start.44) | collective-permute-done | bytes 294944 | tf_op jit(solution)/shard_map/ppermute | solution.py:26
  149.6 16.4 %layer.2 = (bf16[2,128,3072]{2,1,0:T(8,128)(2,1)}, bf16[2,128,3072]{2,1,0:T(8,128)(2,1)}) custom-call(s32[2,4]{1,0:T(2,128)} %bitcast.113, f32[2,3,3072]{2,1,0:T(4,128)} %get-tuple-element.168.mod_ref, bf16[128,1536]{1,0:T(8,128)(2,1)} %copy-done.2, bf16[128,1536]{1,0:T(8,128)(2,1)} %get-tuple-element.165.refs_1_, bf16[128,1536]{1,0:T(8,128)(2,1)} %copy-done.27, ...), custom_call_target="tpu_custom_call" | custom-call | tf_op jit(solution)/shard_map/layer/pallas_call | solution.py:438
  174.0 8.9 %collective-permute-done.48.refs_20_ = bf16[384,384]{1,0:T(8,128)(2,1)} collective-permute-done((bf16[384,384]{1,0:T(8,128)(2,1)S(1)}, bf16[384,384]{1,0:T(8,128)(2,1)}, u32[]{:S(2)}, u32[]{:S(2)}) %collective-permute-start.48) | collective-permute-done | bytes 294944 | tf_op jit(solution)/shard_map/ppermute | solution.py:26
  187.7 5.2 %collective-permute-done.62.refs_19_ = bf16[384,384]{1,0:T(8,128)(2,1)S(1)} collective-permute-done((bf16[384,384]{1,0:T(8,128)(2,1)S(1)}, bf16[384,384]{1,0:T(8,128)(2,1)S(1)}, u32[]{:S(2)}, u32[]{:S(2)}) %collective-permute-start.62) | collective-permute-done | bytes 294944 | tf_op jit(solution)/shard_map/ppermute | solution.py:26
  194.6 4.4 %collective-permute-done.64.refs_28_ = bf16[384,384]{1,0:T(8,128)(2,1)S(1)} collective-permute-done((bf16[384,384]{1,0:T(8,128)(2,1)S(1)}, bf16[384,384]{1,0:T(8,128)(2,1)S(1)}, u32[]{:S(2)}, u32[]{:S(2)}) %collective-permute-start.64) | collective-permute-done | bytes 294944 | tf_op jit(solution)/shard_map/ppermute | solution.py:26
  207.2 4.6 %collective-permute-done.65.refs_25_ = bf16[384,384]{1,0:T(8,128)(2,1)S(1)} collective-permute-done((bf16[384,384]{1,0:T(8,128)(2,1)S(1)}, bf16[384,384]{1,0:T(8,128)(2,1)S(1)}, u32[]{:S(2)}, u32[]{:S(2)}) %collective-permute-start.65) | collective-permute-done | bytes 294944 | tf_op jit(solution)/shard_map/ppermute | solution.py:26
  216.6 3.5 %collective-permute-done.67.refs_22_ = bf16[384,384]{1,0:T(8,128)(2,1)} collective-permute-done((bf16[384,384]{1,0:T(8,128)(2,1)}, bf16[384,384]{1,0:T(8,128)(2,1)}, u32[]{:S(2)}, u32[]{:S(2)}) %collective-permute-start.67) | collective-permute-done | bytes 294944 | tf_op jit(solution)/shard_map/ppermute | solution.py:26
  227.2 8.4 %collective-permute-done.74.refs_34_ = bf16[384,384]{1,0:T(8,128)(2,1)S(1)} collective-permute-done((bf16[384,384]{1,0:T(8,128)(2,1)}, bf16[384,384]{1,0:T(8,128)(2,1)S(1)}, u32[]{:S(2)}, u32[]{:S(2)}) %collective-permute-start.74) | collective-permute-done | bytes 294944 | tf_op jit(solution)/shard_map/ppermute | solution.py:26
  242.1 2.8 collective-permute-done.75.refs_35_
  246.2 4.2 %collective-permute-done.55.refs_4_ = bf16[128,1536]{1,0:T(8,128)(2,1)S(1)} collective-permute-done((bf16[128,1536]{1,0:T(8,128)(2,1)S(1)}, bf16[128,1536]{1,0:T(8,128)(2,1)S(1)}, u32[]{:S(2)}, u32[]{:S(2)}) %collective-permute-start.55) | collective-permute-done | bytes 393248 | tf_op jit(solution)/shard_map/ppermute | solution.py:26
  250.9 3.7 %collective-permute-done.77.refs_36_ = bf16[384,384]{1,0:T(8,128)(2,1)S(1)} collective-permute-done((bf16[384,384]{1,0:T(8,128)(2,1)S(1)}, bf16[384,384]{1,0:T(8,128)(2,1)S(1)}, u32[]{:S(2)}, u32[]{:S(2)}) %collective-permute-start.77) | collective-permute-done | bytes 294944 | tf_op jit(solution)/shard_map/ppermute | solution.py:26
  254.6 6.0 %collective-permute-start.79 = (bf16[384,384]{1,0:T(8,128)(2,1)S(1)}, bf16[384,384]{1,0:T(8,128)(2,1)S(1)}, u32[]{:S(2)}, u32[]{:S(2)}) collective-permute-start(bf16[384,384]{1,0:T(8,128)(2,1)S(1)} %copy-done.35), channel_id=1, source_target_pairs={{0,12},{1,13},{2,14},{3,15},{4,8},{5,9},{6,10},{7,11},{8,4},{9,5},... | collective-permute-start | bytes 884744 | tf_op jit(solution)/shard_map/ppermute | solution.py:26
  262.6 2.7 collective-permute-done.79.refs_38_
  270.8 6.5 %collective-permute-done.80.refs_39_ = bf16[384,384]{1,0:T(8,128)(2,1)S(1)} collective-permute-done((bf16[384,384]{1,0:T(8,128)(2,1)S(1)}, bf16[384,384]{1,0:T(8,128)(2,1)S(1)}, u32[]{:S(2)}, u32[]{:S(2)}) %collective-permute-start.80) | collective-permute-done | bytes 294944 | tf_op jit(solution)/shard_map/ppermute | solution.py:26
  278.6 16.4 %layer.3 = (bf16[2,128,3072]{2,1,0:T(8,128)(2,1)}, bf16[2,128,3072]{2,1,0:T(8,128)(2,1)}) custom-call(s32[2,4]{1,0:T(2,128)} %bitcast.114, f32[2,3,3072]{2,1,0:T(4,128)} %get-tuple-element.167.mod_ref, bf16[128,1536]{1,0:T(8,128)(2,1)} %copy-done, bf16[128,1536]{1,0:T(8,128)(2,1)} %copy-done.4, bf16[128,1536]{1,0:T(8,128)(2,1)} %copy-done.28, ...), custom_call_target="tpu_custom_call" | custom-call | tf_op jit(solution)/shard_map/layer/pallas_call | solution.py:438
  295.1 3.6 %collective-permute-done.82 = bf16[2,128,3072]{2,1,0:T(8,128)(2,1)S(1)} collective-permute-done((bf16[2,128,3072]{2,1,0:T(8,128)(2,1)}, bf16[2,128,3072]{2,1,0:T(8,128)(2,1)S(1)}, u32[]{:S(2)}, u32[]{:S(2)}) %collective-permute-start.82) | collective-permute-done | bytes 1572896 | tf_op jit(solution)/shard_map/ppermute | solution.py:26
  300.3 4.7 %collective-permute-start.85 = (bf16[128,1536]{1,0:T(8,128)(2,1)S(1)}, bf16[128,1536]{1,0:T(8,128)(2,1)S(1)}, u32[]{:S(2)}, u32[]{:S(2)}) collective-permute-start(bf16[128,1536]{1,0:T(8,128)(2,1)S(1)} %get-tuple-element.135), channel_id=1, source_target_pairs={{0,5},{1,4},{2,7},{3,6},{4,1},{5,0},{6,3},{7,2},{8,13},{9,12},{10,... | collective-permute-start | bytes 1179656 | tf_op jit(solution)/shard_map/ppermute | solution.py:26
  307.3 7.6 %collective-permute-done.85 = bf16[128,1536]{1,0:T(8,128)(2,1)S(1)} collective-permute-done((bf16[128,1536]{1,0:T(8,128)(2,1)S(1)}, bf16[128,1536]{1,0:T(8,128)(2,1)S(1)}, u32[]{:S(2)}, u32[]{:S(2)}) %collective-permute-start.85) | collective-permute-done | bytes 393248 | tf_op jit(solution)/shard_map/ppermute | solution.py:26
  314.9 7.9 %collective-permute-done.84 = bf16[128,1536]{1,0:T(8,128)(2,1)S(1)} collective-permute-done((bf16[128,1536]{1,0:T(8,128)(2,1)S(1)}, bf16[128,1536]{1,0:T(8,128)(2,1)S(1)}, u32[]{:S(2)}, u32[]{:S(2)}) %collective-permute-start.84) | collective-permute-done | bytes 393248 | tf_op jit(solution)/shard_map/ppermute | solution.py:26
  (366 shorter events, 136.0 us)
Async XLA Ops:
  12.1 22.8 %collective-permute-start.6 = (bf16[384,768]{1,0:T(8,128)(2,1)S(1)}, bf16[384,768]{1,0:T(8,128)(2,1)S(1)}, u32[]{:S(2)}, u32[]{:S(2)}) collective-permute-start(bf16[384,768]{1,0:T(8,128)(2,1)S(1)} %dynamic-slice_bitcast_fusion.1), channel_id=1, source_target_pairs={{0,16},{1,17},{2,18},{3,19},{4,20},{5,21},{6,22},{7,23},{8,24},{9,... | collective-permute-start | bytes 1769480 | tf_op jit(solution)/shard_map/ppermute | solution.py:26
  12.2 16.8 %collective-permute-start.9 = (bf16[384,384]{1,0:T(8,128)(2,1)S(1)}, bf16[384,384]{1,0:T(8,128)(2,1)S(1)}, u32[]{:S(2)}, u32[]{:S(2)}) collective-permute-start(bf16[384,384]{1,0:T(8,128)(2,1)S(1)} %get-tuple-element.152.refs_8_), channel_id=1, source_target_pairs={{0,8},{1,9},{2,10},{3,11},{4,12},{5,13},{6,14},{7,15},{8,0},{9,1},... | collective-permute-start | bytes 884744 | tf_op jit(solution)/shard_map/ppermute | solution.py:26
  29.0 19.1 %collective-permute-start.5 = (bf16[384,384]{1,0:T(8,128)(2,1)S(1)}, bf16[384,384]{1,0:T(8,128)(2,1)S(1)}, u32[]{:S(2)}, u32[]{:S(2)}) collective-permute-start(bf16[384,384]{1,0:T(8,128)(2,1)S(1)} %get-tuple-element.153), channel_id=1, source_target_pairs={{0,12},{1,13},{2,14},{3,15},{4,8},{5,9},{6,10},{7,11},{8,4},{9,5},... | collective-permute-start | bytes 884744 | tf_op jit(solution)/shard_map/ppermute | solution.py:26
  33.3 16.3 %collective-permute-start.28 = (bf16[384,384]{1,0:T(8,128)(2,1)S(1)}, bf16[384,384]{1,0:T(8,128)(2,1)S(1)}, u32[]{:S(2)}, u32[]{:S(2)}) collective-permute-start(bf16[384,384]{1,0:T(8,128)(2,1)S(1)} %collective-permute-done.27.refs_18_), channel_id=1, source_target_pairs={{0,2},{1,3},{2,0},{3,1},{4,6},{5,7},{6,4},{7,5},{8,10},{9,11},{10,... | collective-permute-start | bytes 884744 | tf_op jit(solution)/shard_map/ppermute | solution.py:26
  35.0 44.5 %collective-permute-start.40 = (bf16[512,768]{1,0:T(8,128)(2,1)S(1)}, bf16[512,768]{1,0:T(8,128)(2,1)}, u32[]{:S(2)}, u32[]{:S(2)}) collective-permute-start(bf16[512,768]{1,0:T(8,128)(2,1)S(1)} %pad_maximum_fusion), channel_id=1, source_target_pairs={{0,16},{1,17},{2,18},{3,19},{4,20},{5,21},{6,22},{7,23},{8,24},{9,... | collective-permute-start | bytes 2359304 | tf_op jit(solution)/shard_map/ppermute | solution.py:26
  46.0 15.3 %collective-permute-start.10 = (bf16[384,384]{1,0:T(8,128)(2,1)S(1)}, bf16[384,384]{1,0:T(8,128)(2,1)S(1)}, u32[]{:S(2)}, u32[]{:S(2)}) collective-permute-start(bf16[384,384]{1,0:T(8,128)(2,1)S(1)} %get-tuple-element.73.refs_16_), channel_id=1, source_target_pairs={{0,8},{1,9},{2,10},{3,11},{4,12},{5,13},{6,14},{7,15},{8,0},{9,1},... | collective-permute-start | bytes 884744 | tf_op jit(solution)/shard_map/ppermute | solution.py:26
  48.1 16.6 %collective-permute-start.31 = (bf16[384,384]{1,0:T(8,128)(2,1)S(1)}, bf16[384,384]{1,0:T(8,128)(2,1)S(1)}, u32[]{:S(2)}, u32[]{:S(2)}) collective-permute-start(bf16[384,384]{1,0:T(8,128)(2,1)S(1)} %get-tuple-element.87), channel_id=1, source_target_pairs={{0,4},{1,5},{2,6},{3,7},{4,0},{5,1},{6,2},{7,3},{8,12},{9,13},{10,... | collective-permute-start | bytes 884744 | tf_op jit(solution)/shard_map/ppermute | solution.py:26
  67.0 25.1 %collective-permute-start.22 = (bf16[128,1536]{1,0:T(8,128)(2,1)S(1)}, bf16[128,1536]{1,0:T(8,128)(2,1)S(1)}, u32[]{:S(2)}, u32[]{:S(2)}) collective-permute-start(bf16[128,1536]{1,0:T(8,128)(2,1)S(1)} %get-tuple-element.80.refs_0_), channel_id=1, source_target_pairs={{0,4},{1,5},{2,6},{3,7},{4,0},{5,1},{6,2},{7,3},{8,12},{9,13},{10,... | collective-permute-start | bytes 1179656 | tf_op jit(solution)/shard_map/ppermute | solution.py:26
  71.4 17.7 %collective-permute-start.11 = (bf16[384,384]{1,0:T(8,128)(2,1)S(1)}, bf16[384,384]{1,0:T(8,128)(2,1)S(1)}, u32[]{:S(2)}, u32[]{:S(2)}) collective-permute-start(bf16[384,384]{1,0:T(8,128)(2,1)S(1)} %get-tuple-element.75.refs_24_), channel_id=1, source_target_pairs={{0,8},{1,9},{2,10},{3,11},{4,12},{5,13},{6,14},{7,15},{8,0},{9,1},... | collective-permute-start | bytes 884744 | tf_op jit(solution)/shard_map/ppermute | solution.py:26
  102.1 15.6 %collective-permute-start.37 = (bf16[384,384]{1,0:T(8,128)(2,1)S(1)}, bf16[384,384]{1,0:T(8,128)(2,1)S(1)}, u32[]{:S(2)}, u32[]{:S(2)}) collective-permute-start(bf16[384,384]{1,0:T(8,128)(2,1)S(1)} %get-tuple-element.90.refs_32_), channel_id=1, source_target_pairs={{0,8},{1,9},{2,10},{3,11},{4,12},{5,13},{6,14},{7,15},{8,0},{9,1},... | collective-permute-start | bytes 884744 | tf_op jit(solution)/shard_map/ppermute | solution.py:26
  107.0 24.9 %collective-permute-start.23 = (bf16[128,1536]{1,0:T(8,128)(2,1)S(1)}, bf16[128,1536]{1,0:T(8,128)(2,1)S(1)}, u32[]{:S(2)}, u32[]{:S(2)}) collective-permute-start(bf16[128,1536]{1,0:T(8,128)(2,1)S(1)} %collective-permute-done.22.refs_4_), channel_id=1, source_target_pairs={{0,16},{1,17},{2,18},{3,19},{4,20},{5,21},{6,22},{7,23},{8,24},{9,... | collective-permute-start | bytes 1179656 | tf_op jit(solution)/shard_map/ppermute | solution.py:26
  112.9 20.6 %collective-permute-start.25 = (bf16[128,1536]{1,0:T(8,128)(2,1)S(1)}, bf16[128,1536]{1,0:T(8,128)(2,1)S(1)}, u32[]{:S(2)}, u32[]{:S(2)}) collective-permute-start(bf16[128,1536]{1,0:T(8,128)(2,1)S(1)} %collective-permute-done.24.refs_6_), channel_id=1, source_target_pairs={{0,16},{1,17},{2,18},{3,19},{4,20},{5,21},{6,22},{7,23},{8,24},{9,... | collective-permute-start | bytes 1179656 | tf_op jit(solution)/shard_map/ppermute | solution.py:26
  116.1 19.6 %collective-permute-start.20 = (bf16[128,1536]{1,0:T(8,128)(2,1)S(1)}, bf16[128,1536]{1,0:T(8,128)(2,1)S(1)}, u32[]{:S(2)}, u32[]{:S(2)}) collective-permute-start(bf16[128,1536]{1,0:T(8,128)(2,1)S(1)} %get-tuple-element.80.refs_0_), channel_id=1, source_target_pairs={{0,1},{1,0},{2,3},{3,2},{4,5},{5,4},{6,7},{7,6},{8,9},{9,8},{10,11... | collective-permute-start | bytes 1179656 | tf_op jit(solution)/shard_map/ppermute | solution.py:26
  126.5 39.5 %collective-permute-start.45 = (bf16[384,384]{1,0:T(8,128)(2,1)S(1)}, bf16[384,384]{1,0:T(8,128)(2,1)S(1)}, u32[]{:S(2)}, u32[]{:S(2)}) collective-permute-start(bf16[384,384]{1,0:T(8,128)(2,1)S(1)} %copy-done.7), channel_id=1, source_target_pairs={{0,8},{1,9},{2,10},{3,11},{4,12},{5,13},{6,14},{7,15},{8,0},{9,1},... | collective-permute-start | bytes 884744 | tf_op jit(solution)/shard_map/ppermute | solution.py:26
  131.9 34.2 %collective-permute-start.46 = (bf16[384,384]{1,0:T(8,128)(2,1)S(1)}, bf16[384,384]{1,0:T(8,128)(2,1)S(1)}, u32[]{:S(2)}, u32[]{:S(2)}) collective-permute-start(bf16[384,384]{1,0:T(8,128)(2,1)S(1)} %copy-done.38), channel_id=1, source_target_pairs={{0,12},{1,13},{2,14},{3,15},{4,8},{5,9},{6,10},{7,11},{8,4},{9,5},... | collective-permute-start | bytes 884744 | tf_op jit(solution)/shard_map/ppermute | solution.py:26
  166.1 16.8 %collective-permute-start.61 = (bf16[384,384]{1,0:T(8,128)(2,1)}, bf16[384,384]{1,0:T(8,128)(2,1)S(1)}, u32[]{:S(2)}, u32[]{:S(2)}) collective-permute-start(bf16[384,384]{1,0:T(8,128)(2,1)} %get-tuple-element.111), channel_id=1, source_target_pairs={{0,4},{1,5},{2,6},{3,7},{4,0},{5,1},{6,2},{7,3},{8,12},{9,13},{10,... | collective-permute-start | bytes 884744 | tf_op jit(solution)/shard_map/ppermute | solution.py:26
  166.2 16.7 %collective-permute-start.48 = (bf16[384,384]{1,0:T(8,128)(2,1)S(1)}, bf16[384,384]{1,0:T(8,128)(2,1)}, u32[]{:S(2)}, u32[]{:S(2)}) collective-permute-start(bf16[384,384]{1,0:T(8,128)(2,1)S(1)} %copy-done.8), channel_id=1, source_target_pairs={{0,8},{1,9},{2,10},{3,11},{4,12},{5,13},{6,14},{7,15},{8,0},{9,1},... | collective-permute-start | bytes 884744 | tf_op jit(solution)/shard_map/ppermute | solution.py:26
  168.9 16.3 %collective-permute-start.59 = (bf16[384,384]{1,0:T(8,128)(2,1)S(1)}, bf16[384,384]{1,0:T(8,128)(2,1)S(1)}, u32[]{:S(2)}, u32[]{:S(2)}) collective-permute-start(bf16[384,384]{1,0:T(8,128)(2,1)S(1)} %copy-done.8), channel_id=1, source_target_pairs={{0,2},{1,3},{2,0},{3,1},{4,6},{5,7},{6,4},{7,5},{8,10},{9,11},{10,... | collective-permute-start | bytes 884744 | tf_op jit(solution)/shard_map/ppermute | solution.py:26
  172.6 29.8 %collective-permute-start.50 = (bf16[128,1536]{1,0:T(8,128)(2,1)S(1)}, bf16[128,1536]{1,0:T(8,128)(2,1)S(1)}, u32[]{:S(2)}, u32[]{:S(2)}) collective-permute-start(bf16[128,1536]{1,0:T(8,128)(2,1)S(1)} %get-tuple-element.138), channel_id=1, source_target_pairs={{0,1},{1,0},{2,3},{3,2},{4,5},{5,4},{6,7},{7,6},{8,9},{9,8},{10,11... | collective-permute-start | bytes 1179656 | tf_op jit(solution)/shard_map/ppermute | solution.py:26
  185.5 17.9 %collective-permute-start.68 = (bf16[384,384]{1,0:T(8,128)(2,1)S(1)}, bf16[384,384]{1,0:T(8,128)(2,1)}, u32[]{:S(2)}, u32[]{:S(2)}) collective-permute-start(bf16[384,384]{1,0:T(8,128)(2,1)S(1)} %copy-done.36), channel_id=1, source_target_pairs={{0,4},{1,5},{2,6},{3,7},{4,0},{5,1},{6,2},{7,3},{8,12},{9,13},{10,... | collective-permute-start | bytes 884744 | tf_op jit(solution)/shard_map/ppermute | solution.py:26
  200.9 22.9 %collective-permute-start.49 = (bf16[128,1536]{1,0:T(8,128)(2,1)}, bf16[128,1536]{1,0:T(8,128)(2,1)}, u32[]{:S(2)}, u32[]{:S(2)}) collective-permute-start(bf16[128,1536]{1,0:T(8,128)(2,1)} %get-tuple-element.102), channel_id=1, source_target_pairs={{0,1},{1,0},{2,3},{3,2},{4,5},{5,4},{6,7},{7,6},{8,9},{9,8},{10,11... | collective-permute-start | bytes 1179656 | tf_op jit(solution)/shard_map/ppermute | solution.py:26
  203.3 21.0 %collective-permute-start.51 = (bf16[128,1536]{1,0:T(8,128)(2,1)}, bf16[128,1536]{1,0:T(8,128)(2,1)}, u32[]{:S(2)}, u32[]{:S(2)}) collective-permute-start(bf16[128,1536]{1,0:T(8,128)(2,1)} %fusion.6), channel_id=1, source_target_pairs={{0,4},{1,5},{2,6},{3,7},{4,0},{5,1},{6,2},{7,3},{8,12},{9,13},{10,... | collective-permute-start | bytes 1179656 | tf_op jit(solution)/shard_map/ppermute | solution.py:26
  203.4 16.7 %collective-permute-start.67 = (bf16[384,384]{1,0:T(8,128)(2,1)}, bf16[384,384]{1,0:T(8,128)(2,1)}, u32[]{:S(2)}, u32[]{:S(2)}) collective-permute-start(bf16[384,384]{1,0:T(8,128)(2,1)} %get-tuple-element.111), channel_id=1, source_target_pairs={{0,12},{1,13},{2,14},{3,15},{4,8},{5,9},{6,10},{7,11},{8,4},{9,5},... | collective-permute-start | bytes 884744 | tf_op jit(solution)/shard_map/ppermute | solution.py:26
  220.1 20.5 %collective-permute-start.73 = (bf16[384,384]{1,0:T(8,128)(2,1)}, bf16[384,384]{1,0:T(8,128)(2,1)S(1)}, u32[]{:S(2)}, u32[]{:S(2)}) collective-permute-start(bf16[384,384]{1,0:T(8,128)(2,1)} %get-tuple-element.118), channel_id=1, source_target_pairs={{0,12},{1,13},{2,14},{3,15},{4,8},{5,9},{6,10},{7,11},{8,4},{9,5},... | collective-permute-start | bytes 884744 | tf_op jit(solution)/shard_map/ppermute | solution.py:26
  225.7 24.6 %collective-permute-start.55 = (bf16[128,1536]{1,0:T(8,128)(2,1)S(1)}, bf16[128,1536]{1,0:T(8,128)(2,1)S(1)}, u32[]{:S(2)}, u32[]{:S(2)}) collective-permute-start(bf16[128,1536]{1,0:T(8,128)(2,1)S(1)} %fusion.11.refs_0_), channel_id=1, source_target_pairs={{0,4},{1,5},{2,6},{3,7},{4,0},{5,1},{6,2},{7,3},{8,12},{9,13},{10,... | collective-permute-start | bytes 1179656 | tf_op jit(solution)/shard_map/ppermute | solution.py:26
  236.0 24.9 %collective-permute-start.81 = (bf16[2,256,384]{2,1,0:T(8,128)(2,1)S(1)}, bf16[2,256,384]{2,1,0:T(8,128)(2,1)S(1)}, u32[]{:S(2)}, u32[]{:S(2)}) collective-permute-start(bf16[2,256,384]{2,1,0:T(8,128)(2,1)S(1)} %bitcast.111), channel_id=1, source_target_pairs={{0,4},{1,5},{2,6},{3,7},{4,0},{5,1},{6,2},{7,3},{8,12},{9,13},{10,... | collective-permute-start | bytes 1179656 | tf_op jit(solution)/shard_map/ppermute | solution.py:26
  238.5 16.1 %collective-permute-start.77 = (bf16[384,384]{1,0:T(8,128)(2,1)S(1)}, bf16[384,384]{1,0:T(8,128)(2,1)S(1)}, u32[]{:S(2)}, u32[]{:S(2)}) collective-permute-start(bf16[384,384]{1,0:T(8,128)(2,1)S(1)} %copy-done.9), channel_id=1, source_target_pairs={{0,8},{1,9},{2,10},{3,11},{4,12},{5,13},{6,14},{7,15},{8,0},{9,1},... | collective-permute-start | bytes 884744 | tf_op jit(solution)/shard_map/ppermute | solution.py:26
  240.6 19.9 %collective-permute-start.72 = (bf16[384,384]{1,0:T(8,128)(2,1)S(1)}, bf16[384,384]{1,0:T(8,128)(2,1)S(1)}, u32[]{:S(2)}, u32[]{:S(2)}) collective-permute-start(bf16[384,384]{1,0:T(8,128)(2,1)S(1)} %copy-done.63), channel_id=1, source_target_pairs={{0,2},{1,3},{2,0},{3,1},{4,6},{5,7},{6,4},{7,5},{8,10},{9,11},{10,... | collective-permute-start | bytes 884744 | tf_op jit(solution)/shard_map/ppermute | solution.py:26
  244.9 22.4 %collective-permute-start.53 = (bf16[128,1536]{1,0:T(8,128)(2,1)S(1)}, bf16[128,1536]{1,0:T(8,128)(2,1)S(1)}, u32[]{:S(2)}, u32[]{:S(2)}) collective-permute-start(bf16[128,1536]{1,0:T(8,128)(2,1)S(1)} %fusion.11.refs_0_), channel_id=1, source_target_pairs={{0,1},{1,0},{2,3},{3,2},{4,5},{5,4},{6,7},{7,6},{8,9},{9,8},{10,11... | collective-permute-start | bytes 1179656 | tf_op jit(solution)/shard_map/ppermute | solution.py:26
  250.3 17.5 %collective-permute-start.57 = (bf16[128,1536]{1,0:T(8,128)(2,1)S(1)}, bf16[128,1536]{1,0:T(8,128)(2,1)S(1)}, u32[]{:S(2)}, u32[]{:S(2)}) collective-permute-start(bf16[128,1536]{1,0:T(8,128)(2,1)S(1)} %collective-permute-done.55.refs_4_), channel_id=1, source_target_pairs={{0,1},{1,0},{2,3},{3,2},{4,5},{5,4},{6,7},{7,6},{8,9},{9,8},{10,11... | collective-permute-start | bytes 1179656 | tf_op jit(solution)/shard_map/ppermute | solution.py:26
  305.0 17.9 %collective-permute-start.84 = (bf16[128,1536]{1,0:T(8,128)(2,1)S(1)}, bf16[128,1536]{1,0:T(8,128)(2,1)S(1)}, u32[]{:S(2)}, u32[]{:S(2)}) collective-permute-start(bf16[128,1536]{1,0:T(8,128)(2,1)S(1)} %get-tuple-element.136), channel_id=1, source_target_pairs={{0,4},{1,5},{2,6},{3,7},{4,0},{5,1},{6,2},{7,3},{8,12},{9,13},{10,... | collective-permute-start | bytes 1179656 | tf_op jit(solution)/shard_map/ppermute | solution.py:26
  305.1 17.8 %collective-permute-start.83 = (bf16[128,1536]{1,0:T(8,128)(2,1)S(1)}, bf16[128,1536]{1,0:T(8,128)(2,1)S(1)}, u32[]{:S(2)}, u32[]{:S(2)}) collective-permute-start(bf16[128,1536]{1,0:T(8,128)(2,1)S(1)} %get-tuple-element.134), channel_id=1, source_target_pairs={{0,1},{1,0},{2,3},{3,2},{4,5},{5,4},{6,7},{7,6},{8,9},{9,8},{10,11... | collective-permute-start | bytes 1179656 | tf_op jit(solution)/shard_map/ppermute | solution.py:26
  (148 other events, 2489.5 us)

commit v6 on v5

--- a/solution.py
+++ b/solution.py
@@ -138,14 +138,12 @@
 
 
 def layer_kernel(plan, ends_ref, mod_ref, *refs):
-    slots, slot_len, cols, n_x, n_w, kr, nr, bw, wc = plan
+    slots, slot_len, cols, n_x, n_w, kr, bw, wc = plan
     x_refs, refs = refs[:n_x], refs[n_x:]
-    w_refs, refs = [refs[t * n_w : (t + 1) * n_w] for t in range(4)], refs[4 * n_w :]
+    w_refs, refs = [refs[t * n_w : (t + 1) * n_w] for t in range(3)], refs[3 * n_w :]
     kv_refs, refs = refs[:slots], refs[slots:]
-    keep_ref, pass_ref, xv, stats, one_plus, xm, wv, ov, raw, queries, keys, values, att, out = refs[:14]
-    x_sem, w_sem, kv_sem, out_sem = refs[14:]
-    s, c = lax.axis_index("section"), lax.axis_index("col")
-    half, lanes_of = slot_len // 2, [slice(h * HD, (h + 1) * HD) for h in range(bw // HD)]
+    att, xv, stats, one_plus, xm, wv, raw, queries, keys, values, x_sem, w_sem, kv_sem = refs
+    lanes_of = [slice(h * HD, (h + 1) * HD) for h in range(bw // HD)]
     one_plus[...] = 1.0 + mod_ref[:, 1:2, :]
     for copy in load_x((slots, slot_len, cols), x_refs, xv, x_sem):
         copy.wait()
@@ -162,7 +160,6 @@
                 pltpu.make_async_copy(kv_refs[slot].at[t], place, kv_sem.at[2 * slot + t])
             )
             kv_copies[-1].start()
-    copies.append(load_rows(w_refs[3], ov, w_sem, 3 * n_w, None))
     for t in range(2):
         raw[t] = jnp.dot(xm[...], wv[t], preferred_element_type=jnp.float32)
     for copy in kv_copies + copies[2]:
@@ -203,7 +200,17 @@
             )
             mixed = jnp.dot(both, values[slot, :, lanes], preferred_element_type=jnp.float32)
             att[rows, lanes] = mixed.astype(jnp.bfloat16)
-    for copy in copies[3]:
+
+
+def project_kernel(plan, att_ref, *refs):
+    slots, slot_len, cols, n_w, nr = plan
+    o_refs, refs = refs[:n_w], refs[n_w:]
+    keep_ref, pass_ref, att, ov, out, o_sem, out_sem = refs
+    s, c = lax.axis_index("section"), lax.axis_index("col")
+    half = slot_len // 2
+    first = pltpu.make_async_copy(att_ref, att, o_sem.at[n_w])
+    first.start()
+    for copy in load_rows(o_refs, ov, o_sem, 0, None) + [first]:
         copy.wait()
     out_copies = []
     for k, (side, out_ref) in enumerate(((1 - s, pass_ref), (s, keep_ref))):
@@ -234,7 +241,7 @@
 
 GATES = {
     "K0.4": ("Q0.4",),
-    "K0.6": ("Q0.6",),
+    "K0.6": ("Q0.6", "K0.1",),
     "V0.4": ("K0.4",),
     "V0.6": ("K0.6",),
     "O0.4": ("V0.4",),
@@ -243,7 +250,7 @@
     "Q1.6": ("O0.6",),
     "K1.4": ("Q1.4",),
     "K1.6": ("Q1.6",),
-    "V1.4": ("K1.4",),
+    "V1.4": ("K1.4", "K1.1",),
     "V1.6": ("K1.6",),
     "O1.4": ("V1.4",),
     "O1.6": ("V1.6",),
@@ -251,7 +258,7 @@
     "Q1.2": ("S0.2",),
     "K1.2": ("K0.2",),
     "V1.2": ("V0.2",),
-    "O1.2": ("O0.2", "O0.5",),
+    "O1.2": ("O0.2", "aK",),
     "S1.2": ("Q1.2",),
     "K0.1": ("Q0.1",),
     "K0.3": ("Q0.3",),
@@ -292,7 +299,6 @@
     "V0.2": ("Q0.6",),
     "v0": ("aQ",),
     "l1": ("O1.6",),
-    "x.0.1": ("Q1.1",),
 }
 TREE = ("x", "r0", "g", )
 
@@ -430,44 +436,58 @@
     def x_pieces(kind):
         return [get(f"{kind}.{di}.{dc}" + end) for di, dc in places for end in ("", "c")]
 
+    every = slots * slot_len
+
     def heads_of(layer):
         pieces = x_pieces("xg"[layer])
-        plan = (slots, slot_len, cols, len(pieces), rows, kr, nr, bw, wc)
-        shape = jax.ShapeDtypeStruct((slots, half, feat), jnp.bfloat16)
-        every = slots * slot_len
+        plan = (slots, slot_len, cols, len(pieces), rows, kr, bw, wc)
         return pl.pallas_call(
             functools.partial(layer_kernel, plan),
-            out_shape=(shape, shape),
+            out_shape=jax.ShapeDtypeStruct((every, bw), jnp.bfloat16),
             in_specs=[pl.BlockSpec(memory_space=pltpu.SMEM), vmem_spec()]
-            + [any_spec()] * (len(pieces) + 4 * rows + slots),
-            out_specs=(any_spec(), any_spec()),
+            + [any_spec()] * (len(pieces) + 3 * rows + slots),
+            out_specs=vmem_spec(),
             scratch_shapes=[
                 pltpu.VMEM((cols, every, wc), jnp.bfloat16),
                 pltpu.VMEM((2, every, 128), jnp.float32),
                 pltpu.VMEM((slots, 1, feat), jnp.float32),
                 pltpu.VMEM((every, feat), jnp.bfloat16),
                 pltpu.VMEM((3, feat, bw), jnp.bfloat16),
-                pltpu.VMEM((rows, bw, nr), jnp.bfloat16),
                 pltpu.VMEM((2, every, bw), jnp.float32),
                 pltpu.VMEM((every, bw), jnp.bfloat16),
                 pltpu.VMEM((slots, 2 * slot_len, bw), jnp.bfloat16),
                 pltpu.VMEM((slots, 2 * slot_len, bw), jnp.bfloat16),
-                pltpu.VMEM((every, bw), jnp.bfloat16),
-                pltpu.VMEM((2, slots, half, feat), jnp.bfloat16),
                 pltpu.SemaphoreType.DMA((len(pieces),)),
-                pltpu.SemaphoreType.DMA((4 * rows,)),
+                pltpu.SemaphoreType.DMA((3 * rows,)),
                 pltpu.SemaphoreType.DMA((2 * slots,)),
-                pltpu.SemaphoreType.DMA((2,)),
             ],
             compiler_params=pltpu.CompilerParams(vmem_limit_bytes=VMEM_LIMIT),
             name="layer",
         )(
-            gated(get("n")[:, :NP], f"v{layer}"),
+            gated(get("n")[:, :NP], f"k{layer}"),
             get("m")[layer],
             *pieces,
-            *[one for kind in "QKVO" for one in of_rows(kind, layer)],
+            *[one for kind in "QKV" for one in of_rows(kind, layer)],
             *stale_of(layer),
         )
+
+    def project(layer):
+        shape = jax.ShapeDtypeStruct((slots, half, feat), jnp.bfloat16)
+        return pl.pallas_call(
+            functools.partial(project_kernel, (slots, slot_len, cols, rows, nr)),
+            out_shape=(shape, shape),
+            in_specs=[any_spec()] * (1 + rows),
+            out_specs=(any_spec(), any_spec()),
+            scratch_shapes=[
+                pltpu.VMEM((every, bw), jnp.bfloat16),
+                pltpu.VMEM((rows, bw, nr), jnp.bfloat16),
+                pltpu.VMEM((2, slots, half, feat), jnp.bfloat16),
+                pltpu.SemaphoreType.DMA((rows + 1,)),
+                pltpu.SemaphoreType.DMA((2,)),
+            ],
+            compiler_params=pltpu.CompilerParams(vmem_limit_bytes=VMEM_LIMIT),
+            name="project",
+        )(gated(get(f"k{layer}"), f"v{layer}"), *of_rows("O", layer))
 
     def parts(layer):
         keep, other = get(f"v{layer}")[0], get(f"p{layer}")
@@ -492,7 +512,8 @@
         return send(name, get(f"u{layer}.{di}").astype(jnp.bfloat16), di, 0)
 
     for layer in range(2):
-        step(f"v{layer}")(functools.partial(heads_of, layer))
+        step(f"k{layer}")(functools.partial(heads_of, layer))
+        step(f"v{layer}")(functools.partial(project, layer))
         step(f"p{layer}")(lambda layer=layer: swap(f"p{layer}", get(f"v{layer}")[1]))
         step(f"t{layer}")(functools.partial(parts, layer))
         for di, dc in places:

time: 328 us -> 315 us (0.960)
  starting transfers between devices: 103 us -> 76.6 us
  local copies, waits for them, and re-layouts: 12.3 us -> 17.3 us
  Pallas kernels: 36.5 us -> 41.4 us
  waiting for transfers between devices: 151 us -> 155 us
    ppermute x87, starting transfers between devices: 103 us -> 76.6 us  [send_to(): return lax.ppermute(array, AXES, pairs)]
    pallas_call x2 -> x4, Pallas kernels: 32.8 us -> 37.6 us  [the longest x2 27.6 us: heads_of(): pl.pallas_call(functools.partial(layer_kernel, plan), out_shape=jax.Shape...]
    ppermute x87, waiting for transfers between devices: 151 us -> 155 us  [send_to(): return lax.ppermute(array, AXES, pairs)]
    unnamed x186 -> x192, local copies, waits for them, and re-layouts: 2.92 us -> 6.92 us
  transfers between devices with their start and end apart: 87 -> 87, of which waited for: 39 -> 38; matrix products, arithmetic and copies ran while one was open for 7% -> 8% of each run, Pallas kernels for 6% -> 12%
where the time goes in v6:
time: 315 us; the launch traced here: 314 us
  waiting for transfers between devices  155 us (49%)
  starting transfers between devices  76.6 us (24%)
  Pallas kernels  41.4 us (13%)
  other arithmetic  22 us (7%)
  local copies, waits for them, and re-layouts  17.3 us (5%)
    ppermute x87, waiting for transfers between devices, send_to(): return lax.ppermute(array, AXES, pairs)  155 us
    ppermute x87, starting transfers between devices, send_to(): return lax.ppermute(array, AXES, pairs)  76.6 us
    pallas_call x2, Pallas kernels, heads_of(): pl.pallas_call(functools.partial(layer_kernel, plan), out_shape=jax.Shape...  27.6 us
    select_n x5, other arithmetic, block_of(): block = jnp.where(s == layer, cut(kind, s * wide + at, bw), other)  10.1 us
    pallas_call x2, Pallas kernels, project(): pl.pallas_call(functools.partial(project_kernel, (slots, slot_len, cols,...  10 us
    unnamed x192, local copies, waits for them, and re-layouts  6.92 us
  transfers between devices with their start and end apart: 87, of which 38 were waited for; matrix products, arithmetic and copies ran while one was open for 8% of the time, Pallas kernels for 12%

profile of v6, /device:TPU:0, one launch (start us, length us, event | category | flops | bytes accessed | tf_op | source)
XLA Modules:
  0.0 314.5 jit_solution(3036652402457368589)
XLA Ops:
  21.5 4.4 %collective-permute-done.2.refs_10_ = bf16[384,384]{1,0:T(8,128)(2,1)S(1)} collective-permute-done((bf16[384,384]{1,0:T(8,128)(2,1)S(1)}, bf16[384,384]{1,0:T(8,128)(2,1)S(1)}, u32[]{:S(2)}, u32[]{:S(2)}) %collective-permute-start.2) | collective-permute-done | bytes 294944 | tf_op jit(solution)/shard_map/ppermute | solution.py:26
  36.1 5.4 %collective-permute-done.5.refs_14_ = bf16[384,384]{1,0:T(8,128)(2,1)} collective-permute-done((bf16[384,384]{1,0:T(8,128)(2,1)S(1)}, bf16[384,384]{1,0:T(8,128)(2,1)}, u32[]{:S(2)}, u32[]{:S(2)}) %collective-permute-start.5) | collective-permute-done | bytes 294944 | tf_op jit(solution)/shard_map/ppermute | solution.py:26
  43.7 5.2 %collective-permute-done.3.refs_2_ = bf16[384,384]{1,0:T(8,128)(2,1)S(1)} collective-permute-done((bf16[384,384]{1,0:T(8,128)(2,1)S(1)}, bf16[384,384]{1,0:T(8,128)(2,1)S(1)}, u32[]{:S(2)}, u32[]{:S(2)}) %collective-permute-start.3) | collective-permute-done | bytes 294944 | tf_op jit(solution)/shard_map/ppermute | solution.py:26
  51.7 6.1 %collective-permute-done.23.refs_20_ = bf16[384,384]{1,0:T(8,128)(2,1)S(1)} collective-permute-done((bf16[384,384]{1,0:T(8,128)(2,1)S(1)}, bf16[384,384]{1,0:T(8,128)(2,1)S(1)}, u32[]{:S(2)}, u32[]{:S(2)}) %collective-permute-start.23) | collective-permute-done | bytes 294944 | tf_op jit(solution)/shard_map/ppermute | solution.py:26
  57.8 3.5 %collective-permute-start.26 = (bf16[384,384]{1,0:T(8,128)(2,1)}, bf16[384,384]{1,0:T(8,128)(2,1)S(1)}, u32[]{:S(2)}, u32[]{:S(2)}) collective-permute-start(bf16[384,384]{1,0:T(8,128)(2,1)} %copy-done.73), channel_id=1, source_target_pairs={{0,12},{1,13},{2,14},{3,15},{4,8},{5,9},{6,10},{7,11},{8,4},{9,5},... | collective-permute-start | bytes 884744 | tf_op jit(solution)/shard_map/ppermute | solution.py:26
  66.8 2.9 collective-permute-done.26.refs_22_
  69.7 4.0 %collective-permute-start.30 = (bf16[384,384]{1,0:T(8,128)(2,1)S(1)}, bf16[384,384]{1,0:T(8,128)(2,1)S(1)}, u32[]{:S(2)}, u32[]{:S(2)}) collective-permute-start(bf16[384,384]{1,0:T(8,128)(2,1)S(1)} %get-tuple-element.80.refs_24_), channel_id=1, source_target_pairs={{0,8},{1,9},{2,10},{3,11},{4,12},{5,13},{6,14},{7,15},{8,0},{9,1},... | collective-permute-start | bytes 884744 | tf_op jit(solution)/shard_map/ppermute | solution.py:26
  81.1 5.2 %collective-permute-done.29.refs_23_ = bf16[384,384]{1,0:T(8,128)(2,1)S(1)} collective-permute-done((bf16[384,384]{1,0:T(8,128)(2,1)S(1)}, bf16[384,384]{1,0:T(8,128)(2,1)S(1)}, u32[]{:S(2)}, u32[]{:S(2)}) %collective-permute-start.29) | collective-permute-done | bytes 294944 | tf_op jit(solution)/shard_map/ppermute | solution.py:26
  88.4 3.9 %collective-permute-done.31.refs_1_ = bf16[384,384]{1,0:T(8,128)(2,1)S(1)} collective-permute-done((bf16[384,384]{1,0:T(8,128)(2,1)S(1)}, bf16[384,384]{1,0:T(8,128)(2,1)S(1)}, u32[]{:S(2)}, u32[]{:S(2)}) %collective-permute-start.31) | collective-permute-done | bytes 294944 | tf_op jit(solution)/shard_map/ppermute | solution.py:26
  95.1 4.7 %collective-permute-done.37.refs_33_ = bf16[2,256,384]{2,1,0:T(8,128)(2,1)S(1)} collective-permute-done((bf16[2,256,384]{2,1,0:T(8,128)(2,1)S(1)}, bf16[2,256,384]{2,1,0:T(8,128)(2,1)S(1)}, u32[]{:S(2)}, u32[]{:S(2)}) %collective-permute-start.37) | collective-permute-done | bytes 393248 | tf_op jit(solution)/shard_map/ppermute | solution.py:26
  105.9 4.5 %collective-permute-done.42.refs_10_ = bf16[384,384]{1,0:T(8,128)(2,1)S(1)} collective-permute-done((bf16[384,384]{1,0:T(8,128)(2,1)S(1)}, bf16[384,384]{1,0:T(8,128)(2,1)S(1)}, u32[]{:S(2)}, u32[]{:S(2)}) %collective-permute-start.42) | collective-permute-done | bytes 294944 | tf_op jit(solution)/shard_map/ppermute | solution.py:26
  114.6 11.5 %collective-permute-done.38.refs_4_ = bf16[384,384]{1,0:T(8,128)(2,1)S(1)} collective-permute-done((bf16[384,384]{1,0:T(8,128)(2,1)S(1)}, bf16[384,384]{1,0:T(8,128)(2,1)S(1)}, u32[]{:S(2)}, u32[]{:S(2)}) %collective-permute-start.38) | collective-permute-done | bytes 294944 | tf_op jit(solution)/shard_map/ppermute | solution.py:26
  127.3 3.7 %modulation.1 = f32[2,3,3072]{2,1,0:T(4,128)} custom-call(bf16[8,256]{1,0:T(8,128)(2,1)} %fusion.21.feats_ref, bf16[3,256,3072]{2,1,0:T(8,128)(2,1)} %bitcast.107), custom_call_target="tpu_custom_call" | custom-call | tf_op jit(solution)/shard_map/modulation/pallas_call | solution.py:407
  138.9 13.8 %layer.2.att_ref = bf16[512,384]{1,0:T(8,128)(2,1)} custom-call(s32[2,4]{1,0:T(2,128)} %bitcast.113, f32[2,3,3072]{2,1,0:T(4,128)} %get-tuple-element.166.mod_ref, bf16[128,1536]{1,0:T(8,128)(2,1)} %copy-done.2, bf16[128,1536]{1,0:T(8,128)(2,1)} %get-tuple-element.163.refs_1_, bf16[128,1536]{1,0:T(8,128)(2,1)} %copy-done.21, bf16[128,1536]{1,0:T(8,128)(2,1)} %copy-done.25, ...), custom_call_target="tpu_custom_call" | custom-call | tf_op jit(solution)/shard_map/layer/pallas_call | solution.py:444
  154.1 5.0 %project.2 = (bf16[2,128,3072]{2,1,0:T(8,128)(2,1)}, bf16[2,128,3072]{2,1,0:T(8,128)(2,1)}) custom-call(bf16[512,384]{1,0:T(8,128)(2,1)} %layer.2.att_ref, bf16[384,384]{1,0:T(8,128)(2,1)} %copy-done.14, bf16[384,384]{1,0:T(8,128)(2,1)} %copy-done.81, bf16[384,384]{1,0:T(8,128)(2,1)} %copy-done.79, bf16[384,384]{1,0:T(8,128)(2,1)} %copy-done.82, ...), custom_call_target="tpu_custom_call" | custom-call | tf_op jit(solution)/shard_map/project/pallas_call | solution.py:476
  166.0 5.0 %collective-permute-done.59.refs_17_ = bf16[384,384]{1,0:T(8,128)(2,1)S(1)} collective-permute-done((bf16[384,384]{1,0:T(8,128)(2,1)S(1)}, bf16[384,384]{1,0:T(8,128)(2,1)S(1)}, u32[]{:S(2)}, u32[]{:S(2)}) %collective-permute-start.59) | collective-permute-done | bytes 294944 | tf_op jit(solution)/shard_map/ppermute | solution.py:26
  171.6 3.0 collective-permute-done.61.refs_18_
  179.8 5.6 %collective-permute-done.62.refs_19_ = bf16[384,384]{1,0:T(8,128)(2,1)S(1)} collective-permute-done((bf16[384,384]{1,0:T(8,128)(2,1)S(1)}, bf16[384,384]{1,0:T(8,128)(2,1)S(1)}, u32[]{:S(2)}, u32[]{:S(2)}) %collective-permute-start.62) | collective-permute-done | bytes 294944 | tf_op jit(solution)/shard_map/ppermute | solution.py:26
  185.9 6.8 %collective-permute-done.64.refs_28_ = bf16[384,384]{1,0:T(8,128)(2,1)S(1)} collective-permute-done((bf16[384,384]{1,0:T(8,128)(2,1)S(1)}, bf16[384,384]{1,0:T(8,128)(2,1)S(1)}, u32[]{:S(2)}, u32[]{:S(2)}) %collective-permute-start.64) | collective-permute-done | bytes 294944 | tf_op jit(solution)/shard_map/ppermute | solution.py:26
  196.9 5.7 %collective-permute-done.65.refs_25_ = bf16[384,384]{1,0:T(8,128)(2,1)S(1)} collective-permute-done((bf16[384,384]{1,0:T(8,128)(2,1)S(1)}, bf16[384,384]{1,0:T(8,128)(2,1)S(1)}, u32[]{:S(2)}, u32[]{:S(2)}) %collective-permute-start.65) | collective-permute-done | bytes 294944 | tf_op jit(solution)/shard_map/ppermute | solution.py:26
  206.0 5.6 %collective-permute-done.67.refs_22_ = bf16[384,384]{1,0:T(8,128)(2,1)} collective-permute-done((bf16[384,384]{1,0:T(8,128)(2,1)}, bf16[384,384]{1,0:T(8,128)(2,1)}, u32[]{:S(2)}, u32[]{:S(2)}) %collective-permute-start.67) | collective-permute-done | bytes 294944 | tf_op jit(solution)/shard_map/ppermute | solution.py:26
  218.2 8.3 %collective-permute-done.74.refs_2_ = bf16[384,384]{1,0:T(8,128)(2,1)S(1)} collective-permute-done((bf16[384,384]{1,0:T(8,128)(2,1)}, bf16[384,384]{1,0:T(8,128)(2,1)S(1)}, u32[]{:S(2)}, u32[]{:S(2)}) %collective-permute-start.74) | collective-permute-done | bytes 294944 | tf_op jit(solution)/shard_map/ppermute | solution.py:26
  228.0 3.7 %collective-permute-start.80 = (bf16[384,384]{1,0:T(8,128)(2,1)S(1)}, bf16[384,384]{1,0:T(8,128)(2,1)S(1)}, u32[]{:S(2)}, u32[]{:S(2)}) collective-permute-start(bf16[384,384]{1,0:T(8,128)(2,1)S(1)} %copy-done.34), channel_id=1, source_target_pairs={{0,12},{1,13},{2,14},{3,15},{4,8},{5,9},{6,10},{7,11},{8,4},{9,5},... | collective-permute-start | bytes 884744 | tf_op jit(solution)/shard_map/ppermute | solution.py:26
  231.8 5.3 %collective-permute-done.75.refs_3_ = bf16[384,384]{1,0:T(8,128)(2,1)S(1)} collective-permute-done((bf16[384,384]{1,0:T(8,128)(2,1)S(1)}, bf16[384,384]{1,0:T(8,128)(2,1)S(1)}, u32[]{:S(2)}, u32[]{:S(2)}) %collective-permute-start.75) | collective-permute-done | bytes 294944 | tf_op jit(solution)/shard_map/ppermute | solution.py:26
  238.7 4.9 %collective-permute-done.55.refs_4_ = bf16[128,1536]{1,0:T(8,128)(2,1)S(1)} collective-permute-done((bf16[128,1536]{1,0:T(8,128)(2,1)S(1)}, bf16[128,1536]{1,0:T(8,128)(2,1)S(1)}, u32[]{:S(2)}, u32[]{:S(2)}) %collective-permute-start.55) | collective-permute-done | bytes 393248 | tf_op jit(solution)/shard_map/ppermute | solution.py:26
  245.1 7.5 %collective-permute-done.78.refs_4_ = bf16[384,384]{1,0:T(8,128)(2,1)S(1)} collective-permute-done((bf16[384,384]{1,0:T(8,128)(2,1)S(1)}, bf16[384,384]{1,0:T(8,128)(2,1)S(1)}, u32[]{:S(2)}, u32[]{:S(2)}) %collective-permute-start.78) | collective-permute-done | bytes 294944 | tf_op jit(solution)/shard_map/ppermute | solution.py:26
  253.9 7.0 %collective-permute-done.77.refs_33_ = bf16[2,256,384]{2,1,0:T(8,128)(2,1)S(1)} collective-permute-done((bf16[2,256,384]{2,1,0:T(8,128)(2,1)S(1)}, bf16[2,256,384]{2,1,0:T(8,128)(2,1)S(1)}, u32[]{:S(2)}, u32[]{:S(2)}) %collective-permute-start.77) | collective-permute-done | bytes 393248 | tf_op jit(solution)/shard_map/ppermute | solution.py:26
  264.0 13.9 %layer.3.att_ref = bf16[512,384]{1,0:T(8,128)(2,1)} custom-call(s32[2,4]{1,0:T(2,128)} %bitcast.114, f32[2,3,3072]{2,1,0:T(4,128)} %get-tuple-element.165.mod_ref, bf16[128,1536]{1,0:T(8,128)(2,1)} %copy-done, bf16[128,1536]{1,0:T(8,128)(2,1)} %copy-done.4, bf16[128,1536]{1,0:T(8,128)(2,1)} %copy-done.26, bf16[128,1536]{1,0:T(8,128)(2,1)} %copy-done.31, ...), custom_call_target="tpu_custom_call" | custom-call | tf_op jit(solution)/shard_map/layer/pallas_call | solution.py:444
  279.3 5.0 %project.3 = (bf16[2,128,3072]{2,1,0:T(8,128)(2,1)}, bf16[2,128,3072]{2,1,0:T(8,128)(2,1)}) custom-call(bf16[512,384]{1,0:T(8,128)(2,1)} %layer.3.att_ref, bf16[384,384]{1,0:T(8,128)(2,1)} %get-tuple-element.121.refs_0_, bf16[384,384]{1,0:T(8,128)(2,1)} %copy-done.84, bf16[384,384]{1,0:T(8,128)(2,1)} %copy-done.83, bf16[384,384]{1,0:T(8,128)(2,1)} %copy-done.86, ...), custom_call_target="tpu_custom_call" | custom-call | tf_op jit(solution)/shard_map/project/pallas_call | solution.py:476
  284.4 3.6 %collective-permute-done.82 = bf16[2,128,3072]{2,1,0:T(8,128)(2,1)S(1)} collective-permute-done((bf16[2,128,3072]{2,1,0:T(8,128)(2,1)}, bf16[2,128,3072]{2,1,0:T(8,128)(2,1)S(1)}, u32[]{:S(2)}, u32[]{:S(2)}) %collective-permute-start.82) | collective-permute-done | bytes 1572896 | tf_op jit(solution)/shard_map/ppermute | solution.py:26
  294.1 8.6 %collective-permute-done.85 = bf16[128,1536]{1,0:T(8,128)(2,1)S(1)} collective-permute-done((bf16[128,1536]{1,0:T(8,128)(2,1)S(1)}, bf16[128,1536]{1,0:T(8,128)(2,1)S(1)}, u32[]{:S(2)}, u32[]{:S(2)}) %collective-permute-start.85) | collective-permute-done | bytes 393248 | tf_op jit(solution)/shard_map/ppermute | solution.py:26
  302.6 7.7 %collective-permute-done.84 = bf16[128,1536]{1,0:T(8,128)(2,1)S(1)} collective-permute-done((bf16[128,1536]{1,0:T(8,128)(2,1)S(1)}, bf16[128,1536]{1,0:T(8,128)(2,1)S(1)}, u32[]{:S(2)}, u32[]{:S(2)}) %collective-permute-start.84) | collective-permute-done | bytes 393248 | tf_op jit(solution)/shard_map/ppermute | solution.py:26
  (374 shorter events, 122.1 us)
Async XLA Ops:
  12.1 22.8 %collective-permute-start.6 = (bf16[384,768]{1,0:T(8,128)(2,1)S(1)}, bf16[384,768]{1,0:T(8,128)(2,1)S(1)}, u32[]{:S(2)}, u32[]{:S(2)}) collective-permute-start(bf16[384,768]{1,0:T(8,128)(2,1)S(1)} %dynamic-slice_bitcast_fusion.1), channel_id=1, source_target_pairs={{0,16},{1,17},{2,18},{3,19},{4,20},{5,21},{6,22},{7,23},{8,24},{9,... | collective-permute-start | bytes 1769480 | tf_op jit(solution)/shard_map/ppermute | solution.py:26
  12.2 16.8 %collective-permute-start.16 = (bf16[384,384]{1,0:T(8,128)(2,1)S(1)}, bf16[384,384]{1,0:T(8,128)(2,1)S(1)}, u32[]{:S(2)}, u32[]{:S(2)}) collective-permute-start(bf16[384,384]{1,0:T(8,128)(2,1)S(1)} %get-tuple-element.150.refs_8_), channel_id=1, source_target_pairs={{0,8},{1,9},{2,10},{3,11},{4,12},{5,13},{6,14},{7,15},{8,0},{9,1},... | collective-permute-start | bytes 884744 | tf_op jit(solution)/shard_map/ppermute | solution.py:26
  31.5 17.4 %collective-permute-start.3 = (bf16[384,384]{1,0:T(8,128)(2,1)S(1)}, bf16[384,384]{1,0:T(8,128)(2,1)S(1)}, u32[]{:S(2)}, u32[]{:S(2)}) collective-permute-start(bf16[384,384]{1,0:T(8,128)(2,1)S(1)} %get-tuple-element.90), channel_id=1, source_target_pairs={{0,4},{1,5},{2,6},{3,7},{4,0},{5,1},{6,2},{7,3},{8,12},{9,13},{10,... | collective-permute-start | bytes 884744 | tf_op jit(solution)/shard_map/ppermute | solution.py:26
  32.2 16.6 %collective-permute-start.19 = (bf16[384,384]{1,0:T(8,128)(2,1)S(1)}, bf16[384,384]{1,0:T(8,128)(2,1)S(1)}, u32[]{:S(2)}, u32[]{:S(2)}) collective-permute-start(bf16[384,384]{1,0:T(8,128)(2,1)S(1)} %collective-permute-done.16.refs_12_), channel_id=1, source_target_pairs={{0,2},{1,3},{2,0},{3,1},{4,6},{5,7},{6,4},{7,5},{8,10},{9,11},{10,... | collective-permute-start | bytes 884744 | tf_op jit(solution)/shard_map/ppermute | solution.py:26
  35.0 43.3 %collective-permute-start.36 = (bf16[512,768]{1,0:T(8,128)(2,1)S(1)}, bf16[512,768]{1,0:T(8,128)(2,1)}, u32[]{:S(2)}, u32[]{:S(2)}) collective-permute-start(bf16[512,768]{1,0:T(8,128)(2,1)S(1)} %pad_maximum_fusion), channel_id=1, source_target_pairs={{0,16},{1,17},{2,18},{3,19},{4,20},{5,21},{6,22},{7,23},{8,24},{9,... | collective-permute-start | bytes 2359304 | tf_op jit(solution)/shard_map/ppermute | solution.py:26
  41.6 16.3 %collective-permute-start.23 = (bf16[384,384]{1,0:T(8,128)(2,1)S(1)}, bf16[384,384]{1,0:T(8,128)(2,1)S(1)}, u32[]{:S(2)}, u32[]{:S(2)}) collective-permute-start(bf16[384,384]{1,0:T(8,128)(2,1)S(1)} %get-tuple-element.73.refs_16_), channel_id=1, source_target_pairs={{0,8},{1,9},{2,10},{3,11},{4,12},{5,13},{6,14},{7,15},{8,0},{9,1},... | collective-permute-start | bytes 884744 | tf_op jit(solution)/shard_map/ppermute | solution.py:26
  65.3 28.2 %collective-permute-start.10 = (bf16[128,1536]{1,0:T(8,128)(2,1)S(1)}, bf16[128,1536]{1,0:T(8,128)(2,1)S(1)}, u32[]{:S(2)}, u32[]{:S(2)}) collective-permute-start(bf16[128,1536]{1,0:T(8,128)(2,1)S(1)} %get-tuple-element.164.refs_0_), channel_id=1, source_target_pairs={{0,4},{1,5},{2,6},{3,7},{4,0},{5,1},{6,2},{7,3},{8,12},{9,13},{10,... | collective-permute-start | bytes 1179656 | tf_op jit(solution)/shard_map/ppermute | solution.py:26
  69.7 18.2 %collective-permute-start.30 = (bf16[384,384]{1,0:T(8,128)(2,1)S(1)}, bf16[384,384]{1,0:T(8,128)(2,1)S(1)}, u32[]{:S(2)}, u32[]{:S(2)}) collective-permute-start(bf16[384,384]{1,0:T(8,128)(2,1)S(1)} %get-tuple-element.80.refs_24_), channel_id=1, source_target_pairs={{0,8},{1,9},{2,10},{3,11},{4,12},{5,13},{6,14},{7,15},{8,0},{9,1},... | collective-permute-start | bytes 884744 | tf_op jit(solution)/shard_map/ppermute | solution.py:26
  81.0 18.8 %collective-permute-start.37 = (bf16[2,256,384]{2,1,0:T(8,128)(2,1)S(1)}, bf16[2,256,384]{2,1,0:T(8,128)(2,1)S(1)}, u32[]{:S(2)}, u32[]{:S(2)}) collective-permute-start(bf16[2,256,384]{2,1,0:T(8,128)(2,1)S(1)} %bitcast.112), channel_id=1, source_target_pairs={{0,4},{1,5},{2,6},{3,7},{4,0},{5,1},{6,2},{7,3},{8,12},{9,13},{10,... | collective-permute-start | bytes 1179656 | tf_op jit(solution)/shard_map/ppermute | solution.py:26
  105.0 21.1 %collective-permute-start.38 = (bf16[384,384]{1,0:T(8,128)(2,1)S(1)}, bf16[384,384]{1,0:T(8,128)(2,1)S(1)}, u32[]{:S(2)}, u32[]{:S(2)}) collective-permute-start(bf16[384,384]{1,0:T(8,128)(2,1)S(1)} %get-tuple-element.87.refs_0_), channel_id=1, source_target_pairs={{0,8},{1,9},{2,10},{3,11},{4,12},{5,13},{6,14},{7,15},{8,0},{9,1},... | collective-permute-start | bytes 884744 | tf_op jit(solution)/shard_map/ppermute | solution.py:26
  105.8 28.6 %collective-permute-start.11 = (bf16[128,1536]{1,0:T(8,128)(2,1)S(1)}, bf16[128,1536]{1,0:T(8,128)(2,1)S(1)}, u32[]{:S(2)}, u32[]{:S(2)}) collective-permute-start(bf16[128,1536]{1,0:T(8,128)(2,1)S(1)} %collective-permute-done.10.refs_4_), channel_id=1, source_target_pairs={{0,16},{1,17},{2,18},{3,19},{4,20},{5,21},{6,22},{7,23},{8,24},{9,... | collective-permute-start | bytes 1179656 | tf_op jit(solution)/shard_map/ppermute | solution.py:26
  110.4 22.5 %collective-permute-start.9 = (bf16[128,1536]{1,0:T(8,128)(2,1)S(1)}, bf16[128,1536]{1,0:T(8,128)(2,1)S(1)}, u32[]{:S(2)}, u32[]{:S(2)}) collective-permute-start(bf16[128,1536]{1,0:T(8,128)(2,1)S(1)} %collective-permute-done.8.refs_2_), channel_id=1, source_target_pairs={{0,16},{1,17},{2,18},{3,19},{4,20},{5,21},{6,22},{7,23},{8,24},{9,... | collective-permute-start | bytes 1179656 | tf_op jit(solution)/shard_map/ppermute | solution.py:26
  111.8 19.3 %collective-permute-start.41 = (bf16[384,384]{1,0:T(8,128)(2,1)S(1)}, bf16[384,384]{1,0:T(8,128)(2,1)S(1)}, u32[]{:S(2)}, u32[]{:S(2)}) collective-permute-start(bf16[384,384]{1,0:T(8,128)(2,1)S(1)} %copy-done.52), channel_id=1, source_target_pairs={{0,12},{1,13},{2,14},{3,15},{4,8},{5,9},{6,10},{7,11},{8,4},{9,5},... | collective-permute-start | bytes 884744 | tf_op jit(solution)/shard_map/ppermute | solution.py:26
  114.1 17.1 %collective-permute-start.39 = (bf16[384,384]{1,0:T(8,128)(2,1)S(1)}, bf16[384,384]{1,0:T(8,128)(2,1)S(1)}, u32[]{:S(2)}, u32[]{:S(2)}) collective-permute-start(bf16[384,384]{1,0:T(8,128)(2,1)S(1)} %copy-done.7), channel_id=1, source_target_pairs={{0,2},{1,3},{2,0},{3,1},{4,6},{5,7},{6,4},{7,5},{8,10},{9,11},{10,... | collective-permute-start | bytes 884744 | tf_op jit(solution)/shard_map/ppermute | solution.py:26
  132.8 26.4 %collective-permute-start.45 = (bf16[384,384]{1,0:T(8,128)(2,1)S(1)}, bf16[384,384]{1,0:T(8,128)(2,1)S(1)}, u32[]{:S(2)}, u32[]{:S(2)}) collective-permute-start(bf16[384,384]{1,0:T(8,128)(2,1)S(1)} %copy-done.7), channel_id=1, source_target_pairs={{0,8},{1,9},{2,10},{3,11},{4,12},{5,13},{6,14},{7,15},{8,0},{9,1},... | collective-permute-start | bytes 884744 | tf_op jit(solution)/shard_map/ppermute | solution.py:26
  132.9 26.4 %collective-permute-start.46 = (bf16[384,384]{1,0:T(8,128)(2,1)S(1)}, bf16[384,384]{1,0:T(8,128)(2,1)S(1)}, u32[]{:S(2)}, u32[]{:S(2)}) collective-permute-start(bf16[384,384]{1,0:T(8,128)(2,1)S(1)} %copy-done.37), channel_id=1, source_target_pairs={{0,12},{1,13},{2,14},{3,15},{4,8},{5,9},{6,10},{7,11},{8,4},{9,5},... | collective-permute-start | bytes 884744 | tf_op jit(solution)/shard_map/ppermute | solution.py:26
  134.4 18.3 %collective-permute-start.40 = (bf16[384,384]{1,0:T(8,128)(2,1)S(1)}, bf16[384,384]{1,0:T(8,128)(2,1)S(1)}, u32[]{:S(2)}, u32[]{:S(2)}) collective-permute-start(bf16[384,384]{1,0:T(8,128)(2,1)S(1)} %collective-permute-done.38.refs_4_), channel_id=1, source_target_pairs={{0,2},{1,3},{2,0},{3,1},{4,6},{5,7},{6,4},{7,5},{8,10},{9,11},{10,... | collective-permute-start | bytes 884744 | tf_op jit(solution)/shard_map/ppermute | solution.py:26
  134.9 17.8 %collective-permute-start.44 = (bf16[384,384]{1,0:T(8,128)(2,1)S(1)}, bf16[384,384]{1,0:T(8,128)(2,1)S(1)}, u32[]{:S(2)}, u32[]{:S(2)}) collective-permute-start(bf16[384,384]{1,0:T(8,128)(2,1)S(1)} %collective-permute-done.41.refs_6_), channel_id=1, source_target_pairs={{0,2},{1,3},{2,0},{3,1},{4,6},{5,7},{6,4},{7,5},{8,10},{9,11},{10,... | collective-permute-start | bytes 884744 | tf_op jit(solution)/shard_map/ppermute | solution.py:26
  161.3 16.5 %collective-permute-start.48 = (bf16[384,384]{1,0:T(8,128)(2,1)S(1)}, bf16[384,384]{1,0:T(8,128)(2,1)}, u32[]{:S(2)}, u32[]{:S(2)}) collective-permute-start(bf16[384,384]{1,0:T(8,128)(2,1)S(1)} %copy-done.8), channel_id=1, source_target_pairs={{0,8},{1,9},{2,10},{3,11},{4,12},{5,13},{6,14},{7,15},{8,0},{9,1},... | collective-permute-start | bytes 884744 | tf_op jit(solution)/shard_map/ppermute | solution.py:26
  165.0 28.5 %collective-permute-start.50 = (bf16[128,1536]{1,0:T(8,128)(2,1)S(1)}, bf16[128,1536]{1,0:T(8,128)(2,1)S(1)}, u32[]{:S(2)}, u32[]{:S(2)}) collective-permute-start(bf16[128,1536]{1,0:T(8,128)(2,1)S(1)} %get-tuple-element.136), channel_id=1, source_target_pairs={{0,1},{1,0},{2,3},{3,2},{4,5},{5,4},{6,7},{7,6},{8,9},{9,8},{10,11... | collective-permute-start | bytes 1179656 | tf_op jit(solution)/shard_map/ppermute | solution.py:26
  193.2 21.9 %collective-permute-start.49 = (bf16[128,1536]{1,0:T(8,128)(2,1)}, bf16[128,1536]{1,0:T(8,128)(2,1)}, u32[]{:S(2)}, u32[]{:S(2)}) collective-permute-start(bf16[128,1536]{1,0:T(8,128)(2,1)} %get-tuple-element.100), channel_id=1, source_target_pairs={{0,1},{1,0},{2,3},{3,2},{4,5},{5,4},{6,7},{7,6},{8,9},{9,8},{10,11... | collective-permute-start | bytes 1179656 | tf_op jit(solution)/shard_map/ppermute | solution.py:26
  194.4 21.9 %collective-permute-start.51 = (bf16[128,1536]{1,0:T(8,128)(2,1)}, bf16[128,1536]{1,0:T(8,128)(2,1)}, u32[]{:S(2)}, u32[]{:S(2)}) collective-permute-start(bf16[128,1536]{1,0:T(8,128)(2,1)} %fusion.6), channel_id=1, source_target_pairs={{0,4},{1,5},{2,6},{3,7},{4,0},{5,1},{6,2},{7,3},{8,12},{9,13},{10,... | collective-permute-start | bytes 1179656 | tf_op jit(solution)/shard_map/ppermute | solution.py:26
  194.4 17.2 %collective-permute-start.67 = (bf16[384,384]{1,0:T(8,128)(2,1)}, bf16[384,384]{1,0:T(8,128)(2,1)}, u32[]{:S(2)}, u32[]{:S(2)}) collective-permute-start(bf16[384,384]{1,0:T(8,128)(2,1)} %get-tuple-element.109), channel_id=1, source_target_pairs={{0,12},{1,13},{2,14},{3,15},{4,8},{5,9},{6,10},{7,11},{8,4},{9,5},... | collective-permute-start | bytes 884744 | tf_op jit(solution)/shard_map/ppermute | solution.py:26
  211.6 16.4 %collective-permute-start.73 = (bf16[384,384]{1,0:T(8,128)(2,1)}, bf16[384,384]{1,0:T(8,128)(2,1)S(1)}, u32[]{:S(2)}, u32[]{:S(2)}) collective-permute-start(bf16[384,384]{1,0:T(8,128)(2,1)} %get-tuple-element.116), channel_id=1, source_target_pairs={{0,12},{1,13},{2,14},{3,15},{4,8},{5,9},{6,10},{7,11},{8,4},{9,5},... | collective-permute-start | bytes 884744 | tf_op jit(solution)/shard_map/ppermute | solution.py:26
  215.1 16.6 %collective-permute-start.71 = (bf16[384,384]{1,0:T(8,128)(2,1)}, bf16[384,384]{1,0:T(8,128)(2,1)S(1)}, u32[]{:S(2)}, u32[]{:S(2)}) collective-permute-start(bf16[384,384]{1,0:T(8,128)(2,1)} %get-tuple-element.121.refs_0_), channel_id=1, source_target_pairs={{0,2},{1,3},{2,0},{3,1},{4,6},{5,7},{6,4},{7,5},{8,10},{9,11},{10,... | collective-permute-start | bytes 884744 | tf_op jit(solution)/shard_map/ppermute | solution.py:26
  217.8 25.8 %collective-permute-start.55 = (bf16[128,1536]{1,0:T(8,128)(2,1)S(1)}, bf16[128,1536]{1,0:T(8,128)(2,1)S(1)}, u32[]{:S(2)}, u32[]{:S(2)}) collective-permute-start(bf16[128,1536]{1,0:T(8,128)(2,1)S(1)} %fusion.11.refs_0_), channel_id=1, source_target_pairs={{0,4},{1,5},{2,6},{3,7},{4,0},{5,1},{6,2},{7,3},{8,12},{9,13},{10,... | collective-permute-start | bytes 1179656 | tf_op jit(solution)/shard_map/ppermute | solution.py:26
  228.0 17.1 %collective-permute-start.80 = (bf16[384,384]{1,0:T(8,128)(2,1)S(1)}, bf16[384,384]{1,0:T(8,128)(2,1)S(1)}, u32[]{:S(2)}, u32[]{:S(2)}) collective-permute-start(bf16[384,384]{1,0:T(8,128)(2,1)S(1)} %copy-done.34), channel_id=1, source_target_pairs={{0,12},{1,13},{2,14},{3,15},{4,8},{5,9},{6,10},{7,11},{8,4},{9,5},... | collective-permute-start | bytes 884744 | tf_op jit(solution)/shard_map/ppermute | solution.py:26
  231.7 20.9 %collective-permute-start.78 = (bf16[384,384]{1,0:T(8,128)(2,1)S(1)}, bf16[384,384]{1,0:T(8,128)(2,1)S(1)}, u32[]{:S(2)}, u32[]{:S(2)}) collective-permute-start(bf16[384,384]{1,0:T(8,128)(2,1)S(1)} %copy-done.13), channel_id=1, source_target_pairs={{0,8},{1,9},{2,10},{3,11},{4,12},{5,13},{6,14},{7,15},{8,0},{9,1},... | collective-permute-start | bytes 884744 | tf_op jit(solution)/shard_map/ppermute | solution.py:26
  231.7 20.9 %collective-permute-start.72 = (bf16[384,384]{1,0:T(8,128)(2,1)S(1)}, bf16[384,384]{1,0:T(8,128)(2,1)S(1)}, u32[]{:S(2)}, u32[]{:S(2)}) collective-permute-start(bf16[384,384]{1,0:T(8,128)(2,1)S(1)} %copy-done.63), channel_id=1, source_target_pairs={{0,2},{1,3},{2,0},{3,1},{4,6},{5,7},{6,4},{7,5},{8,10},{9,11},{10,... | collective-permute-start | bytes 884744 | tf_op jit(solution)/shard_map/ppermute | solution.py:26
  260.9 17.0 %collective-permute-start.79 = (bf16[384,384]{1,0:T(8,128)(2,1)S(1)}, bf16[384,384]{1,0:T(8,128)(2,1)S(1)}, u32[]{:S(2)}, u32[]{:S(2)}) collective-permute-start(bf16[384,384]{1,0:T(8,128)(2,1)S(1)} %collective-permute-done.78.refs_4_), channel_id=1, source_target_pairs={{0,2},{1,3},{2,0},{3,1},{4,6},{5,7},{6,4},{7,5},{8,10},{9,11},{10,... | collective-permute-start | bytes 884744 | tf_op jit(solution)/shard_map/ppermute | solution.py:26
  290.2 20.1 %collective-permute-start.84 = (bf16[128,1536]{1,0:T(8,128)(2,1)S(1)}, bf16[128,1536]{1,0:T(8,128)(2,1)S(1)}, u32[]{:S(2)}, u32[]{:S(2)}) collective-permute-start(bf16[128,1536]{1,0:T(8,128)(2,1)S(1)} %get-tuple-element.134), channel_id=1, source_target_pairs={{0,4},{1,5},{2,6},{3,7},{4,0},{5,1},{6,2},{7,3},{8,12},{9,13},{10,... | collective-permute-start | bytes 1179656 | tf_op jit(solution)/shard_map/ppermute | solution.py:26
  292.7 17.6 %collective-permute-start.83 = (bf16[128,1536]{1,0:T(8,128)(2,1)S(1)}, bf16[128,1536]{1,0:T(8,128)(2,1)S(1)}, u32[]{:S(2)}, u32[]{:S(2)}) collective-permute-start(bf16[128,1536]{1,0:T(8,128)(2,1)S(1)} %get-tuple-element.132), channel_id=1, source_target_pairs={{0,1},{1,0},{2,3},{3,2},{4,5},{5,4},{6,7},{7,6},{8,9},{9,8},{10,11... | collective-permute-start | bytes 1179656 | tf_op jit(solution)/shard_map/ppermute | solution.py:26
  (151 other events, 2337.2 us)

commit v7 on v6

--- a/solution.py
+++ b/solution.py
@@ -149,7 +149,10 @@
         copy.wait()
     copies = [load_rows(w_refs[t], wv.at[t], w_sem, t * n_w, kr) for t in range(2)]
     modulate((slots, slot_len, cols), wc, mod_ref, xv, stats, one_plus, xm)
-    for copy in copies[0] + copies[1]:
+    for copy in copies[0]:
+        copy.wait()
+    raw[0] = jnp.dot(xm[...], wv[0], preferred_element_type=jnp.float32)
+    for copy in copies[1]:
         copy.wait()
     copies.append(load_rows(w_refs[2], wv.at[2], w_sem, 2 * n_w, kr))
     kv_copies = []
@@ -160,8 +163,7 @@
                 pltpu.make_async_copy(kv_refs[slot].at[t], place, kv_sem.at[2 * slot + t])
             )
             kv_copies[-1].start()
-    for t in range(2):
-        raw[t] = jnp.dot(xm[...], wv[t], preferred_element_type=jnp.float32)
+    raw[1] = jnp.dot(xm[...], wv[1], preferred_element_type=jnp.float32)
     for copy in kv_copies + copies[2]:
         copy.wait()
 

time: 315 us -> 316 us (level)
  no operation moved by 1% of the time
where the time goes in v7:
time: 316 us; the launch traced here: 315 us
  waiting for transfers between devices  156 us (49%)
  starting transfers between devices  76.5 us (24%)
  Pallas kernels  41.7 us (13%)
  other arithmetic  22 us (7%)
  local copies, waits for them, and re-layouts  17.3 us (5%)
    ppermute x87, waiting for transfers between devices, send_to(): return lax.ppermute(array, AXES, pairs)  156 us
    ppermute x87, starting transfers between devices, send_to(): return lax.ppermute(array, AXES, pairs)  76.5 us
    pallas_call x2, Pallas kernels, heads_of(): pl.pallas_call(functools.partial(layer_kernel, plan), out_shape=jax.Shape...  28 us
    select_n x5, other arithmetic, block_of(): block = jnp.where(s == layer, cut(kind, s * wide + at, bw), other)  10.1 us
    pallas_call x2, Pallas kernels, project(): pl.pallas_call(functools.partial(project_kernel, (slots, slot_len, cols,...  10 us
    unnamed x192, local copies, waits for them, and re-layouts  6.93 us
  transfers between devices with their start and end apart: 87, of which 38 were waited for; matrix products, arithmetic and copies ran while one was open for 8% of the time, Pallas kernels for 12%

profile of v7, /device:TPU:0, one launch (start us, length us, event | category | flops | bytes accessed | tf_op | source)
XLA Modules:
  0.0 314.8 jit_solution(18186342676147018454)
XLA Ops:
  21.5 4.4 %collective-permute-done.2.refs_10_ = bf16[384,384]{1,0:T(8,128)(2,1)S(1)} collective-permute-done((bf16[384,384]{1,0:T(8,128)(2,1)S(1)}, bf16[384,384]{1,0:T(8,128)(2,1)S(1)}, u32[]{:S(2)}, u32[]{:S(2)}) %collective-permute-start.2) | collective-permute-done | bytes 294944 | tf_op jit(solution)/shard_map/ppermute | solution.py:26
  36.1 5.4 %collective-permute-done.5.refs_14_ = bf16[384,384]{1,0:T(8,128)(2,1)} collective-permute-done((bf16[384,384]{1,0:T(8,128)(2,1)S(1)}, bf16[384,384]{1,0:T(8,128)(2,1)}, u32[]{:S(2)}, u32[]{:S(2)}) %collective-permute-start.5) | collective-permute-done | bytes 294944 | tf_op jit(solution)/shard_map/ppermute | solution.py:26
  43.7 5.2 %collective-permute-done.3.refs_2_ = bf16[384,384]{1,0:T(8,128)(2,1)S(1)} collective-permute-done((bf16[384,384]{1,0:T(8,128)(2,1)S(1)}, bf16[384,384]{1,0:T(8,128)(2,1)S(1)}, u32[]{:S(2)}, u32[]{:S(2)}) %collective-permute-start.3) | collective-permute-done | bytes 294944 | tf_op jit(solution)/shard_map/ppermute | solution.py:26
  51.7 6.1 %collective-permute-done.23.refs_20_ = bf16[384,384]{1,0:T(8,128)(2,1)S(1)} collective-permute-done((bf16[384,384]{1,0:T(8,128)(2,1)S(1)}, bf16[384,384]{1,0:T(8,128)(2,1)S(1)}, u32[]{:S(2)}, u32[]{:S(2)}) %collective-permute-start.23) | collective-permute-done | bytes 294944 | tf_op jit(solution)/shard_map/ppermute | solution.py:26
  57.8 3.5 %collective-permute-start.26 = (bf16[384,384]{1,0:T(8,128)(2,1)}, bf16[384,384]{1,0:T(8,128)(2,1)S(1)}, u32[]{:S(2)}, u32[]{:S(2)}) collective-permute-start(bf16[384,384]{1,0:T(8,128)(2,1)} %copy-done.73), channel_id=1, source_target_pairs={{0,12},{1,13},{2,14},{3,15},{4,8},{5,9},{6,10},{7,11},{8,4},{9,5},... | collective-permute-start | bytes 884744 | tf_op jit(solution)/shard_map/ppermute | solution.py:26
  66.8 2.9 collective-permute-done.26.refs_22_
  69.7 4.0 %collective-permute-start.30 = (bf16[384,384]{1,0:T(8,128)(2,1)S(1)}, bf16[384,384]{1,0:T(8,128)(2,1)S(1)}, u32[]{:S(2)}, u32[]{:S(2)}) collective-permute-start(bf16[384,384]{1,0:T(8,128)(2,1)S(1)} %get-tuple-element.80.refs_24_), channel_id=1, source_target_pairs={{0,8},{1,9},{2,10},{3,11},{4,12},{5,13},{6,14},{7,15},{8,0},{9,1},... | collective-permute-start | bytes 884744 | tf_op jit(solution)/shard_map/ppermute | solution.py:26
  81.1 5.2 %collective-permute-done.29.refs_23_ = bf16[384,384]{1,0:T(8,128)(2,1)S(1)} collective-permute-done((bf16[384,384]{1,0:T(8,128)(2,1)S(1)}, bf16[384,384]{1,0:T(8,128)(2,1)S(1)}, u32[]{:S(2)}, u32[]{:S(2)}) %collective-permute-start.29) | collective-permute-done | bytes 294944 | tf_op jit(solution)/shard_map/ppermute | solution.py:26
  88.4 3.9 %collective-permute-done.31.refs_1_ = bf16[384,384]{1,0:T(8,128)(2,1)S(1)} collective-permute-done((bf16[384,384]{1,0:T(8,128)(2,1)S(1)}, bf16[384,384]{1,0:T(8,128)(2,1)S(1)}, u32[]{:S(2)}, u32[]{:S(2)}) %collective-permute-start.31) | collective-permute-done | bytes 294944 | tf_op jit(solution)/shard_map/ppermute | solution.py:26
  95.1 4.7 %collective-permute-done.37.refs_33_ = bf16[2,256,384]{2,1,0:T(8,128)(2,1)S(1)} collective-permute-done((bf16[2,256,384]{2,1,0:T(8,128)(2,1)S(1)}, bf16[2,256,384]{2,1,0:T(8,128)(2,1)S(1)}, u32[]{:S(2)}, u32[]{:S(2)}) %collective-permute-start.37) | collective-permute-done | bytes 393248 | tf_op jit(solution)/shard_map/ppermute | solution.py:26
  105.9 4.5 %collective-permute-done.42.refs_10_ = bf16[384,384]{1,0:T(8,128)(2,1)S(1)} collective-permute-done((bf16[384,384]{1,0:T(8,128)(2,1)S(1)}, bf16[384,384]{1,0:T(8,128)(2,1)S(1)}, u32[]{:S(2)}, u32[]{:S(2)}) %collective-permute-start.42) | collective-permute-done | bytes 294944 | tf_op jit(solution)/shard_map/ppermute | solution.py:26
  114.6 11.5 %collective-permute-done.38.refs_4_ = bf16[384,384]{1,0:T(8,128)(2,1)S(1)} collective-permute-done((bf16[384,384]{1,0:T(8,128)(2,1)S(1)}, bf16[384,384]{1,0:T(8,128)(2,1)S(1)}, u32[]{:S(2)}, u32[]{:S(2)}) %collective-permute-start.38) | collective-permute-done | bytes 294944 | tf_op jit(solution)/shard_map/ppermute | solution.py:26
  127.3 3.7 %modulation.1 = f32[2,3,3072]{2,1,0:T(4,128)} custom-call(bf16[8,256]{1,0:T(8,128)(2,1)} %fusion.21.feats_ref, bf16[3,256,3072]{2,1,0:T(8,128)(2,1)} %bitcast.107), custom_call_target="tpu_custom_call" | custom-call | tf_op jit(solution)/shard_map/modulation/pallas_call | solution.py:409
  138.9 14.0 %layer.2.att_ref = bf16[512,384]{1,0:T(8,128)(2,1)} custom-call(s32[2,4]{1,0:T(2,128)} %bitcast.113, f32[2,3,3072]{2,1,0:T(4,128)} %get-tuple-element.166.mod_ref, bf16[128,1536]{1,0:T(8,128)(2,1)} %copy-done.2, bf16[128,1536]{1,0:T(8,128)(2,1)} %get-tuple-element.163.refs_1_, bf16[128,1536]{1,0:T(8,128)(2,1)} %copy-done.21, bf16[128,1536]{1,0:T(8,128)(2,1)} %copy-done.25, ...), custom_call_target="tpu_custom_call" | custom-call | tf_op jit(solution)/shard_map/layer/pallas_call | solution.py:446
  154.3 5.0 %project.2 = (bf16[2,128,3072]{2,1,0:T(8,128)(2,1)}, bf16[2,128,3072]{2,1,0:T(8,128)(2,1)}) custom-call(bf16[512,384]{1,0:T(8,128)(2,1)} %layer.2.att_ref, bf16[384,384]{1,0:T(8,128)(2,1)} %copy-done.14, bf16[384,384]{1,0:T(8,128)(2,1)} %copy-done.81, bf16[384,384]{1,0:T(8,128)(2,1)} %copy-done.79, bf16[384,384]{1,0:T(8,128)(2,1)} %copy-done.82, ...), custom_call_target="tpu_custom_call" | custom-call | tf_op jit(solution)/shard_map/project/pallas_call | solution.py:478
  166.2 5.0 %collective-permute-done.59.refs_17_ = bf16[384,384]{1,0:T(8,128)(2,1)S(1)} collective-permute-done((bf16[384,384]{1,0:T(8,128)(2,1)S(1)}, bf16[384,384]{1,0:T(8,128)(2,1)S(1)}, u32[]{:S(2)}, u32[]{:S(2)}) %collective-permute-start.59) | collective-permute-done | bytes 294944 | tf_op jit(solution)/shard_map/ppermute | solution.py:26
  171.7 3.0 collective-permute-done.61.refs_18_
  180.0 5.6 %collective-permute-done.62.refs_19_ = bf16[384,384]{1,0:T(8,128)(2,1)S(1)} collective-permute-done((bf16[384,384]{1,0:T(8,128)(2,1)S(1)}, bf16[384,384]{1,0:T(8,128)(2,1)S(1)}, u32[]{:S(2)}, u32[]{:S(2)}) %collective-permute-start.62) | collective-permute-done | bytes 294944 | tf_op jit(solution)/shard_map/ppermute | solution.py:26
  186.1 6.8 %collective-permute-done.64.refs_28_ = bf16[384,384]{1,0:T(8,128)(2,1)S(1)} collective-permute-done((bf16[384,384]{1,0:T(8,128)(2,1)S(1)}, bf16[384,384]{1,0:T(8,128)(2,1)S(1)}, u32[]{:S(2)}, u32[]{:S(2)}) %collective-permute-start.64) | collective-permute-done | bytes 294944 | tf_op jit(solution)/shard_map/ppermute | solution.py:26
  197.1 5.7 %collective-permute-done.65.refs_25_ = bf16[384,384]{1,0:T(8,128)(2,1)S(1)} collective-permute-done((bf16[384,384]{1,0:T(8,128)(2,1)S(1)}, bf16[384,384]{1,0:T(8,128)(2,1)S(1)}, u32[]{:S(2)}, u32[]{:S(2)}) %collective-permute-start.65) | collective-permute-done | bytes 294944 | tf_op jit(solution)/shard_map/ppermute | solution.py:26
  206.2 5.6 %collective-permute-done.67.refs_22_ = bf16[384,384]{1,0:T(8,128)(2,1)} collective-permute-done((bf16[384,384]{1,0:T(8,128)(2,1)}, bf16[384,384]{1,0:T(8,128)(2,1)}, u32[]{:S(2)}, u32[]{:S(2)}) %collective-permute-start.67) | collective-permute-done | bytes 294944 | tf_op jit(solution)/shard_map/ppermute | solution.py:26
  218.4 8.0 %collective-permute-done.74.refs_2_ = bf16[384,384]{1,0:T(8,128)(2,1)S(1)} collective-permute-done((bf16[384,384]{1,0:T(8,128)(2,1)}, bf16[384,384]{1,0:T(8,128)(2,1)S(1)}, u32[]{:S(2)}, u32[]{:S(2)}) %collective-permute-start.74) | collective-permute-done | bytes 294944 | tf_op jit(solution)/shard_map/ppermute | solution.py:26
  228.2 3.7 %collective-permute-start.80 = (bf16[384,384]{1,0:T(8,128)(2,1)S(1)}, bf16[384,384]{1,0:T(8,128)(2,1)S(1)}, u32[]{:S(2)}, u32[]{:S(2)}) collective-permute-start(bf16[384,384]{1,0:T(8,128)(2,1)S(1)} %copy-done.34), channel_id=1, source_target_pairs={{0,12},{1,13},{2,14},{3,15},{4,8},{5,9},{6,10},{7,11},{8,4},{9,5},... | collective-permute-start | bytes 884744 | tf_op jit(solution)/shard_map/ppermute | solution.py:26
  232.0 5.3 %collective-permute-done.75.refs_3_ = bf16[384,384]{1,0:T(8,128)(2,1)S(1)} collective-permute-done((bf16[384,384]{1,0:T(8,128)(2,1)S(1)}, bf16[384,384]{1,0:T(8,128)(2,1)S(1)}, u32[]{:S(2)}, u32[]{:S(2)}) %collective-permute-start.75) | collective-permute-done | bytes 294944 | tf_op jit(solution)/shard_map/ppermute | solution.py:26
  238.6 5.0 %collective-permute-done.55.refs_4_ = bf16[128,1536]{1,0:T(8,128)(2,1)S(1)} collective-permute-done((bf16[128,1536]{1,0:T(8,128)(2,1)S(1)}, bf16[128,1536]{1,0:T(8,128)(2,1)S(1)}, u32[]{:S(2)}, u32[]{:S(2)}) %collective-permute-start.55) | collective-permute-done | bytes 393248 | tf_op jit(solution)/shard_map/ppermute | solution.py:26
  245.3 7.4 %collective-permute-done.78.refs_4_ = bf16[384,384]{1,0:T(8,128)(2,1)S(1)} collective-permute-done((bf16[384,384]{1,0:T(8,128)(2,1)S(1)}, bf16[384,384]{1,0:T(8,128)(2,1)S(1)}, u32[]{:S(2)}, u32[]{:S(2)}) %collective-permute-start.78) | collective-permute-done | bytes 294944 | tf_op jit(solution)/shard_map/ppermute | solution.py:26
  254.0 7.0 %collective-permute-done.77.refs_33_ = bf16[2,256,384]{2,1,0:T(8,128)(2,1)S(1)} collective-permute-done((bf16[2,256,384]{2,1,0:T(8,128)(2,1)S(1)}, bf16[2,256,384]{2,1,0:T(8,128)(2,1)S(1)}, u32[]{:S(2)}, u32[]{:S(2)}) %collective-permute-start.77) | collective-permute-done | bytes 393248 | tf_op jit(solution)/shard_map/ppermute | solution.py:26
  264.1 14.0 %layer.3.att_ref = bf16[512,384]{1,0:T(8,128)(2,1)} custom-call(s32[2,4]{1,0:T(2,128)} %bitcast.114, f32[2,3,3072]{2,1,0:T(4,128)} %get-tuple-element.165.mod_ref, bf16[128,1536]{1,0:T(8,128)(2,1)} %copy-done, bf16[128,1536]{1,0:T(8,128)(2,1)} %copy-done.4, bf16[128,1536]{1,0:T(8,128)(2,1)} %copy-done.26, bf16[128,1536]{1,0:T(8,128)(2,1)} %copy-done.31, ...), custom_call_target="tpu_custom_call" | custom-call | tf_op jit(solution)/shard_map/layer/pallas_call | solution.py:446
  279.6 5.0 %project.3 = (bf16[2,128,3072]{2,1,0:T(8,128)(2,1)}, bf16[2,128,3072]{2,1,0:T(8,128)(2,1)}) custom-call(bf16[512,384]{1,0:T(8,128)(2,1)} %layer.3.att_ref, bf16[384,384]{1,0:T(8,128)(2,1)} %get-tuple-element.121.refs_0_, bf16[384,384]{1,0:T(8,128)(2,1)} %copy-done.84, bf16[384,384]{1,0:T(8,128)(2,1)} %copy-done.83, bf16[384,384]{1,0:T(8,128)(2,1)} %copy-done.86, ...), custom_call_target="tpu_custom_call" | custom-call | tf_op jit(solution)/shard_map/project/pallas_call | solution.py:478
  284.7 3.6 %collective-permute-done.82 = bf16[2,128,3072]{2,1,0:T(8,128)(2,1)S(1)} collective-permute-done((bf16[2,128,3072]{2,1,0:T(8,128)(2,1)}, bf16[2,128,3072]{2,1,0:T(8,128)(2,1)S(1)}, u32[]{:S(2)}, u32[]{:S(2)}) %collective-permute-start.82) | collective-permute-done | bytes 1572896 | tf_op jit(solution)/shard_map/ppermute | solution.py:26
  294.3 8.6 %collective-permute-done.85 = bf16[128,1536]{1,0:T(8,128)(2,1)S(1)} collective-permute-done((bf16[128,1536]{1,0:T(8,128)(2,1)S(1)}, bf16[128,1536]{1,0:T(8,128)(2,1)S(1)}, u32[]{:S(2)}, u32[]{:S(2)}) %collective-permute-start.85) | collective-permute-done | bytes 393248 | tf_op jit(solution)/shard_map/ppermute | solution.py:26
  302.9 7.7 %collective-permute-done.84 = bf16[128,1536]{1,0:T(8,128)(2,1)S(1)} collective-permute-done((bf16[128,1536]{1,0:T(8,128)(2,1)S(1)}, bf16[128,1536]{1,0:T(8,128)(2,1)S(1)}, u32[]{:S(2)}, u32[]{:S(2)}) %collective-permute-start.84) | collective-permute-done | bytes 393248 | tf_op jit(solution)/shard_map/ppermute | solution.py:26
  (374 shorter events, 122.3 us)
Async XLA Ops:
  12.1 22.8 %collective-permute-start.6 = (bf16[384,768]{1,0:T(8,128)(2,1)S(1)}, bf16[384,768]{1,0:T(8,128)(2,1)S(1)}, u32[]{:S(2)}, u32[]{:S(2)}) collective-permute-start(bf16[384,768]{1,0:T(8,128)(2,1)S(1)} %dynamic-slice_bitcast_fusion.1), channel_id=1, source_target_pairs={{0,16},{1,17},{2,18},{3,19},{4,20},{5,21},{6,22},{7,23},{8,24},{9,... | collective-permute-start | bytes 1769480 | tf_op jit(solution)/shard_map/ppermute | solution.py:26
  12.2 16.8 %collective-permute-start.16 = (bf16[384,384]{1,0:T(8,128)(2,1)S(1)}, bf16[384,384]{1,0:T(8,128)(2,1)S(1)}, u32[]{:S(2)}, u32[]{:S(2)}) collective-permute-start(bf16[384,384]{1,0:T(8,128)(2,1)S(1)} %get-tuple-element.150.refs_8_), channel_id=1, source_target_pairs={{0,8},{1,9},{2,10},{3,11},{4,12},{5,13},{6,14},{7,15},{8,0},{9,1},... | collective-permute-start | bytes 884744 | tf_op jit(solution)/shard_map/ppermute | solution.py:26
  31.5 17.4 %collective-permute-start.3 = (bf16[384,384]{1,0:T(8,128)(2,1)S(1)}, bf16[384,384]{1,0:T(8,128)(2,1)S(1)}, u32[]{:S(2)}, u32[]{:S(2)}) collective-permute-start(bf16[384,384]{1,0:T(8,128)(2,1)S(1)} %get-tuple-element.90), channel_id=1, source_target_pairs={{0,4},{1,5},{2,6},{3,7},{4,0},{5,1},{6,2},{7,3},{8,12},{9,13},{10,... | collective-permute-start | bytes 884744 | tf_op jit(solution)/shard_map/ppermute | solution.py:26
  32.2 16.6 %collective-permute-start.19 = (bf16[384,384]{1,0:T(8,128)(2,1)S(1)}, bf16[384,384]{1,0:T(8,128)(2,1)S(1)}, u32[]{:S(2)}, u32[]{:S(2)}) collective-permute-start(bf16[384,384]{1,0:T(8,128)(2,1)S(1)} %collective-permute-done.16.refs_12_), channel_id=1, source_target_pairs={{0,2},{1,3},{2,0},{3,1},{4,6},{5,7},{6,4},{7,5},{8,10},{9,11},{10,... | collective-permute-start | bytes 884744 | tf_op jit(solution)/shard_map/ppermute | solution.py:26
  35.0 43.3 %collective-permute-start.36 = (bf16[512,768]{1,0:T(8,128)(2,1)S(1)}, bf16[512,768]{1,0:T(8,128)(2,1)}, u32[]{:S(2)}, u32[]{:S(2)}) collective-permute-start(bf16[512,768]{1,0:T(8,128)(2,1)S(1)} %pad_maximum_fusion), channel_id=1, source_target_pairs={{0,16},{1,17},{2,18},{3,19},{4,20},{5,21},{6,22},{7,23},{8,24},{9,... | collective-permute-start | bytes 2359304 | tf_op jit(solution)/shard_map/ppermute | solution.py:26
  41.6 16.3 %collective-permute-start.23 = (bf16[384,384]{1,0:T(8,128)(2,1)S(1)}, bf16[384,384]{1,0:T(8,128)(2,1)S(1)}, u32[]{:S(2)}, u32[]{:S(2)}) collective-permute-start(bf16[384,384]{1,0:T(8,128)(2,1)S(1)} %get-tuple-element.73.refs_16_), channel_id=1, source_target_pairs={{0,8},{1,9},{2,10},{3,11},{4,12},{5,13},{6,14},{7,15},{8,0},{9,1},... | collective-permute-start | bytes 884744 | tf_op jit(solution)/shard_map/ppermute | solution.py:26
  65.3 28.2 %collective-permute-start.10 = (bf16[128,1536]{1,0:T(8,128)(2,1)S(1)}, bf16[128,1536]{1,0:T(8,128)(2,1)S(1)}, u32[]{:S(2)}, u32[]{:S(2)}) collective-permute-start(bf16[128,1536]{1,0:T(8,128)(2,1)S(1)} %get-tuple-element.164.refs_0_), channel_id=1, source_target_pairs={{0,4},{1,5},{2,6},{3,7},{4,0},{5,1},{6,2},{7,3},{8,12},{9,13},{10,... | collective-permute-start | bytes 1179656 | tf_op jit(solution)/shard_map/ppermute | solution.py:26
  69.7 18.2 %collective-permute-start.30 = (bf16[384,384]{1,0:T(8,128)(2,1)S(1)}, bf16[384,384]{1,0:T(8,128)(2,1)S(1)}, u32[]{:S(2)}, u32[]{:S(2)}) collective-permute-start(bf16[384,384]{1,0:T(8,128)(2,1)S(1)} %get-tuple-element.80.refs_24_), channel_id=1, source_target_pairs={{0,8},{1,9},{2,10},{3,11},{4,12},{5,13},{6,14},{7,15},{8,0},{9,1},... | collective-permute-start | bytes 884744 | tf_op jit(solution)/shard_map/ppermute | solution.py:26
  81.0 18.8 %collective-permute-start.37 = (bf16[2,256,384]{2,1,0:T(8,128)(2,1)S(1)}, bf16[2,256,384]{2,1,0:T(8,128)(2,1)S(1)}, u32[]{:S(2)}, u32[]{:S(2)}) collective-permute-start(bf16[2,256,384]{2,1,0:T(8,128)(2,1)S(1)} %bitcast.112), channel_id=1, source_target_pairs={{0,4},{1,5},{2,6},{3,7},{4,0},{5,1},{6,2},{7,3},{8,12},{9,13},{10,... | collective-permute-start | bytes 1179656 | tf_op jit(solution)/shard_map/ppermute | solution.py:26
  105.0 21.1 %collective-permute-start.38 = (bf16[384,384]{1,0:T(8,128)(2,1)S(1)}, bf16[384,384]{1,0:T(8,128)(2,1)S(1)}, u32[]{:S(2)}, u32[]{:S(2)}) collective-permute-start(bf16[384,384]{1,0:T(8,128)(2,1)S(1)} %get-tuple-element.87.refs_0_), channel_id=1, source_target_pairs={{0,8},{1,9},{2,10},{3,11},{4,12},{5,13},{6,14},{7,15},{8,0},{9,1},... | collective-permute-start | bytes 884744 | tf_op jit(solution)/shard_map/ppermute | solution.py:26
  105.8 28.6 %collective-permute-start.11 = (bf16[128,1536]{1,0:T(8,128)(2,1)S(1)}, bf16[128,1536]{1,0:T(8,128)(2,1)S(1)}, u32[]{:S(2)}, u32[]{:S(2)}) collective-permute-start(bf16[128,1536]{1,0:T(8,128)(2,1)S(1)} %collective-permute-done.10.refs_4_), channel_id=1, source_target_pairs={{0,16},{1,17},{2,18},{3,19},{4,20},{5,21},{6,22},{7,23},{8,24},{9,... | collective-permute-start | bytes 1179656 | tf_op jit(solution)/shard_map/ppermute | solution.py:26
  110.4 22.5 %collective-permute-start.9 = (bf16[128,1536]{1,0:T(8,128)(2,1)S(1)}, bf16[128,1536]{1,0:T(8,128)(2,1)S(1)}, u32[]{:S(2)}, u32[]{:S(2)}) collective-permute-start(bf16[128,1536]{1,0:T(8,128)(2,1)S(1)} %collective-permute-done.8.refs_2_), channel_id=1, source_target_pairs={{0,16},{1,17},{2,18},{3,19},{4,20},{5,21},{6,22},{7,23},{8,24},{9,... | collective-permute-start | bytes 1179656 | tf_op jit(solution)/shard_map/ppermute | solution.py:26
  111.8 19.3 %collective-permute-start.41 = (bf16[384,384]{1,0:T(8,128)(2,1)S(1)}, bf16[384,384]{1,0:T(8,128)(2,1)S(1)}, u32[]{:S(2)}, u32[]{:S(2)}) collective-permute-start(bf16[384,384]{1,0:T(8,128)(2,1)S(1)} %copy-done.52), channel_id=1, source_target_pairs={{0,12},{1,13},{2,14},{3,15},{4,8},{5,9},{6,10},{7,11},{8,4},{9,5},... | collective-permute-start | bytes 884744 | tf_op jit(solution)/shard_map/ppermute | solution.py:26
  114.1 17.1 %collective-permute-start.39 = (bf16[384,384]{1,0:T(8,128)(2,1)S(1)}, bf16[384,384]{1,0:T(8,128)(2,1)S(1)}, u32[]{:S(2)}, u32[]{:S(2)}) collective-permute-start(bf16[384,384]{1,0:T(8,128)(2,1)S(1)} %copy-done.7), channel_id=1, source_target_pairs={{0,2},{1,3},{2,0},{3,1},{4,6},{5,7},{6,4},{7,5},{8,10},{9,11},{10,... | collective-permute-start | bytes 884744 | tf_op jit(solution)/shard_map/ppermute | solution.py:26
  132.8 26.5 %collective-permute-start.45 = (bf16[384,384]{1,0:T(8,128)(2,1)S(1)}, bf16[384,384]{1,0:T(8,128)(2,1)S(1)}, u32[]{:S(2)}, u32[]{:S(2)}) collective-permute-start(bf16[384,384]{1,0:T(8,128)(2,1)S(1)} %copy-done.7), channel_id=1, source_target_pairs={{0,8},{1,9},{2,10},{3,11},{4,12},{5,13},{6,14},{7,15},{8,0},{9,1},... | collective-permute-start | bytes 884744 | tf_op jit(solution)/shard_map/ppermute | solution.py:26
  132.9 26.5 %collective-permute-start.46 = (bf16[384,384]{1,0:T(8,128)(2,1)S(1)}, bf16[384,384]{1,0:T(8,128)(2,1)S(1)}, u32[]{:S(2)}, u32[]{:S(2)}) collective-permute-start(bf16[384,384]{1,0:T(8,128)(2,1)S(1)} %copy-done.37), channel_id=1, source_target_pairs={{0,12},{1,13},{2,14},{3,15},{4,8},{5,9},{6,10},{7,11},{8,4},{9,5},... | collective-permute-start | bytes 884744 | tf_op jit(solution)/shard_map/ppermute | solution.py:26
  134.4 18.5 %collective-permute-start.40 = (bf16[384,384]{1,0:T(8,128)(2,1)S(1)}, bf16[384,384]{1,0:T(8,128)(2,1)S(1)}, u32[]{:S(2)}, u32[]{:S(2)}) collective-permute-start(bf16[384,384]{1,0:T(8,128)(2,1)S(1)} %collective-permute-done.38.refs_4_), channel_id=1, source_target_pairs={{0,2},{1,3},{2,0},{3,1},{4,6},{5,7},{6,4},{7,5},{8,10},{9,11},{10,... | collective-permute-start | bytes 884744 | tf_op jit(solution)/shard_map/ppermute | solution.py:26
  134.9 18.0 %collective-permute-start.44 = (bf16[384,384]{1,0:T(8,128)(2,1)S(1)}, bf16[384,384]{1,0:T(8,128)(2,1)S(1)}, u32[]{:S(2)}, u32[]{:S(2)}) collective-permute-start(bf16[384,384]{1,0:T(8,128)(2,1)S(1)} %collective-permute-done.41.refs_6_), channel_id=1, source_target_pairs={{0,2},{1,3},{2,0},{3,1},{4,6},{5,7},{6,4},{7,5},{8,10},{9,11},{10,... | collective-permute-start | bytes 884744 | tf_op jit(solution)/shard_map/ppermute | solution.py:26
  161.5 16.5 %collective-permute-start.48 = (bf16[384,384]{1,0:T(8,128)(2,1)S(1)}, bf16[384,384]{1,0:T(8,128)(2,1)}, u32[]{:S(2)}, u32[]{:S(2)}) collective-permute-start(bf16[384,384]{1,0:T(8,128)(2,1)S(1)} %copy-done.8), channel_id=1, source_target_pairs={{0,8},{1,9},{2,10},{3,11},{4,12},{5,13},{6,14},{7,15},{8,0},{9,1},... | collective-permute-start | bytes 884744 | tf_op jit(solution)/shard_map/ppermute | solution.py:26
  165.2 28.4 %collective-permute-start.50 = (bf16[128,1536]{1,0:T(8,128)(2,1)S(1)}, bf16[128,1536]{1,0:T(8,128)(2,1)S(1)}, u32[]{:S(2)}, u32[]{:S(2)}) collective-permute-start(bf16[128,1536]{1,0:T(8,128)(2,1)S(1)} %get-tuple-element.136), channel_id=1, source_target_pairs={{0,1},{1,0},{2,3},{3,2},{4,5},{5,4},{6,7},{7,6},{8,9},{9,8},{10,11... | collective-permute-start | bytes 1179656 | tf_op jit(solution)/shard_map/ppermute | solution.py:26
  193.3 21.9 %collective-permute-start.49 = (bf16[128,1536]{1,0:T(8,128)(2,1)}, bf16[128,1536]{1,0:T(8,128)(2,1)}, u32[]{:S(2)}, u32[]{:S(2)}) collective-permute-start(bf16[128,1536]{1,0:T(8,128)(2,1)} %get-tuple-element.100), channel_id=1, source_target_pairs={{0,1},{1,0},{2,3},{3,2},{4,5},{5,4},{6,7},{7,6},{8,9},{9,8},{10,11... | collective-permute-start | bytes 1179656 | tf_op jit(solution)/shard_map/ppermute | solution.py:26
  194.6 22.0 %collective-permute-start.51 = (bf16[128,1536]{1,0:T(8,128)(2,1)}, bf16[128,1536]{1,0:T(8,128)(2,1)}, u32[]{:S(2)}, u32[]{:S(2)}) collective-permute-start(bf16[128,1536]{1,0:T(8,128)(2,1)} %fusion.6), channel_id=1, source_target_pairs={{0,4},{1,5},{2,6},{3,7},{4,0},{5,1},{6,2},{7,3},{8,12},{9,13},{10,... | collective-permute-start | bytes 1179656 | tf_op jit(solution)/shard_map/ppermute | solution.py:26
  194.6 17.2 %collective-permute-start.67 = (bf16[384,384]{1,0:T(8,128)(2,1)}, bf16[384,384]{1,0:T(8,128)(2,1)}, u32[]{:S(2)}, u32[]{:S(2)}) collective-permute-start(bf16[384,384]{1,0:T(8,128)(2,1)} %get-tuple-element.109), channel_id=1, source_target_pairs={{0,12},{1,13},{2,14},{3,15},{4,8},{5,9},{6,10},{7,11},{8,4},{9,5},... | collective-permute-start | bytes 884744 | tf_op jit(solution)/shard_map/ppermute | solution.py:26
  211.8 16.4 %collective-permute-start.73 = (bf16[384,384]{1,0:T(8,128)(2,1)}, bf16[384,384]{1,0:T(8,128)(2,1)S(1)}, u32[]{:S(2)}, u32[]{:S(2)}) collective-permute-start(bf16[384,384]{1,0:T(8,128)(2,1)} %get-tuple-element.116), channel_id=1, source_target_pairs={{0,12},{1,13},{2,14},{3,15},{4,8},{5,9},{6,10},{7,11},{8,4},{9,5},... | collective-permute-start | bytes 884744 | tf_op jit(solution)/shard_map/ppermute | solution.py:26
  215.3 16.6 %collective-permute-start.71 = (bf16[384,384]{1,0:T(8,128)(2,1)}, bf16[384,384]{1,0:T(8,128)(2,1)S(1)}, u32[]{:S(2)}, u32[]{:S(2)}) collective-permute-start(bf16[384,384]{1,0:T(8,128)(2,1)} %get-tuple-element.121.refs_0_), channel_id=1, source_target_pairs={{0,2},{1,3},{2,0},{3,1},{4,6},{5,7},{6,4},{7,5},{8,10},{9,11},{10,... | collective-permute-start | bytes 884744 | tf_op jit(solution)/shard_map/ppermute | solution.py:26
  218.0 25.7 %collective-permute-start.55 = (bf16[128,1536]{1,0:T(8,128)(2,1)S(1)}, bf16[128,1536]{1,0:T(8,128)(2,1)S(1)}, u32[]{:S(2)}, u32[]{:S(2)}) collective-permute-start(bf16[128,1536]{1,0:T(8,128)(2,1)S(1)} %fusion.11.refs_0_), channel_id=1, source_target_pairs={{0,4},{1,5},{2,6},{3,7},{4,0},{5,1},{6,2},{7,3},{8,12},{9,13},{10,... | collective-permute-start | bytes 1179656 | tf_op jit(solution)/shard_map/ppermute | solution.py:26
  228.2 17.1 %collective-permute-start.80 = (bf16[384,384]{1,0:T(8,128)(2,1)S(1)}, bf16[384,384]{1,0:T(8,128)(2,1)S(1)}, u32[]{:S(2)}, u32[]{:S(2)}) collective-permute-start(bf16[384,384]{1,0:T(8,128)(2,1)S(1)} %copy-done.34), channel_id=1, source_target_pairs={{0,12},{1,13},{2,14},{3,15},{4,8},{5,9},{6,10},{7,11},{8,4},{9,5},... | collective-permute-start | bytes 884744 | tf_op jit(solution)/shard_map/ppermute | solution.py:26
  231.9 20.8 %collective-permute-start.78 = (bf16[384,384]{1,0:T(8,128)(2,1)S(1)}, bf16[384,384]{1,0:T(8,128)(2,1)S(1)}, u32[]{:S(2)}, u32[]{:S(2)}) collective-permute-start(bf16[384,384]{1,0:T(8,128)(2,1)S(1)} %copy-done.13), channel_id=1, source_target_pairs={{0,8},{1,9},{2,10},{3,11},{4,12},{5,13},{6,14},{7,15},{8,0},{9,1},... | collective-permute-start | bytes 884744 | tf_op jit(solution)/shard_map/ppermute | solution.py:26
  231.9 20.8 %collective-permute-start.72 = (bf16[384,384]{1,0:T(8,128)(2,1)S(1)}, bf16[384,384]{1,0:T(8,128)(2,1)S(1)}, u32[]{:S(2)}, u32[]{:S(2)}) collective-permute-start(bf16[384,384]{1,0:T(8,128)(2,1)S(1)} %copy-done.63), channel_id=1, source_target_pairs={{0,2},{1,3},{2,0},{3,1},{4,6},{5,7},{6,4},{7,5},{8,10},{9,11},{10,... | collective-permute-start | bytes 884744 | tf_op jit(solution)/shard_map/ppermute | solution.py:26
  261.0 17.1 %collective-permute-start.79 = (bf16[384,384]{1,0:T(8,128)(2,1)S(1)}, bf16[384,384]{1,0:T(8,128)(2,1)S(1)}, u32[]{:S(2)}, u32[]{:S(2)}) collective-permute-start(bf16[384,384]{1,0:T(8,128)(2,1)S(1)} %collective-permute-done.78.refs_4_), channel_id=1, source_target_pairs={{0,2},{1,3},{2,0},{3,1},{4,6},{5,7},{6,4},{7,5},{8,10},{9,11},{10,... | collective-permute-start | bytes 884744 | tf_op jit(solution)/shard_map/ppermute | solution.py:26
  290.5 20.1 %collective-permute-start.84 = (bf16[128,1536]{1,0:T(8,128)(2,1)S(1)}, bf16[128,1536]{1,0:T(8,128)(2,1)S(1)}, u32[]{:S(2)}, u32[]{:S(2)}) collective-permute-start(bf16[128,1536]{1,0:T(8,128)(2,1)S(1)} %get-tuple-element.134), channel_id=1, source_target_pairs={{0,4},{1,5},{2,6},{3,7},{4,0},{5,1},{6,2},{7,3},{8,12},{9,13},{10,... | collective-permute-start | bytes 1179656 | tf_op jit(solution)/shard_map/ppermute | solution.py:26
  293.0 17.6 %collective-permute-start.83 = (bf16[128,1536]{1,0:T(8,128)(2,1)S(1)}, bf16[128,1536]{1,0:T(8,128)(2,1)S(1)}, u32[]{:S(2)}, u32[]{:S(2)}) collective-permute-start(bf16[128,1536]{1,0:T(8,128)(2,1)S(1)} %get-tuple-element.132), channel_id=1, source_target_pairs={{0,1},{1,0},{2,3},{3,2},{4,5},{5,4},{6,7},{7,6},{8,9},{9,8},{10,11... | collective-permute-start | bytes 1179656 | tf_op jit(solution)/shard_map/ppermute | solution.py:26
  (151 other events, 2337.9 us)
